TPU v7x, 256 devices: a whole 4x4x8 slice. The times are simulated.
256 devices in a mesh: space: 32 (over x, z_hi, y), chan: 8 (over z_lo, core).
Axes of the slice: x: 4, y: 4, z: 8 (z_hi: 2, z_lo: 4; z = z_hi * 4 + z_lo), core: 2. Of those that a mesh axis runs over, the one named last changes fastest.
Arguments:
- volume: bfloat16 [64, 64, 32, 128], P('chan', 'space'), may hold values from -6 to 6
- weight_one: bfloat16 [64, 64, 3, 3, 3], P('chan'), may hold values from -0.15625 to 0.15625
- bias_one: float32 [64], P('chan'), may hold values from -0.5 to 0.5
- weight_two: bfloat16 [64, 64, 3, 3, 3], P('chan'), may hold values from -0.15625 to 0.15625
- bias_two: float32 [64], P('chan'), may hold values from -0.5 to 0.5
- cotangent: bfloat16 [64, 64, 32, 128], P('chan', 'space'), may hold values from -6 to 6
Outputs:
- features: bfloat16 [64, 64, 32, 128], P('chan', 'space')
- grad_w_one: float32 [64, 64, 3, 3, 3], P('chan')
- grad_b_one: float32 [64], P('chan')
- grad_w_two: float32 [64, 64, 3, 3, 3], P('chan')
- grad_b_two: float32 [64], P('chan')
All inputs are finite; a program needn't handle non-finite values.
Results may differ from a plain program's by a relative error of at most 0.03.
The roundings to bfloat16 on the way count: a program that leaves them out, or rounds other values in their place, can miss the bound.
Values may be sent and summed in bfloat16 or wider, within the bound.
No kernel may reach another device: no remote copies, remote signals or barrier semaphores. Data moves between devices by JAX's collectives and lax.ppermute only.
A program may use at most 128 MiB of HBM per device.

v0:
```python
import jax
import jax.numpy as jnp
from jax import lax
from jax.sharding import PartitionSpec as P

SLOPE = 0.2


def padded(array, sides, width):
    for axis, dim in sides:
        count, length = (lax.axis_size(axis), array.shape[dim])
        up = [(i, (i + 1) % count) for i in range(count - 1)]
        down = [(j, i) for i, j in up]
        last = lax.slice_in_dim(array, length - width, length, axis=dim)
        initial = lax.slice_in_dim(array, 0, width, axis=dim)
        before = lax.ppermute(last, axis, up)
        after = lax.ppermute(initial, axis, down)
        array = jnp.concatenate([before, array, after], axis=dim)
    return array


def conv_inner(inputs, kernel, side):
    return lax.conv_general_dilated(
        inputs[None],
        kernel,
        (1, 1, 1),
        ((0, 0), (side, side), (1, 1)),
        dimension_numbers=("NCDHW", "OIDHW", "NCDHW"),
        preferred_element_type=jnp.float32,
    )[0]


def conv_back_inner(delta, kernel, side):
    flipped = jnp.flip(kernel, (2, 3, 4))
    return lax.conv_general_dilated(
        delta[None],
        flipped,
        (1, 1, 1),
        ((0, 0), (side, side), (1, 1)),
        dimension_numbers=("NCDHW", "IODHW", "NCDHW"),
        preferred_element_type=jnp.float32,
    )[0]


def kernel_grad_inner(inputs, delta, side):
    result = lax.conv_general_dilated(
        inputs[None],
        delta[None],
        (1, 1, 1),
        ((0, 0), (side, side), (1, 1)),
        dimension_numbers=("CNDHW", "IODHW", "NCDHW"),
        preferred_element_type=jnp.float32,
    )
    return jnp.transpose(result, (1, 0, 2, 3, 4))


def surround(field):
    gathered = lax.all_gather(field, "chan", axis=0, tiled=True)
    return padded(gathered, (("space", 1),), 1)


def shards(volume, weight_one, bias_one, weight_two, bias_two, cotangent):
    own_channels = volume.shape[0]
    total_cells = volume.shape[1] * lax.axis_size("space") * volume.shape[2] * volume.shape[3]
    factor = total_cells ** (-0.5)
    wide_input = surround(volume)
    pre_one = conv_inner(wide_input, weight_one, 1) + bias_one[:, None, None, None]
    act_one = jnp.where(pre_one > 0, pre_one, SLOPE * pre_one).astype(jnp.bfloat16)
    wide_act = surround(act_one)
    pre_two = conv_inner(wide_act, weight_two, 1) + bias_two[:, None, None, None]
    features = jnp.where(pre_two > 0, pre_two, SLOPE * pre_two).astype(jnp.bfloat16)
    delta_two = (cotangent.astype(jnp.float32) * jnp.where(pre_two > 0, 1.0, SLOPE)).astype(
        jnp.bfloat16
    )
    kernel_two = kernel_grad_inner(wide_act, delta_two, 1)
    offset_two = jnp.sum(delta_two.astype(jnp.float32), axis=(1, 2, 3))
    delta_rim = padded(delta_two, (("space", 1),), 1)
    all_delta, all_kernel = (
        lax.all_gather(delta_rim, "chan", axis=0, tiled=True),
        lax.all_gather(weight_two, "chan", axis=0, tiled=True),
    )
    own_kernel = lax.dynamic_slice_in_dim(
        all_kernel, lax.axis_index("chan") * own_channels, own_channels, 1
    )
    back_one = conv_back_inner(all_delta, own_kernel, 1)
    delta_one = (back_one * jnp.where(pre_one > 0, 1.0, SLOPE)).astype(jnp.bfloat16)
    kernel_one = kernel_grad_inner(wide_input, delta_one, 1)
    offset_one = jnp.sum(delta_one.astype(jnp.float32), axis=(1, 2, 3))
    summed = lax.psum((kernel_one, offset_one, kernel_two, offset_two), "space")
    return (
        features,
        summed[0] * factor,
        summed[1] * factor,
        summed[2] * factor,
        summed[3] * factor,
    )


def solution(mesh):
    in_specs = (
        P("chan", "space", None, None),
        P("chan", None, None, None, None),
        P("chan"),
        P("chan", None, None, None, None),
        P("chan"),
        P("chan", "space", None, None),
    )
    out_specs = (
        P("chan", "space", None, None),
        P("chan", None, None, None, None),
        P("chan"),
        P("chan", None, None, None, None),
        P("chan"),
    )
    return jax.shard_map(shards, mesh=mesh, in_specs=in_specs, out_specs=out_specs, check_vma=False)
```

profile of v0, /device:TPU:8, one launch (start us, length us, event | category | flops | bytes accessed | tf_op | source)
XLA Modules:
  0.0 920.7 jit_solution(4110129641885603056)
XLA Ops:
  8.0 42.1 %all-gather.4.cloned.1.call-done = bf16[64,2,32,128]{3,2,1,0:T(8,128)(2,1)} async-done(((bf16[8,2,32,128]{3,2,1,0:T(8,128)(2,1)}), bf16[64,2,32,128]{3,2,1,0:T(8,128)(2,1)}) %all-gather.4.cloned.1.call-update) | async-done | bytes 1048592 | tf_op jit(solution)/shard_map/all_gather | solution.py:58
  50.1 2.1 fusion.90
  52.1 3.4 collective-permute-start
  55.5 3.2 collective-permute-start.1
  58.8 4.7 copy.105
  64.5 2.8 copy.104
  67.8 3.7 copy.106
  71.5 2.1 maximum_bitcast_fusion
  73.6 3.3 fusion.88
  78.8 18.8 %broadcast_select_fusion.2 = f32[2,32,8,17,8]{4,2,3,1,0:T(8,128)} fusion(pred[8,17]{0,1:T(8,128)(4,1)S(1)} %copy-done.7, bf16[8,64,3,3,3]{1,0,4,3,2:T(8,128)(2,1)S(1)} %copy-done, bf16[64,4,32,1,7,2]{0,4,5,2,1,3:T(8,128)(2,1)S(1)} %slice.36, bf16[64,4,32,1,8,17]{0,4,5,2,1,3:T(8,128)(2,1)S(1)} %copy.108), kind=kOutput, calls=%fused_computation.53 | convolution fusion | flops 243175424 | bytes 2763912 | tf_op jit(solution)/shard_map/conv_general_dilated | solution.py:23
  97.5 2.9 copy.109
  101.6 71.4 %all-gather.6.cloned.1.call-done = bf16[64,2,32,128]{2,0,3,1:T(8,128)(2,1)} async-done(((bf16[8,2,32,128]{2,0,3,1:T(8,128)(2,1)}), bf16[64,2,32,128]{2,0,3,1:T(8,128)(2,1)}) %all-gather.6.cloned.1.call-update) | async-done | bytes 1048592 | tf_op jit(solution)/shard_map/all_gather | solution.py:58
  173.0 4.5 fusion.89
  177.5 3.9 copy.110
  181.5 3.4 collective-permute-start.2
  184.9 3.0 copy.111
  187.9 3.2 collective-permute-start.3
  192.2 5.6 collective-permute-done.2
  197.8 3.9 copy.112
  201.7 2.8 collective-permute-done.3
  204.5 4.6 copy.113
  209.1 9.0 fusion.37
  218.1 9.6 %pad.2 = bf16[64,4,32,1,136]{2,0,4,1,3:T(8,128)(2,1)} pad(bf16[64,4,32,1,128]{2,0,4,1,3:T(8,128)(2,1)} %get-tuple-element.37, bf16[]{:T(256)} %constant.7), padding=0_0x0_0x0_0x0_0x1_7 | pad | bytes 4325378 | tf_op jit(solution)/shard_map/broadcast_in_dim | solution.py:24
  227.7 10.0 %copy.116 = bf16[64,4,32,1,8,17]{0,4,5,2,1,3:T(8,128)(2,1)} copy(bf16[64,4,32,1,8,17]{2,0,5,4,1,3:T(8,128)(2,1)} %bitcast.84) | data formatting | bytes 4456448 | tf_op jit(solution)/shard_map/conv_general_dilated | solution.py:23
  238.9 20.0 %broadcast_select_fusion.1 = f32[2,32,8,17,8]{4,2,3,1,0:T(8,128)} fusion(pred[8,17]{0,1:T(8,128)(4,1)S(1)} %copy-done.7, bf16[8,64,3,3,3]{1,0,4,3,2:T(8,128)(2,1)S(1)} %copy-done.4, bf16[64,4,32,1,7,2]{0,4,5,2,1,3:T(8,128)(2,1)S(1)} %slice.40, bf16[64,4,32,1,8,17]{0,4,5,2,1,3:T(8,128)(2,1)} %copy.116), kind=kOutput, calls=%fused_computation.52 | convolution fusion | flops 243175424 | bytes 2763912 | tf_op jit(solution)/shard_map/conv_general_dilated | solution.py:23
  258.9 2.9 copy.117
  261.9 2.1 convert_reduce_fusion
  264.7 5.6 collective-permute-start.4
  270.3 1.9 collective-permute-start.5
  272.6 3.9 collective-permute-done.4
  276.6 11.8 %collective-permute-done.5 = bf16[8,1,32,128]{2,0,3,1:T(8,128)(2,1)S(1)} collective-permute-done((bf16[8,1,32,128]{2,0,3,1:T(8,128)(2,1)S(1)}, bf16[8,1,32,128]{2,0,3,1:T(8,128)(2,1)S(1)}, u32[]{:S(2)}, u32[]{:S(2)}) %collective-permute-start.5) | collective-permute-done | bytes 65568 | tf_op jit(solution)/shard_map/ppermute | solution.py:17
  289.5 21.3 %all_gather.15 = bf16[64,64,3,3,3]{1,0,4,3,2:T(8,128)(2,1)} all-gather(bf16[8,64,3,3,3]{1,0,4,3,2:T(8,128)(2,1)S(1)} %copy-done.4), channel_id=1, replica_groups=mesh['space'=32,'chan'=8] {'chan'}, dimensions={0}, use_global_device_ids=true | all-gather | bytes 248832 | tf_op jit(solution)/shard_map/all_gather | solution.py:80
  310.7 4.6 fusion.86
  315.4 2.7 copy.143
  318.3 2.7 copy.142
  321.1 3.8 copy.122
  324.9 2.6 fusion.33
  327.5 2.6 fusion.35
  330.1 6.4 copy.135
  336.5 20.3 %copy.134 = bf16[1,64,4,32,128]{1,0,4,3,2:T(2,128)(2,1)} copy(bf16[1,64,4,32,128]{3,1,4,2,0:T(8,128)(2,1)} %get-tuple-element.36) | data formatting | bytes 4194304 | tf_op jit(solution)/shard_map/broadcast_in_dim | solution.py:24
  356.8 86.9 %fusion.92 = f32[8,64,3,3,3]{1,0,4,3,2:T(8,128)} fusion(bf16[1,64,4,32,128]{1,0,4,3,2:T(2,128)(2,1)} %copy.134, bf16[1,8,2,32,128]{1,0,4,3,2:T(2,128)(2,1)} %copy.135), kind=kOutput, calls=%fused_computation.101 | convolution fusion | flops 220618752 | bytes 2283520 | tf_op jit(solution)/shard_map/transpose | solution.py:54
  443.8 8.8 copy.127
  452.6 3.0 pad.4
  455.7 1.7 copy.129
  457.6 10.6 %broadcast_select_fusion = f32[2,32,8,17,8]{4,2,3,1,0:T(8,128)} fusion(pred[8,17]{0,1:T(8,128)(4,1)S(1)} %copy-done.7, bf16[64,4,32,1,7,2]{0,4,5,2,1,3:T(8,128)(2,1)S(1)} %slice.48, bf16[64,4,32,1,8,17]{0,4,5,2,1,3:T(8,128)(2,1)S(1)} %copy.129, bf16[64,64,3,3,3]{1,0,4,3,2:T(8,128)(2,1)S(1)} %copy-done.2, s32[]{:T(128)S(6)} %select_n.23), kind=kOutput, calls=%fused_computation.51 | convolution fusion | flops 243175424 | bytes 2957452 | tf_op jit(solution)/shard_map/conv_general_dilated | solution.py:35
  468.1 2.9 copy.132
  472.0 13.6 %fusion.55 = f32[8,64,3,3,3]{1,0,4,3,2:T(8,128)} fusion(f32[2,32,8,17,8]{4,2,3,1,0:T(8,128)} %broadcast_select_fusion, f32[2,32,8,17,8]{4,2,3,1,0:T(8,128)} %broadcast_select_fusion.2, f32[8]{0:T(128)S(1)} %copy-done.5, pred[8,17]{0,1:T(8,128)(4,1)S(1)} %copy-done.7, bf16[64,4,32,8,17,1]{0,3,5,4,2,1:T(8,128)(2,1)} %fusion.33, ...), kind=kOutput, calls=%fused_computation.59 | convolution fusion | flops 256106496 | bytes 7297192 | tf_op jit(solution)/shard_map/transpose | solution.py:54
  486.6 424.5 %all-reduce.3.cloned.1.call-done = (f32[8,64,3,3,3]{1,0,4,3,2:T(8,128)}, f32[8]{0:T(128)}, f32[8,64,3,3,3]{1,0,4,3,2:T(8,128)}, f32[8]{0:T(128)}) async-done(((f32[8,64,3,3,3]{1,0,4,3,2:T(8,128)}, f32[8]{0:T(128)}, f32[8,64,3,3,3]{1,0,4,3,2:T(8,128)}, f32[8]{0:T(128)}), (f32[8,64,3,3,3]{1,0,4,3,2:T(8,128)}, f32[8]{0:T(128)}, f32[8,64,3,3,3]{1,0,4,3,2:T(8,128)}, f32[8]{0:T(128)})) %all-reduce.3.cloned.1.call-update) | async-done | bytes 110672 | tf_op jit(solution)/shard_map/psum | solution.py:89
  (50 shorter events, 15.0 us)
Async XLA Ops:
  7.2 71.6 %copy-start = (bf16[8,64,3,3,3]{1,0,4,3,2:T(8,128)(2,1)S(1)}, bf16[8,64,3,3,3]{1,0,4,3,2:T(8,128)(2,1)}, u32[]{:S(2)}) copy-start(bf16[8,64,3,3,3]{1,0,4,3,2:T(8,128)(2,1)} %param.7) | copy-start | bytes 82948
  7.2 42.9 %all-gather.4.cloned.1.call-start = ((), (), s32[]{:S(2)}) async-start(), calls=%async_computation | async-start | bytes 1179648 | tf_op jit(solution)/shard_map/all_gather | solution.py:58
  7.9 165.1 %all-gather.6.cloned.1.call-start = ((), (), s32[]{:S(2)}) async-start(), calls=%async_computation.1 | async-start | bytes 4718592 | tf_op jit(solution)/shard_map/all_gather | solution.py:58
  52.1 12.3 %collective-permute-start = (bf16[64,1,32,128]{3,2,1,0:T(8,128)(2,1)S(1)}, bf16[64,1,32,128]{3,2,1,0:T(8,128)(2,1)}, u32[]{:S(2)}, u32[]{:S(2)}) collective-permute-start(bf16[64,1,32,128]{3,2,1,0:T(8,128)(2,1)S(1)} %get-tuple-element.47), channel_id=1, source_target_pairs={{0,8},{8,16},{16,24},{24,32},{32,40},{40,48},{48,56},{56,64},{64,7... | collective-permute-start | bytes 1572872 | tf_op jit(solution)/shard_map/ppermute | solution.py:16
  55.5 12.3 %collective-permute-start.1 = (bf16[64,1,32,128]{3,2,1,0:T(8,128)(2,1)}, bf16[64,1,32,128]{3,2,1,0:T(8,128)(2,1)}, u32[]{:S(2)}, u32[]{:S(2)}) collective-permute-start(bf16[64,1,32,128]{3,2,1,0:T(8,128)(2,1)} %get-tuple-element.48), channel_id=1, source_target_pairs={{8,0},{16,8},{24,16},{32,24},{40,32},{48,40},{56,48},{64,56},{72,6... | collective-permute-start | bytes 1572872 | tf_op jit(solution)/shard_map/ppermute | solution.py:17
  76.9 1.9 copy-start.7
  97.5 2.9 copy-start.5
  101.6 342.2 %all-gather.8.cloned.1.call-start = ((), (), s32[]{:S(2)}) async-start(), calls=%async_computation.2 | async-start | bytes 2359296 | tf_op jit(solution)/shard_map/all_gather | solution.py:79
  177.5 13.6 %copy-start.3 = (bf16[8,2,32,128]{3,2,1,0:T(8,128)(2,1)S(1)}, bf16[8,2,32,128]{3,2,1,0:T(8,128)(2,1)}, u32[]{:S(2)}) copy-start(bf16[8,2,32,128]{3,2,1,0:T(8,128)(2,1)} %param.11) | copy-start | bytes 393220
  181.5 16.3 %collective-permute-start.2 = (bf16[64,1,32,128]{3,2,1,0:T(8,128)(2,1)}, bf16[64,1,32,128]{3,2,1,0:T(8,128)(2,1)}, u32[]{:S(2)}, u32[]{:S(2)}) collective-permute-start(bf16[64,1,32,128]{3,2,1,0:T(8,128)(2,1)} %copy.110), channel_id=1, source_target_pairs={{0,8},{8,16},{16,24},{24,32},{32,40},{40,48},{48,56},{56,64},{64,7... | collective-permute-start | bytes 1572872 | tf_op jit(solution)/shard_map/ppermute | solution.py:16
  187.9 16.6 %collective-permute-start.3 = (bf16[64,1,32,128]{3,2,1,0:T(8,128)(2,1)}, bf16[64,1,32,128]{3,2,1,0:T(8,128)(2,1)}, u32[]{:S(2)}, u32[]{:S(2)}) collective-permute-start(bf16[64,1,32,128]{3,2,1,0:T(8,128)(2,1)} %copy.111), channel_id=1, source_target_pairs={{8,0},{16,8},{24,16},{32,24},{40,32},{48,40},{56,48},{64,56},{72,6... | collective-permute-start | bytes 1572872 | tf_op jit(solution)/shard_map/ppermute | solution.py:17
  227.7 11.2 %copy-start.4 = (bf16[8,64,3,3,3]{1,0,4,3,2:T(8,128)(2,1)S(1)}, bf16[8,64,3,3,3]{1,0,4,3,2:T(8,128)(2,1)}, u32[]{:S(2)}) copy-start(bf16[8,64,3,3,3]{1,0,4,3,2:T(8,128)(2,1)} %param.9) | copy-start | bytes 82948
  258.9 2.9 copy-start.6
  264.7 11.7 %collective-permute-start.4 = (bf16[8,1,32,128]{2,0,3,1:T(8,128)(2,1)}, bf16[8,1,32,128]{2,0,3,1:T(8,128)(2,1)S(1)}, u32[]{:S(2)}, u32[]{:S(2)}) collective-permute-start(bf16[8,1,32,128]{2,0,3,1:T(8,128)(2,1)} %get-tuple-element.49), channel_id=1, source_target_pairs={{0,8},{8,16},{16,24},{24,32},{32,40},{40,48},{48,56},{56,64},{64,7... | collective-permute-start | bytes 196616 | tf_op jit(solution)/shard_map/ppermute | solution.py:16
  270.3 18.1 %collective-permute-start.5 = (bf16[8,1,32,128]{2,0,3,1:T(8,128)(2,1)S(1)}, bf16[8,1,32,128]{2,0,3,1:T(8,128)(2,1)S(1)}, u32[]{:S(2)}, u32[]{:S(2)}) collective-permute-start(bf16[8,1,32,128]{2,0,3,1:T(8,128)(2,1)S(1)} %get-tuple-element.50), channel_id=1, source_target_pairs={{8,0},{16,8},{24,16},{32,24},{40,32},{48,40},{56,48},{64,56},{72,6... | collective-permute-start | bytes 196616 | tf_op jit(solution)/shard_map/ppermute | solution.py:17
  289.4 621.7 %all-reduce.3.cloned.1.call-start = ((), (), s32[]{:S(2)}) async-start(), calls=%async_computation.3 | async-start | bytes 444416 | tf_op jit(solution)/shard_map/psum | solution.py:89
  315.4 2.7 slice-start
  315.4 2.7 slice-start.1
  455.7 1.9 copy-start.2
  472.0 441.9 %copy-start.1 = (bf16[8,64,3,3,3]{1,0,4,3,2:T(8,128)(2,1)S(1)}, bf16[8,64,3,3,3]{1,0,4,3,2:T(8,128)(2,1)}, u32[]{:S(2)}) copy-start(bf16[8,64,3,3,3]{1,0,4,3,2:T(8,128)(2,1)} %param.7) | copy-start | bytes 82948
Sparse Core Ops, SparseCore 0:
  9.8 40.2 all-gather.3
  101.7 71.3 all-gather.5
  289.5 55.8 all-gather.7
  485.7 425.3 all-reduce.2
where the time goes:
time: 928 us; the launch traced here: 921 us
  waiting for transfers between devices  564 us (61%)
  matrix products  150 us (16%)
  local copies, waits for them, and re-layouts  126 us (14%)
  other arithmetic  23.9 us (3%)
  blocking collectives  21.3 us (2%)
  starting transfers between devices  20.9 us (2%)
  between operations  14.4 us (2%)
    psum x1, waiting for transfers between devices, shards(): summed = lax.psum((kernel_one, offset_one, kernel_two, offset_two), 'space')  425 us
    all_gather x2, waiting for transfers between devices, surround(): gathered = lax.all_gather(field, 'chan', axis=0, tiled=True)  114 us
    transpose x2, matrix products, kernel_grad_inner(): return jnp.transpose(result, (1, 0, 2, 3, 4))  101 us
    broadcast_in_dim x6, local copies, waits for them, and re-layouts, conv_inner(): inputs[None]  41.7 us
    conv_general_dilated x2, matrix products, conv_inner(): lax.conv_general_dilated(inputs[None], kernel, (1, 1, 1), ((0, 0), (side,...  38.8 us
    all_gather x1, blocking collectives, shards(): lax.all_gather(weight_two, 'chan', axis=0, tiled=True)  21.3 us
    conv_general_dilated x6, local copies, waits for them, and re-layouts, conv_inner(): lax.conv_general_dilated(inputs[None], kernel, (1, 1, 1), ((0, 0), (side,...  18.9 us
  transfers between devices with their start and end apart: 10, of which 9 were waited for; matrix products, arithmetic and copies ran while one was open for 16% of the time, Pallas kernels for 0%

commit v1 on v0

v1 whole, which is shorter than its diff:
```python
import jax
import jax.numpy as jnp
from jax import lax
from jax.experimental import pallas as pl
from jax.experimental.pallas import tpu as pltpu
from jax.sharding import Mesh, PartitionSpec as P

SLOPE = 0.2
F32 = jnp.float32
BF16 = jnp.bfloat16
SPACE = ("x", "h", "y")
PLANE = ("x", "y")
CHAN = ("l", "c")
CONTRACT_LAST = (((1,), (1,)), ((), ()))
VMEM_LIMIT = 48 * 1024 * 1024


def leaky(value):
    return jnp.where(value > 0, value, SLOPE * value)


def lanes(shape):
    return lax.broadcasted_iota(jnp.int32, shape, 1)


def tile(index, count=1):
    return pl.ds(pl.multiple_of(index * 128, 128), count * 128)


def along_y(array, step):
    y = lanes(array.shape) % 32
    edge = 0 if step == 1 else 31
    moved = pltpu.roll(array, step % array.shape[1], 1)
    return jnp.where(y == edge, 0.0, moved)


def add_y_taps(product):
    width = product.shape[1]
    split = product.reshape(8, 3, 8, width)
    below, middle, above = (split[:, k].reshape(64, width) for k in range(3))
    return middle + along_y(below, 1) + along_y(above, -1)


def stack_y(delta):
    parts = [along_y(delta, -1), delta, along_y(delta, 1)]
    parts = [part.reshape(8, 1, 8, part.shape[1]) for part in parts]
    return jnp.concatenate(parts, axis=1).reshape(192, delta.shape[1]).astype(BF16)


def stack_x(act):
    return (
        pltpu.roll(act, 32, 1).astype(BF16),
        act.astype(BF16),
        pltpu.roll(act, 96, 1).astype(BF16),
    )


def prepare_kernel(volume, cotangent, out, turned):
    turned[...] = jnp.zeros_like(turned)
    for ch in range(8):
        both = jnp.concatenate([volume[ch], cotangent[ch]], axis=0).astype(F32)
        turned[pl.ds(24 + ch, 128, stride=8), :] = both.T
    for block in range(8):
        out[block] = turned[pl.ds(block * 128, 176), :].astype(BF16)


def unpack_kernel(received, field, packed):
    low = lanes((64, 128)) < 64

    def body(j, carry):
        rows = pl.ds(pl.multiple_of(j * 16, 16), 16)
        pieces = [received[src, rows, :].astype(F32) for src in range(8)]
        even = jnp.concatenate([piece[:8] for piece in pieces], axis=0)
        odd = jnp.concatenate([piece[8:] for piece in pieces], axis=0)
        field[2 * j] = even.astype(BF16)
        field[2 * j + 1] = odd.astype(BF16)
        packed[j] = jnp.where(low, even, pltpu.roll(odd, 64, 1)).astype(BF16)
        return carry

    lax.fori_loop(0, 11, body, 0)


def forward_kernel(place, field, before, after, weights, act, wide, delta, feats, to_prev, to_next, pre, bias):
    lane = lanes((64, 128))

    def widen(j, carry):
        p = before[j].astype(F32)
        n = after[j].astype(F32)
        for half in range(2):
            row = 2 * j + half
            own = field[row].astype(F32)
            low = p if half == 0 else pltpu.roll(p, 64, 1)
            high = pltpu.roll(n, 64, 1) if half == 0 else n
            minus = jnp.where(lane < 64, low, pltpu.roll(own, 64, 1))
            plus = jnp.where(lane < 64, own, high)
            zero = jnp.where(lane < 32, pltpu.roll(minus, 96, 1), pltpu.roll(plus, 32, 1))
            wide[0:64, tile(row)] = minus.astype(BF16)
            wide[64:128, tile(row)] = zero.astype(BF16)
            wide[128:192, tile(row)] = plus.astype(BF16)
        return carry

    lax.fori_loop(0, 11, widen, 0)

    extra = weights[:, 1152:1280].astype(F32).reshape(8, 3, 8, 128)[:, 0].reshape(64, 128)
    for layer in range(2):
        parts = [extra[:, 3 * layer + k : 3 * layer + k + 1] for k in range(3)]
        bias[layer] = jnp.broadcast_to(parts[0] + parts[1] + parts[2], (64, 128))

    first, last = (place[0] == 0, place[0] == 31)
    outside = jnp.logical_or(
        jnp.logical_and(lane < 32, first), jnp.logical_and(lane >= 96, last)
    )

    def one(m, carry):
        product = sum(
            jnp.dot(
                weights[:, dz * 192 : dz * 192 + 192],
                wide[:, tile(2 * m + dz, 2)],
                preferred_element_type=F32,
            )
            for dz in range(3)
        )
        for half in range(2):
            row = 2 * m + half
            value = leaky(add_y_taps(product[:, half * 128 : half * 128 + 128]) + bias[0])
            z = place[1] * 16 + row - 2
            gone = jnp.logical_or(outside, jnp.logical_or(z < 0, z > 127))
            minus, zero, plus = stack_x(jnp.where(gone, 0.0, value))
            act[0:64, tile(row)] = minus
            act[64:128, tile(row)] = zero
            act[128:192, tile(row)] = plus
        return carry

    lax.fori_loop(0, 10, one, 0)

    own_lanes = jnp.logical_and(lane >= 32, lane < 96)

    def two(m, carry):
        product = sum(
            jnp.dot(
                weights[:, 576 + dz * 192 : 768 + dz * 192],
                act[:, tile(2 * m + dz, 2)],
                preferred_element_type=F32,
            )
            for dz in range(3)
        )
        for half in range(2):
            row = 2 * m + half
            value = add_y_taps(product[:, half * 128 : half * 128 + 128]) + bias[1]
            cot = pltpu.roll(field[row + 2].astype(F32), 96, 1)
            grad = jnp.where(value > 0, cot, SLOPE * cot)
            delta[row] = jnp.where(own_lanes, grad, 0.0).astype(BF16)
            pre[row] = leaky(value)
        return carry

    lax.fori_loop(0, 9, two, 0)

    for z in range(8):
        low = pltpu.roll(pre[z + 1], 96, 1)
        high = pltpu.roll(pre[z + 9], 32, 1)
        feats[z] = jnp.where(lane < 64, low, high).astype(BF16)

    for g in range(5):
        left = jnp.zeros((64, 128), F32)
        right = jnp.zeros((64, 128), F32)
        for i in range(4):
            if g + 5 * i < 18:
                row = delta[g + 5 * i].astype(F32)
                here = jnp.logical_and(lane >= 32 * i, lane < 32 * i + 32)
                left = jnp.where(here, pltpu.roll(row, (32 * i - 32) % 128, 1), left)
                right = jnp.where(here, pltpu.roll(row, (32 * i - 64) % 128, 1), right)
        to_prev[g] = left.astype(BF16)
        to_next[g] = right.astype(BF16)


def kernel_grad(stacked, wide, start, total, out, column):
    for dz in range(3):
        product = lax.dot_general(
            stacked[...],
            wide[:, (start + dz) * 128 : (start + dz) * 128 + 2048],
            CONTRACT_LAST,
            preferred_element_type=F32,
        )
        out[:, column + dz * 192 : column + dz * 192 + 192] = product.astype(BF16)
    summed = jnp.broadcast_to(jnp.sum(total, axis=1, keepdims=True), (64, 64))
    rows = jnp.broadcast_to(summed.reshape(8, 1, 8, 64), (8, 3, 8, 64)).reshape(192, 64)
    out[:, column + 576 : column + 640] = rows.astype(BF16)


def second_grad_kernel(delta, act, out, stacked):
    def body(z, total):
        value = delta[z + 1].astype(F32)
        stacked[:, tile(z)] = stack_y(value)
        return total + value

    total = lax.fori_loop(0, 16, body, jnp.zeros((64, 128), F32))
    kernel_grad(stacked, act, 1, total, out, 0)


def backward_kernel(delta, from_prev, from_next, weights, act, wide, grad_two, out, turned, stacked, own):
    lane = lanes((64, 128))
    for k in range(9):
        block = weights[:, 576 + 64 * k : 640 + 64 * k].astype(F32)
        turned[64 * k : 64 * k + 64, :] = block.T.astype(BF16)

    for row in range(18):
        g, i = (row % 5, row // 5)
        left = pltpu.roll(from_prev[g].astype(F32), (-32 * i) % 128, 1)
        right = pltpu.roll(from_next[g].astype(F32), (96 - 32 * i) % 128, 1)
        value = jnp.where(lane < 32, left, jnp.where(lane >= 96, right, delta[row].astype(F32)))
        stacked[:, row * 128 : row * 128 + 128] = stack_y(value)

    own_lanes = jnp.logical_and(lane >= 32, lane < 96)

    def body(m, total):
        product = sum(
            jnp.dot(
                turned[dz * 192 : dz * 192 + 192, :],
                stacked[:, tile(2 * m + 2 - dz, 2)],
                preferred_element_type=F32,
            )
            for dz in range(3)
        )
        for half in range(2):
            part = product[:, half * 128 : half * 128 + 128]
            back = part[64:128] + pltpu.roll(part[0:64], 96, 1) + pltpu.roll(part[128:192], 32, 1)
            positive = act[64:128, tile(2 * m + 2 + half)].astype(F32) > 0
            value = jnp.where(positive, back, SLOPE * back)
            value = jnp.where(own_lanes, value, 0.0).astype(BF16).astype(F32)
            own[:, tile(2 * m + half)] = stack_y(value)
            total = total + value
        return total

    total = lax.fori_loop(0, 8, body, jnp.zeros((64, 128), F32))
    out[:, 0:640] = grad_two[...]
    kernel_grad(own, wide, 2, total, out, 640)


def call(kernel, out_shapes, scratch, *args, scalars=0, flops=0):
    vmem = pl.BlockSpec(memory_space=pltpu.VMEM)
    smem = pl.BlockSpec(memory_space=pltpu.SMEM)
    outs = [jax.ShapeDtypeStruct(shape, dtype) for shape, dtype in out_shapes]
    size = sum(a.size * a.dtype.itemsize for a in args)
    size += sum(o.size * o.dtype.itemsize for o in outs)
    return pl.pallas_call(
        kernel,
        out_shape=outs,
        in_specs=[smem] * scalars + [vmem] * (len(args) - scalars),
        out_specs=[vmem] * len(outs),
        scratch_shapes=[pltpu.VMEM(shape, dtype) for shape, dtype in scratch],
        compiler_params=pltpu.CompilerParams(vmem_limit_bytes=VMEM_LIMIT),
        cost_estimate=pl.CostEstimate(flops=flops, bytes_accessed=size, transcendentals=0),
    )(*args)


def weight_rows(kernel):
    return jnp.transpose(kernel, (3, 0, 4, 2, 1)).reshape(24, 576)


def three_parts(bias):
    high = lax.reduce_precision(bias, 8, 7)
    middle = lax.reduce_precision(bias - high, 8, 7)
    low = bias - high - middle
    return [high, middle, low]


def restore(rows, column, factor):
    kernel = rows[:, column : column + 576].reshape(3, 8, 3, 3, 64)
    return (
        jnp.transpose(kernel, (1, 4, 3, 0, 2)) * factor,
        rows[0:8, column + 576] * factor,
    )


def shards(volume, weight_one, bias_one, weight_two, bias_two, cotangent):
    factor = float(volume.shape[1] * 32 * volume.shape[2] * volume.shape[3]) ** (-0.5)
    s, c = (lax.axis_index(SPACE), lax.axis_index(CHAN))
    up = [(i, i + 1) for i in range(31)]
    down = [(i + 1, i) for i in range(31)]

    offsets = jnp.stack(three_parts(bias_one) + three_parts(bias_two), axis=1)
    offsets = jnp.pad(offsets, ((0, 16), (0, 122))).astype(BF16)
    local = jnp.concatenate([weight_rows(weight_one), weight_rows(weight_two), offsets], axis=1)
    weights = lax.all_gather(local, CHAN, axis=0, tiled=True)

    (pieces,) = call(
        prepare_kernel,
        [((8, 176, 128), BF16)],
        [((1072, 128), F32)],
        volume.reshape(8, 64, 128),
        cotangent.reshape(8, 64, 128),
    )
    received = lax.all_to_all(pieces, CHAN, 0, 0)
    field, packed = call(
        unpack_kernel, [((22, 64, 128), BF16), ((11, 64, 128), BF16)], [], received
    )
    before = lax.ppermute(packed, SPACE, up)
    after = lax.ppermute(packed, SPACE, down)

    place = jnp.stack([s, c]).astype(jnp.int32)
    act, wide, delta, feats, to_prev, to_next = call(
        forward_kernel,
        [
            ((192, 2560), BF16),
            ((192, 2816), BF16),
            ((18, 64, 128), BF16),
            ((8, 64, 128), BF16),
            ((5, 64, 128), BF16),
            ((5, 64, 128), BF16),
        ],
        [((18, 64, 128), F32), ((2, 64, 128), F32)],
        place,
        field,
        before,
        after,
        weights,
        scalars=1,
        flops=2 * 192 * 576 * 128 * 38,
    )
    from_next = lax.ppermute(to_prev, SPACE, down)
    from_prev = lax.ppermute(to_next, SPACE, up)
    (grad_two,) = call(
        second_grad_kernel,
        [((192, 640), BF16)],
        [((192, 2048), BF16)],
        delta,
        act,
        flops=2 * 192 * 576 * 2048,
    )
    (grads,) = call(
        backward_kernel,
        [((192, 1280), BF16)],
        [((576, 192), BF16), ((192, 2304), BF16), ((192, 2048), BF16)],
        delta,
        from_prev,
        from_next,
        weights,
        act,
        wide,
        grad_two,
        flops=4 * 192 * 576 * 2048,
    )

    shares = lax.all_to_all(grads.reshape(8, 24, 1280), CHAN, 0, 0)
    mine = jnp.sum(shares.astype(F32), axis=0)
    mine = jnp.pad(mine.reshape(240, 128), ((0, 16), (0, 0))).reshape(16, 16, 128)
    shares = lax.all_to_all(mine, PLANE, 0, 0)
    part = jnp.sum(shares, axis=0)
    part = part + lax.ppermute(part, "h", [(0, 1), (1, 0)])
    whole = lax.all_to_all(jnp.broadcast_to(part, (16, 16, 128)), PLANE, 0, 0)
    rows = whole.reshape(256, 128)[:240].reshape(24, 1280)
    kernel_two, offset_two = restore(rows, 0, factor)
    kernel_one, offset_one = restore(rows, 640, factor)

    feats = jnp.transpose(feats.reshape(8, 8, 8, 128), (1, 0, 2, 3))
    feats = lax.all_to_all(feats, CHAN, 0, 0)
    feats = feats.reshape(8, 8, 8, 2, 2, 32)
    features = jnp.transpose(feats, (2, 4, 5, 0, 3, 1)).reshape(8, 2, 32, 128)
    return features, kernel_one, offset_one, kernel_two, offset_two


def solution(mesh):
    fine = Mesh(mesh.devices.reshape(4, 2, 4, 4, 2), ("x", "h", "y", "l", "c"))
    field = P(CHAN, SPACE, None, None)
    kernel = P(CHAN, None, None, None, None)
    in_specs = (field, kernel, P(CHAN), kernel, P(CHAN), field)
    out_specs = (field, kernel, P(CHAN), kernel, P(CHAN))
    return jax.shard_map(shards, mesh=fine, in_specs=in_specs, out_specs=out_specs, check_vma=False)
```

time: 928 us -> 145 us (0.16)
  waiting for transfers between devices: 564 us -> 36.8 us
  matrix products: 150 us -> 0 us
  local copies, waits for them, and re-layouts: 126 us -> 7.76 us
  other arithmetic: 23.9 us -> 0.93 us
  starting transfers between devices: 20.9 us -> 42.3 us
  Pallas kernels: 0 us -> 19.8 us
  between operations: 14.4 us -> 0.85 us
  blocking collectives: 21.3 us -> 34.7 us
    psum x1 -> x0, waiting for transfers between devices: 425 us -> none  [shards(): summed = lax.psum((kernel_one, offset_one, kernel_two, offset_two), 'space')]
    all_gather x3 -> x0, waiting for transfers between devices: 114 us -> none  [the longest x2 114 us: surround(): gathered = lax.all_gather(field, 'chan', axis=0, tiled=True)]
    transpose x2 -> x0, matrix products: 101 us -> none  [kernel_grad_inner(): return jnp.transpose(result, (1, 0, 2, 3, 4))]
    broadcast_in_dim x8 -> x1, local copies, waits for them, and re-layouts: 51.1 us -> 0.66 us  [shards(): whole = lax.all_to_all(jnp.broadcast_to(part, (16, 16, 128)), PLANE, 0, 0)]
    conv_general_dilated x3 -> x0, matrix products: 49.4 us -> none  [the longest x2 38.8 us: conv_inner(): lax.conv_general_dilated(inputs[None], kernel, (1, 1, 1), ((0, 0), (side,...]
    all_to_all x0 -> x4, starting transfers between devices: none -> 28.5 us  [the longest x1 14.2 us: shards(): shares = lax.all_to_all(mine, PLANE, 0, 0)]
    conv_general_dilated x9 -> x0, local copies, waits for them, and re-layouts: 23.7 us -> none  [the longest x6 18.9 us: conv_inner(): lax.conv_general_dilated(inputs[None], kernel, (1, 1, 1), ((0, 0), (side,...]
    all_to_all x0 -> x4, waiting for transfers between devices: none -> 21.4 us  [the longest x1 10.6 us: shards(): received = lax.all_to_all(pieces, CHAN, 0, 0)]
  transfers between devices with their start and end apart: 10 -> 9, of which waited for: 9 -> 5; matrix products, arithmetic and copies ran while one was open for 16% -> 2% of each run, Pallas kernels for 0% -> 2%
where the time goes in v1:
time: 145 us; the launch traced here: 143 us
  starting transfers between devices  42.3 us (29%)
  waiting for transfers between devices  36.8 us (25%)
  blocking collectives  34.7 us (24%)
  Pallas kernels  19.8 us (14%)
  local copies, waits for them, and re-layouts  7.76 us (5%)
    all_to_all x1, blocking collectives, shards(): shares = lax.all_to_all(grads.reshape(8, 24, 1280), CHAN, 0, 0)  19.9 us
    pallas_call x5, Pallas kernels, call(): pl.pallas_call(kernel, out_shape=outs, in_specs=[smem] * scalars + [vmem]...  19.8 us
    all_gather x1, blocking collectives, shards(): weights = lax.all_gather(local, CHAN, axis=0, tiled=True)  14.8 us
    all_to_all x1, starting transfers between devices, shards(): shares = lax.all_to_all(mine, PLANE, 0, 0)  14.2 us
    all_to_all x1, waiting for transfers between devices, shards(): received = lax.all_to_all(pieces, CHAN, 0, 0)  10.6 us
    ppermute x1, waiting for transfers between devices, shards(): from_next = lax.ppermute(to_prev, SPACE, down)  9.87 us
    all_to_all x1, starting transfers between devices, shards(): received = lax.all_to_all(pieces, CHAN, 0, 0)  5.9 us
    all_to_all x1, waiting for transfers between devices, shards(): shares = lax.all_to_all(mine, PLANE, 0, 0)  5.71 us
  transfers between devices with their start and end apart: 9, of which 5 were waited for; matrix products, arithmetic and copies ran while one was open for 2% of the time, Pallas kernels for 2%

profile of v1, /device:TPU:8, one launch (start us, length us, event | category | flops | bytes accessed | tf_op | source)
XLA Modules:
  0.0 143.1 jit_solution(15010602818527348080)
XLA Ops:
  0.7 0.9 copy-done
  1.6 0.9 copy-done.1
  2.5 0.9 shard_map.101
  3.4 5.9 %all-to-all-start = ((bf16[8,176,128]{2,1,0:T(8,128)(2,1)}), bf16[8,176,128]{2,1,0:T(8,128)(2,1)S(1)}, u32[]{:S(2)}, u32[]{:S(2)}) async-start(bf16[8,176,128]{2,1,0:T(8,128)(2,1)} %shard_map.101), calls=%async_computation | async-start | bytes 720896 | tf_op jit(solution)/shard_map/all_to_all | solution.py:293
  9.3 0.1 copy.48
  9.4 0.1 copy.51
  9.5 0.1 copy.50
  9.6 0.1 copy.49
  9.7 0.1 copy.47
  9.8 0.1 copy.46
  9.9 0.1 reshape.58
  10.1 0.1 reshape.59
  10.2 0.1 stack.46
  10.3 0.1 concatenate.3
  10.4 0.1 pad_add_fusion.place
  10.5 10.6 %all-to-all-done.received = bf16[8,176,128]{2,1,0:T(8,128)(2,1)S(1)} async-done(((bf16[8,176,128]{2,1,0:T(8,128)(2,1)}), bf16[8,176,128]{2,1,0:T(8,128)(2,1)S(1)}, u32[]{:S(2)}, u32[]{:S(2)}) %all-to-all-start) | async-done | bytes 360480 | tf_op jit(solution)/shard_map/all_to_all | solution.py:293
  21.1 0.8 shard_map.102
  22.0 2.3 %collective-permute-start.1 = (bf16[11,64,128]{2,1,0:T(8,128)(2,1)S(1)}, bf16[11,64,128]{2,1,0:T(8,128)(2,1)S(1)}, u32[]{:S(2)}, u32[]{:S(2)}) collective-permute-start(bf16[11,64,128]{2,1,0:T(8,128)(2,1)S(1)} %get-tuple-element.14), channel_id=1, source_target_pairs={{8,0},{16,8},{24,16},{32,24},{40,32},{48,40},{56,48},{64,56},{72,6... | collective-permute-start | bytes 540680 | tf_op jit(solution)/shard_map/ppermute | solution.py:298
  24.3 3.5 %collective-permute-start = (bf16[11,64,128]{2,1,0:T(8,128)(2,1)S(1)}, bf16[11,64,128]{2,1,0:T(8,128)(2,1)S(1)}, u32[]{:S(2)}, u32[]{:S(2)}) collective-permute-start(bf16[11,64,128]{2,1,0:T(8,128)(2,1)S(1)} %get-tuple-element.14), channel_id=1, source_target_pairs={{0,8},{8,16},{16,24},{24,32},{32,40},{40,48},{48,56},{56,64},{64,7... | collective-permute-start | bytes 540680 | tf_op jit(solution)/shard_map/ppermute | solution.py:297
  27.8 14.8 %all_gather.3.weights = bf16[192,1280]{1,0:T(8,128)(2,1)S(1)} all-gather(bf16[24,1280]{1,0:T(8,128)(2,1)S(1)} %concatenate.3), channel_id=1, replica_groups=mesh['x'=4,'h'=2,'y'=4,'l'=4,'c'=2] {'l','c'}, dimensions={0}, use_global_device_ids=true | all-gather | bytes 552960 | tf_op jit(solution)/shard_map/all_gather | solution.py:284
  42.7 10.1 %shard_map.103 = (bf16[192,2560]{1,0:T(8,128)(2,1)S(1)}, bf16[192,2816]{1,0:T(8,128)(2,1)S(1)}, bf16[18,64,128]{2,1,0:T(8,128)(2,1)S(1)}, bf16[8,64,128]{2,1,0:T...) custom-call(s32[2]{0:T(128)S(1)} %pad_add_fusion.place, ...), custom_call_target="tpu_custom_call" | custom-call | flops 1075838976 | bytes 3866632 | tf_op jit(solution)/shard_map/pallas_call | solution.py:245
  52.7 3.5 %collective-permute-start.2 = (bf16[5,64,128]{2,1,0:T(8,128)(2,1)S(1)}, bf16[5,64,128]{2,1,0:T(8,128)(2,1)S(1)}, u32[]{:S(2)}, u32[]{:S(2)}) collective-permute-start(bf16[5,64,128]{2,1,0:T(8,128)(2,1)S(1)} %get-tuple-element.17), channel_id=1, source_target_pairs={{0,8},{8,16},{16,24},{24,32},{32,40},{40,48},{48,56},{56,64},{64,7... | collective-permute-start | bytes 245768 | tf_op jit(solution)/shard_map/ppermute | solution.py:321
  56.2 2.4 %collective-permute-start.3 = (bf16[5,64,128]{2,1,0:T(8,128)(2,1)S(1)}, bf16[5,64,128]{2,1,0:T(8,128)(2,1)S(1)}, u32[]{:S(2)}, u32[]{:S(2)}) collective-permute-start(bf16[5,64,128]{2,1,0:T(8,128)(2,1)S(1)} %get-tuple-element.18), channel_id=1, source_target_pairs={{8,0},{16,8},{24,16},{32,24},{40,32},{48,40},{56,48},{64,56},{72,6... | collective-permute-start | bytes 245768 | tf_op jit(solution)/shard_map/ppermute | solution.py:320
  58.6 2.2 %shard_map.104.grad_two = bf16[192,640]{1,0:T(8,128)(2,1)S(1)} custom-call(bf16[18,64,128]{2,1,0:T(8,128)(2,1)S(1)} %get-tuple-element.16.delta, bf16[192,2560]{1,0:T(8,128)(2,1)S(1)} %get-tuple-element.19.act), custom_call_target="tpu_custom_call" | custom-call | flops 452984832 | bytes 1523712 | tf_op jit(solution)/shard_map/pallas_call | solution.py:245
  60.8 0.0 collective-permute-done.2.from_prev
  60.8 9.9 %collective-permute-done.3.from_next = bf16[5,64,128]{2,1,0:T(8,128)(2,1)S(1)} collective-permute-done((bf16[5,64,128]{2,1,0:T(8,128)(2,1)S(1)}, bf16[5,64,128]{2,1,0:T(8,128)(2,1)S(1)}, u32[]{:S(2)}, u32[]{:S(2)}) %collective-permute-start.3) | collective-permute-done | bytes 81952 | tf_op jit(solution)/shard_map/ppermute | solution.py:320
  70.7 5.8 %shard_map.105 = bf16[192,1280]{1,0:T(8,128)(2,1)S(1)} custom-call(bf16[18,64,128]{2,1,0:T(8,128)(2,1)S(1)} %get-tuple-element.16.delta, bf16[5,64,128]{2,1,0:T(8,128)(2,1)S(1)} %collective-permute-done.2.from_prev, bf16[5,64,128]{2,1,0:T(8,128)(2,1)S(1)} %collective-permute-done.3.from_next, bf16[192,1280]{1,0:T(8,128)(2,1)S(1)} %all_gather.3.weights, ...), custom_call_target="tpu_custom_call" | custom-call | flops 905969664 | bytes 3751936 | tf_op jit(solution)/shard_map/pallas_call | solution.py:245
  76.5 19.9 %all_to_all.25 = bf16[8,24,1280]{2,1,0:T(8,128)(2,1)S(1)} all-to-all(bf16[8,24,1280]{2,1,0:T(8,128)(2,1)S(1)} %bitcast.31), channel_id=1, replica_groups=mesh['x'=4,'h'=2,'y'=4,'l'=4,'c'=2] {'l','c'}, dimensions={0} | all-to-all | bytes 983040 | tf_op jit(solution)/shard_map/all_to_all | solution.py:344
  96.3 0.1 convert_reduce_fusion
  96.4 0.7 pad.10
  97.1 14.2 %all-to-all-start.3 = ((f32[16,16,128]{2,1,0:T(8,128)}), f32[16,16,128]{2,1,0:T(8,128)S(1)}, u32[]{:S(2)}, u32[]{:S(2)}) async-start(f32[16,16,128]{2,1,0:T(8,128)} %bitcast.17), calls=%async_computation.3 | async-start | bytes 262144 | tf_op jit(solution)/shard_map/all_to_all | solution.py:347
  111.2 0.7 copy_bitcast_fusion
  111.9 5.7 %all-to-all-done.3 = f32[16,16,128]{2,1,0:T(8,128)S(1)} async-done(((f32[16,16,128]{2,1,0:T(8,128)}), f32[16,16,128]{2,1,0:T(8,128)S(1)}, u32[]{:S(2)}, u32[]{:S(2)}) %all-to-all-start.3) | async-done | bytes 131104 | tf_op jit(solution)/shard_map/all_to_all | solution.py:347
  117.6 3.4 %all-to-all-start.1 = ((bf16[8,8,8,128]{3,2,1,0:T(8,128)(2,1)}), bf16[8,8,8,128]{3,2,1,0:T(8,128)(2,1)S(1)}, u32[]{:S(2)}, u32[]{:S(2)}) async-start(bf16[8,8,8,128]{3,2,1,0:T(8,128)(2,1)} %copy_bitcast_fusion), calls=%async_computation.1 | async-start | bytes 262144 | tf_op jit(solution)/shard_map/all_to_all | solution.py:356
  121.0 2.2 %collective-permute-start.4 = (f32[16,128]{1,0:T(8,128)S(1)}, f32[16,128]{1,0:T(8,128)S(1)}, u32[]{:S(2)}, u32[]{:S(2)}) collective-permute-start(f32[16,128]{1,0:T(8,128)S(1)} %reduce_sum.19), channel_id=1, source_target_pairs={{0,32},{32,0},{1,33},{33,1},{2,34},{34,2},{3,35},{35,3},{4,36},{36... | collective-permute-start | bytes 24584 | tf_op jit(solution)/shard_map/ppermute | solution.py:349
  123.2 5.5 %collective-permute-done.4 = f32[16,128]{1,0:T(8,128)S(1)} collective-permute-done((f32[16,128]{1,0:T(8,128)S(1)}, f32[16,128]{1,0:T(8,128)S(1)}, u32[]{:S(2)}, u32[]{:S(2)}) %collective-permute-start.4) | collective-permute-done | bytes 8224 | tf_op jit(solution)/shard_map/ppermute | solution.py:349
  128.7 0.0 all-to-all-done.1
  128.7 0.7 broadcast_in_dim.3
  129.3 5.1 %all-to-all-start.4 = ((f32[16,16,128]{2,1,0:T(8,128)}), f32[16,16,128]{2,1,0:T(8,128)S(1)}, u32[]{:S(2)}, u32[]{:S(2)}) async-start(f32[16,16,128]{2,1,0:T(8,128)} %broadcast_in_dim.3), calls=%async_computation.4 | async-start | bytes 262144 | tf_op jit(solution)/shard_map/all_to_all | solution.py:350
  134.4 0.2 reshape.61
  134.6 0.2 copy.53
  134.8 0.8 copy.54
  135.7 5.1 %all-to-all-done.4 = f32[16,16,128]{2,1,0:T(8,128)S(1)} async-done(((f32[16,16,128]{2,1,0:T(8,128)}), f32[16,16,128]{2,1,0:T(8,128)S(1)}, u32[]{:S(2)}, u32[]{:S(2)}) %all-to-all-start.4) | async-done | bytes 131104 | tf_op jit(solution)/shard_map/all_to_all | solution.py:350
  140.8 0.7 fusion
  141.6 0.1 mul.48
  141.7 0.7 copy.56
  142.3 0.1 mul.43
  142.5 0.7 copy.55
  (23 shorter events, 0.2 us)
Async XLA Ops:
  0.6 8.7 %copy-start.4 = (f32[8]{0:T(128)S(1)}, f32[8]{0:T(128)}, u32[]{:S(2)}) copy-start(f32[8]{0:T(128)} %param.8) | copy-start | bytes 100
  0.6 8.8 %copy-start.5 = (f32[8]{0:T(128)S(1)}, f32[8]{0:T(128)}, u32[]{:S(2)}) copy-start(f32[8]{0:T(128)} %param.10) | copy-start | bytes 100
  0.7 0.9 copy-start
  1.6 0.9 copy-start.1
  2.5 7.4 %copy-start.2 = (bf16[8,64,3,3,3]{1,0,4,3,2:T(8,128)(2,1)S(1)}, bf16[8,64,3,3,3]{1,0,4,3,2:T(8,128)(2,1)}, u32[]{:S(2)}) copy-start(bf16[8,64,3,3,3]{1,0,4,3,2:T(8,128)(2,1)} %param.7) | copy-start | bytes 82948
  2.5 7.6 %copy-start.3 = (bf16[8,64,3,3,3]{1,0,4,3,2:T(8,128)(2,1)S(1)}, bf16[8,64,3,3,3]{1,0,4,3,2:T(8,128)(2,1)}, u32[]{:S(2)}) copy-start(bf16[8,64,3,3,3]{1,0,4,3,2:T(8,128)(2,1)} %param.9) | copy-start | bytes 82948
  3.4 17.8 %all-to-all-start = ((bf16[8,176,128]{2,1,0:T(8,128)(2,1)}), bf16[8,176,128]{2,1,0:T(8,128)(2,1)S(1)}, u32[]{:S(2)}, u32[]{:S(2)}) async-start(bf16[8,176,128]{2,1,0:T(8,128)(2,1)} %shard_map.101), calls=%async_computation | async-start | bytes 720896 | tf_op jit(solution)/shard_map/all_to_all | solution.py:293
  22.0 20.7 %collective-permute-start.1 = (bf16[11,64,128]{2,1,0:T(8,128)(2,1)S(1)}, bf16[11,64,128]{2,1,0:T(8,128)(2,1)S(1)}, u32[]{:S(2)}, u32[]{:S(2)}) collective-permute-start(bf16[11,64,128]{2,1,0:T(8,128)(2,1)S(1)} %get-tuple-element.14), channel_id=1, source_target_pairs={{8,0},{16,8},{24,16},{32,24},{40,32},{48,40},{56,48},{64,56},{72,6... | collective-permute-start | bytes 540680 | tf_op jit(solution)/shard_map/ppermute | solution.py:298
  24.3 18.3 %collective-permute-start = (bf16[11,64,128]{2,1,0:T(8,128)(2,1)S(1)}, bf16[11,64,128]{2,1,0:T(8,128)(2,1)S(1)}, u32[]{:S(2)}, u32[]{:S(2)}) collective-permute-start(bf16[11,64,128]{2,1,0:T(8,128)(2,1)S(1)} %get-tuple-element.14), channel_id=1, source_target_pairs={{0,8},{8,16},{16,24},{24,32},{32,40},{40,48},{48,56},{56,64},{64,7... | collective-permute-start | bytes 540680 | tf_op jit(solution)/shard_map/ppermute | solution.py:297
  52.7 8.0 %collective-permute-start.2 = (bf16[5,64,128]{2,1,0:T(8,128)(2,1)S(1)}, bf16[5,64,128]{2,1,0:T(8,128)(2,1)S(1)}, u32[]{:S(2)}, u32[]{:S(2)}) collective-permute-start(bf16[5,64,128]{2,1,0:T(8,128)(2,1)S(1)} %get-tuple-element.17), channel_id=1, source_target_pairs={{0,8},{8,16},{16,24},{24,32},{32,40},{40,48},{48,56},{56,64},{64,7... | collective-permute-start | bytes 245768 | tf_op jit(solution)/shard_map/ppermute | solution.py:321
  56.2 14.4 %collective-permute-start.3 = (bf16[5,64,128]{2,1,0:T(8,128)(2,1)S(1)}, bf16[5,64,128]{2,1,0:T(8,128)(2,1)S(1)}, u32[]{:S(2)}, u32[]{:S(2)}) collective-permute-start(bf16[5,64,128]{2,1,0:T(8,128)(2,1)S(1)} %get-tuple-element.18), channel_id=1, source_target_pairs={{8,0},{16,8},{24,16},{32,24},{40,32},{48,40},{56,48},{64,56},{72,6... | collective-permute-start | bytes 245768 | tf_op jit(solution)/shard_map/ppermute | solution.py:320
  97.1 20.6 %all-to-all-start.3 = ((f32[16,16,128]{2,1,0:T(8,128)}), f32[16,16,128]{2,1,0:T(8,128)S(1)}, u32[]{:S(2)}, u32[]{:S(2)}) async-start(f32[16,16,128]{2,1,0:T(8,128)} %bitcast.17), calls=%async_computation.3 | async-start | bytes 262144 | tf_op jit(solution)/shard_map/all_to_all | solution.py:347
  117.6 11.1 %all-to-all-start.1 = ((bf16[8,8,8,128]{3,2,1,0:T(8,128)(2,1)}), bf16[8,8,8,128]{3,2,1,0:T(8,128)(2,1)S(1)}, u32[]{:S(2)}, u32[]{:S(2)}) async-start(bf16[8,8,8,128]{3,2,1,0:T(8,128)(2,1)} %copy_bitcast_fusion), calls=%async_computation.1 | async-start | bytes 262144 | tf_op jit(solution)/shard_map/all_to_all | solution.py:356
  121.0 7.6 %collective-permute-start.4 = (f32[16,128]{1,0:T(8,128)S(1)}, f32[16,128]{1,0:T(8,128)S(1)}, u32[]{:S(2)}, u32[]{:S(2)}) collective-permute-start(f32[16,128]{1,0:T(8,128)S(1)} %reduce_sum.19), channel_id=1, source_target_pairs={{0,32},{32,0},{1,33},{33,1},{2,34},{34,2},{3,35},{35,3},{4,36},{36... | collective-permute-start | bytes 24584 | tf_op jit(solution)/shard_map/ppermute | solution.py:349
  129.3 11.4 %all-to-all-start.4 = ((f32[16,16,128]{2,1,0:T(8,128)}), f32[16,16,128]{2,1,0:T(8,128)S(1)}, u32[]{:S(2)}, u32[]{:S(2)}) async-start(f32[16,16,128]{2,1,0:T(8,128)} %broadcast_in_dim.3), calls=%async_computation.4 | async-start | bytes 262144 | tf_op jit(solution)/shard_map/all_to_all | solution.py:350

commit v2 on v0

v2 whole, which is shorter than its diff:
```python
import functools

import jax
import jax.numpy as jnp
from jax import lax
from jax.experimental import pallas as pl
from jax.experimental.pallas import tpu as pltpu
from jax.sharding import Mesh, PartitionSpec as P

SLOPE = 0.2
F32 = jnp.float32
BF16 = jnp.bfloat16
SPACE = ("x", "h", "y")
PLANE = ("x", "y")
CHAN = ("l", "c")
CONTRACT_LAST = (((1,), (1,)), ((), ()))
VMEM_LIMIT = 48 * 1024 * 1024


def leaky(value):
    return jnp.maximum(value, SLOPE * value)


def lanes(shape):
    return lax.broadcasted_iota(jnp.int32, shape, 1)


def tiles(index, count=1):
    return slice(index * 128, (index + count) * 128)


def along_y(array, step):
    y = lanes(array.shape) % 32
    edge = 0 if step == 1 else 31
    moved = pltpu.roll(array, step % array.shape[1], 1)
    return jnp.where(y == edge, 0.0, moved)


def add_y_taps(product):
    width = product.shape[1]
    split = product.reshape(8, 3, 8, width)
    below, middle, above = (split[:, k].reshape(64, width) for k in range(3))
    return middle + along_y(below, 1) + along_y(above, -1)


def stack_y(delta):
    parts = [along_y(delta, -1), delta, along_y(delta, 1)]
    parts = [part.reshape(8, 1, 8, part.shape[1]) for part in parts]
    return jnp.concatenate(parts, axis=1).reshape(192, delta.shape[1]).astype(BF16)


def conv_tiles(weights, column, stacked, start):
    return sum(
        jnp.dot(
            weights[:, column + dz * 192 : column + dz * 192 + 192],
            stacked[:, tiles(start + dz, 2)],
            preferred_element_type=F32,
        )
        for dz in range(3)
    )


def weight_prepare_kernel(weight_one, bias_one, weight_two, bias_two, units):
    row = lax.broadcasted_iota(jnp.int32, (8, 128), 0)
    lane = lanes((8, 128))

    rows = []
    for t in range(9):
        for dy in range(3):
            halves = []
            for half in range(2):
                layer, k = divmod(2 * t + half, 9)
                dz, dx = divmod(k, 3)
                halves.append((weight_two if layer else weight_one)[dx * 9 + dy * 3 + dz].astype(F32))
            rows.append(jnp.concatenate(halves, axis=1))
    packed = jnp.zeros((8, 128), F32)
    for layer, bias in enumerate((bias_one, bias_two)):
        value = sum(jnp.where(row == o, bias[o], 0.0) for o in range(8))
        for part in range(3):
            rounded = value.astype(BF16).astype(F32)
            packed = jnp.where(lane == 3 * layer + part, rounded, packed)
            value = value - rounded
    rows.append(packed)
    units[...] = jnp.concatenate(rows, axis=0).astype(BF16)


def prepare_kernel(place, volume, cotangent, out, held, turned, arrived):
    copies = [
        pltpu.make_async_copy(ref, held.at[k], arrived.at[k])
        for k, ref in enumerate((volume, cotangent))
    ]
    for copy in copies:
        copy.start()
    low = lanes((88, 128)) < 64
    turned[0:24] = jnp.zeros((24, 128), F32)
    turned[1048:1072] = jnp.zeros((24, 128), F32)
    for copy in copies:
        copy.wait()
    for ch in range(8):
        both = jnp.concatenate([held[0, ch], held[1, ch]], axis=0).astype(F32)
        turned[pl.ds(24 + ch, 128, stride=8), :] = both.T
    for block in range(8):
        target = jnp.where(place[3] == 1, 6 - 2 * (block // 2) + block % 2, block)
        rows = turned[block * 128 : block * 128 + 176].reshape(11, 2, 8, 128)
        even, odd = (rows[:, k].reshape(88, 128) for k in range(2))
        field = jnp.where(low, even, pltpu.roll(odd, 64, 1))
        left = turned[block * 128 + 16 : block * 128 + 96]
        right = turned[block * 128 + 80 : block * 128 + 160]
        cots = jnp.where(low[:80], pltpu.roll(left, 64, 1), right)
        out[target] = jnp.concatenate([field, cots], axis=0).astype(BF16)


def unpack_kernel(received, field, cots):
    pieces = [received[src].astype(F32) for src in range(8)]
    for j in range(21):
        both = jnp.concatenate([piece[8 * j : 8 * j + 8] for piece in pieces], axis=0).astype(BF16)
        if j < 11:
            field[j] = both
        else:
            cots[j - 11] = both


def weights_kernel(place, mine, other, out, back, bias):
    first = place[2] == 0
    for k in range(4):
        group = lax.rem(place[4] + 4 - k, 4)
        ours, theirs = (ref[k].astype(F32) for ref in (mine, other))
        pair = (jnp.where(first, ours, theirs), jnp.where(first, theirs, ours))
        rows = pl.ds(pl.multiple_of(48 * group, 16), 48)
        for t in range(9):
            block = jnp.concatenate([x[24 * t : 24 * t + 24] for x in pair], axis=0)
            out[rows, tiles(t)] = block.astype(BF16)
        extra = jnp.concatenate([x[216:224] for x in pair], axis=0)
        rows = pl.ds(pl.multiple_of(16 * group, 16), 16)
        for layer in range(2):
            parts = [extra[:, 3 * layer + k : 3 * layer + k + 1] for k in range(3)]
            bias[layer, rows] = jnp.broadcast_to(parts[0] + parts[1] + parts[2], (16, 128))
    kernel = out[:, 576:1152].astype(F32).reshape(8, 3, 8, 576)
    turned = [kernel[:, 2 - e].reshape(64, 576).T for e in range(3)]
    for column in range(9):
        block = [part[64 * (8 - column) : 64 * (8 - column) + 64].reshape(8, 1, 8, 64) for part in turned]
        block = jnp.concatenate(block, axis=1).reshape(192, 64)
        back[:, 64 * column : 64 * column + 64] = block.astype(BF16)


def forward_kernel(
    place, own, before, after, cotangent, weights, bias, act, wide, delta, feats, to_prev, to_next, post
):
    lane = lanes((64, 128))
    low = lane < 64

    for j in range(11):
        p, o, n = (ref[j].astype(F32) for ref in (before, own, after))
        turned = pltpu.roll(o, 64, 1)
        for half in range(2):
            if half == 0:
                minus = jnp.where(low, p, turned)
                plus = jnp.where(low, o, pltpu.roll(n, 64, 1))
            else:
                minus = jnp.where(low, pltpu.roll(p, 64, 1), o)
                plus = jnp.where(low, turned, n)
            zero = jnp.where(lane < 32, pltpu.roll(minus, 96, 1), pltpu.roll(plus, 32, 1))
            wide[0:64, tiles(2 * j + half)] = minus.astype(BF16)
            wide[64:128, tiles(2 * j + half)] = zero.astype(BF16)
            wide[128:192, tiles(2 * j + half)] = plus.astype(BF16)

    outside = jnp.logical_or(
        jnp.logical_and(lane < 32, place[0] == 0), jnp.logical_and(lane >= 96, place[0] == 31)
    )
    for m in range(10):
        product = conv_tiles(weights, 0, wide, 2 * m)
        for half in range(2):
            row = 2 * m + half
            value = leaky(add_y_taps(product[:, tiles(half)]) + bias[0])
            gone = outside
            if row < 2:
                gone = jnp.logical_or(outside, place[1] == 0)
            if row >= 18:
                gone = jnp.logical_or(outside, place[1] == 7)
            value = jnp.where(gone, 0.0, value)
            swapped = pltpu.roll(value, 64, 1).astype(BF16)
            if row < 12:
                left = slice(row * 128, row * 128 + 64)
                act[0:64, left] = value.astype(BF16)[:, 0:64]
                act[64:128, left] = pltpu.roll(value, 96, 1).astype(BF16)[:, 0:64]
                act[128:192, left] = swapped[:, 0:64]
            if row >= 8:
                right = slice((row - 8) * 128 + 64, (row - 8) * 128 + 128)
                act[0:64, right] = swapped[:, 64:128]
                act[64:128, right] = pltpu.roll(value, 32, 1).astype(BF16)[:, 64:128]
                act[128:192, right] = value.astype(BF16)[:, 64:128]

    front = lane % 64 < 32
    for m in range(5):
        product = conv_tiles(weights, 576, act, 2 * m)
        grads = []
        for half in range(2):
            row = 2 * m + half
            value = add_y_taps(product[:, tiles(half)]) + bias[1]
            cot = cotangent[row].astype(F32)
            grad = jnp.where(value > 0, cot, SLOPE * cot).astype(BF16)
            delta[row] = grad
            grads.append(grad.astype(F32))
            post[row] = leaky(value)
        to_prev[m] = jnp.where(front, grads[0], pltpu.roll(grads[1], 32, 1)).astype(BF16)
        to_next[m] = jnp.where(front, pltpu.roll(grads[0], 96, 1), grads[1]).astype(BF16)

    for block in range(8):
        turn = lax.rem(block // 2 + 4 - place[4], 4)
        same = jnp.where(place[2] == block % 2, 0, 1)
        piece = [post[z + 1, 8 * block : 8 * block + 8] for z in range(8)]
        feats[turn, same] = jnp.concatenate(piece, axis=0).astype(BF16)


def kernel_grad(stacked, wide, start):
    products = [
        lax.dot_general(
            stacked[...],
            wide[:, tiles(start + dz, 8)],
            CONTRACT_LAST,
            preferred_element_type=F32,
        )
        for dz in range(3)
    ]
    return jnp.concatenate(products, axis=1)


def second_grad_kernel(delta, act, wide, out, total, narrow, stacked):
    low = lanes((192, 128)) < 64
    for k in range(8):
        value = delta[k + 1].astype(F32)
        stacked[:, tiles(k)] = stack_y(value)
        total[...] = value if k == 0 else total[...] + value
    out[...] = kernel_grad(stacked, act, 1)
    for k in range(10):
        left = pltpu.roll(wide[:, tiles(k + 2)].astype(F32), 96, 1)
        right = pltpu.roll(wide[:, tiles(k + 10)].astype(F32), 32, 1)
        narrow[:, tiles(k)] = jnp.where(low, left, right).astype(BF16)


def backward_kernel(
    place, delta, from_prev, from_next, weights, act, narrow, grad_two, total_two, keep, send, stacked, own, both
):
    lane = lanes((64, 128))
    front = lane % 64 < 32
    for m in range(5):
        prev, after = (from_prev[m].astype(F32), from_next[m].astype(F32))
        for half in range(2):
            row = 2 * m + half
            value = delta[row].astype(F32)
            left = pltpu.roll(prev, 96, 1) if half else prev
            right = after if half else pltpu.roll(after, 32, 1)
            minus = jnp.where(front, left, pltpu.roll(value, 32, 1))
            plus = jnp.where(front, pltpu.roll(value, 96, 1), right)
            stacked[0:64, tiles(row)] = minus.astype(BF16)
            stacked[64:128, tiles(row)] = delta[row]
            stacked[128:192, tiles(row)] = plus.astype(BF16)

    total = jnp.zeros((64, 128), F32)
    for m in range(4):
        product = conv_tiles(weights, 0, stacked, 2 * m)
        for half in range(2):
            back = add_y_taps(product[:, tiles(half)])
            positive = act[64:128, tiles(2 * m + 2 + half)].astype(F32) > 0
            value = jnp.where(positive, back, SLOPE * back).astype(BF16).astype(F32)
            own[:, tiles(2 * m + half)] = stack_y(value)
            total = total + value

    both[:, 0:576] = grad_two[...]
    both[:, 576:1152] = kernel_grad(own, narrow, 0)
    offsets = jnp.where(
        lane == 0,
        jnp.sum(total_two[...], axis=1, keepdims=True),
        jnp.sum(total, axis=1, keepdims=True),
    )
    def block(index):
        rows = [both[24 * index + 8 * (u // 9) : 24 * index + 8 * (u // 9) + 8, tiles(u % 9)] for u in range(27)]
        return jnp.concatenate(rows + [offsets[8 * index : 8 * index + 8]], axis=0)

    first = place[2] == 0
    for group in range(4):
        even, odd = (block(2 * group), block(2 * group + 1))
        keep[group] = jnp.where(first, even, odd).astype(BF16)
        send[group] = jnp.where(first, odd, even).astype(BF16)


def finish_kernel(factor, whole, kernel_two, kernel_one, offsets):
    total = sum(whole[k].astype(F32) for k in range(16)) * factor
    units = [total[8 * u : 8 * u + 8] for u in range(28)]
    for dy in range(3):
        for column in range(9):
            value = units[dy * 9 + column]
            for half in range(2):
                layer, k = divmod(2 * column + half, 9)
                dz, dx = divmod(k, 3)
                target = kernel_one if layer else kernel_two
                target[dx * 9 + dy * 3 + dz] = value[:, 64 * half : 64 * half + 64]
    offsets[...] = units[27]


def features_kernel(place, *refs):
    pieces, other, out, turned = (refs[:4], refs[4], refs[5], refs[6])
    for k in range(4):
        group = lax.rem(place[4] + 4 - k, 4)
        group = jnp.where(place[3] == 1, 3 - group, group)
        for same in range(2):
            value = (pieces[k][0] if same == 0 else other[k]).astype(F32)
            core = place[2] if same == 0 else 1 - place[2]
            start = pl.multiple_of(128 * (2 * group + core), 128)
            turned[pl.ds(start, 64), :] = value
            turned[pl.ds(start + 64, 64), :] = pltpu.roll(value, 64, 1)
    for o in range(8):
        out[o] = turned[pl.ds(o, 128, stride=8), :].T[0:64].astype(BF16)


def call(kernel, out_shapes, scratch, *args, scalars=(), far=(), flops=0):
    vmem = pl.BlockSpec(memory_space=pltpu.VMEM)
    smem = pl.BlockSpec(memory_space=pltpu.SMEM)
    anywhere = pl.BlockSpec(memory_space=pl.ANY)
    outs = [jax.ShapeDtypeStruct(shape, dtype) for shape, dtype in out_shapes]
    size = sum(a.size * a.dtype.itemsize for a in args)
    size += sum(o.size * o.dtype.itemsize for o in outs)
    return pl.pallas_call(
        kernel,
        out_shape=outs,
        in_specs=[smem if k in scalars else anywhere if k in far else vmem for k in range(len(args))],
        out_specs=[vmem] * len(outs),
        scratch_shapes=[pltpu.VMEM(*x) if isinstance(x, tuple) else x for x in scratch],
        compiler_params=pltpu.CompilerParams(vmem_limit_bytes=VMEM_LIMIT),
        cost_estimate=pl.CostEstimate(flops=flops, bytes_accessed=size, transcendentals=0),
    )(*args)


def neighbours():
    pairs = []
    for here in range(31):
        there = here + 1
        turn = (here // 4) % 2 != (there // 4) % 2
        pairs += [(here * 4 + l, there * 4 + (3 - l if turn else l)) for l in range(4)]
    return pairs, [(b, a) for a, b in pairs]


def shards(volume, weight_one, bias_one, weight_two, bias_two, cotangent):
    factor = float(volume.shape[1] * 32 * volume.shape[2] * volume.shape[3]) ** (-0.5)
    h, l, c = (lax.axis_index(name) for name in ("h", "l", "c"))
    mirrored = h == 1
    block = 2 * jnp.where(mirrored, 3 - l, l) + c
    place = [lax.axis_index(SPACE), block, c, h, l]
    place = jnp.stack(place).astype(jnp.int32)
    up, down = neighbours()
    near = SPACE + ("l",)
    swap = [(0, 1), (1, 0)]

    def spread(pieces):
        turns = [[(i, (i + k) % 4) for i in range(4)] for k in range(4)]
        return [pieces[0]] + [lax.ppermute(pieces[k], "l", turns[k]) for k in range(1, 4)]

    (units,) = call(
        weight_prepare_kernel,
        [((224, 128), BF16)],
        [],
        jnp.transpose(weight_one, (2, 3, 4, 0, 1)).reshape(27, 8, 64),
        bias_one,
        jnp.transpose(weight_two, (2, 3, 4, 0, 1)).reshape(27, 8, 64),
        bias_two,
        scalars=(1, 3),
    )
    mine = jnp.stack(spread([units] * 4))
    other = lax.ppermute(mine, "c", swap)
    weights, weights_back, bias = call(
        weights_kernel,
        [((192, 1152), BF16), ((192, 576), BF16), ((2, 64, 128), F32)],
        [],
        place,
        mine,
        other,
        scalars=(0,),
    )

    (pieces,) = call(
        prepare_kernel,
        [((8, 168, 128), BF16)],
        [((2, 8, 64, 128), BF16), ((1072, 128), F32), pltpu.SemaphoreType.DMA((2,))],
        place,
        volume.reshape(8, 64, 128),
        cotangent.reshape(8, 64, 128),
        scalars=(0,),
        far=(1, 2),
    )
    received = lax.all_to_all(pieces, CHAN, 0, 0)
    field, cots = call(
        unpack_kernel, [((11, 64, 128), BF16), ((10, 64, 128), BF16)], [], received
    )
    before = lax.ppermute(field, near, up)
    after = lax.ppermute(field, near, down)

    act, wide, delta, feats, to_prev, to_next = call(
        forward_kernel,
        [
            ((192, 1536), BF16),
            ((192, 2816), BF16),
            ((10, 64, 128), BF16),
            ((4, 2, 64, 128), BF16),
            ((5, 64, 128), BF16),
            ((5, 64, 128), BF16),
        ],
        [((10, 64, 128), F32)],
        place,
        field,
        before,
        after,
        cots,
        weights,
        bias,
        scalars=(0,),
        flops=2 * 192 * 576 * 128 * 30,
    )
    from_next = lax.ppermute(to_prev, near, down)
    from_prev = lax.ppermute(to_next, near, up)
    grad_two, total_two, narrow = call(
        second_grad_kernel,
        [((192, 576), F32), ((64, 128), F32), ((192, 1280), BF16)],
        [((192, 1024), BF16)],
        delta,
        act,
        wide,
        flops=2 * 192 * 576 * 1024,
    )
    keep, send = call(
        backward_kernel,
        [((4, 224, 128), BF16), ((4, 224, 128), BF16)],
        [((192, 1280), BF16), ((192, 1024), BF16), ((192, 1152), F32)],
        place,
        delta,
        from_prev,
        from_next,
        weights_back,
        act,
        narrow,
        grad_two,
        total_two,
        scalars=(0,),
        flops=4 * 192 * 576 * 1024,
    )

    part = keep.astype(F32) + lax.ppermute(send, "c", swap).astype(F32)
    part = jnp.broadcast_to(part.astype(BF16)[None], (2, 4, 224, 128)).reshape(8, 224, 128)
    part = lax.all_to_all(part, ("h", "l"), 0, 0)
    part = jnp.sum(part.astype(F32), axis=0).astype(BF16)
    whole = lax.all_to_all(jnp.broadcast_to(part, (16, 224, 128)), PLANE, 0, 0)
    kernel_two, kernel_one, offsets = call(
        functools.partial(finish_kernel, factor),
        [((27, 8, 64), F32), ((27, 8, 64), F32), ((8, 128), F32)],
        [],
        whole,
    )
    kernel_one, kernel_two = (
        jnp.transpose(k.reshape(3, 3, 3, 8, 64), (3, 4, 0, 1, 2)) for k in (kernel_one, kernel_two)
    )

    feats = spread([feats[k] for k in range(4)])
    other = lax.ppermute(jnp.stack([piece[1] for piece in feats]), "c", swap)
    (features,) = call(
        features_kernel,
        [((8, 64, 128), BF16)],
        [((1024, 128), F32)],
        place,
        *feats,
        other,
        scalars=(0,),
    )
    return features.reshape(8, 2, 32, 128), kernel_one, offsets[:, 1], kernel_two, offsets[:, 0]


def solution(mesh):
    fine = Mesh(mesh.devices.reshape(4, 2, 4, 4, 2), ("x", "h", "y", "l", "c"))
    field = P(CHAN, SPACE, None, None)
    kernel = P(CHAN, None, None, None, None)
    in_specs = (field, kernel, P(CHAN), kernel, P(CHAN), field)
    out_specs = (field, kernel, P(CHAN), kernel, P(CHAN))
    return jax.shard_map(shards, mesh=fine, in_specs=in_specs, out_specs=out_specs, check_vma=False)
```

time: 928 us -> 120 us (0.13)
  waiting for transfers between devices: 564 us -> 34.6 us
  matrix products: 150 us -> 0 us
  local copies, waits for them, and re-layouts: 126 us -> 3.74 us
  other arithmetic: 23.9 us -> 0.17 us
  starting transfers between devices: 20.9 us -> 43.2 us
  Pallas kernels: 0 us -> 14.3 us
  between operations: 14.4 us -> 0.86 us
    psum x1 -> x0, waiting for transfers between devices: 425 us -> none  [shards(): summed = lax.psum((kernel_one, offset_one, kernel_two, offset_two), 'space')]
    all_gather x3 -> x0, waiting for transfers between devices: 114 us -> none  [the longest x2 114 us: surround(): gathered = lax.all_gather(field, 'chan', axis=0, tiled=True)]
    transpose x2 -> x0, matrix products: 101 us -> none  [kernel_grad_inner(): return jnp.transpose(result, (1, 0, 2, 3, 4))]
    broadcast_in_dim x8 -> x2, local copies, waits for them, and re-layouts: 51.1 us -> 1.12 us  [the longest x1 1.06 us: shards(): whole = lax.all_to_all(jnp.broadcast_to(part, (16, 224, 128)), PLANE, 0, 0)]
    conv_general_dilated x3 -> x0, matrix products: 49.4 us -> none  [the longest x2 38.8 us: conv_inner(): lax.conv_general_dilated(inputs[None], kernel, (1, 1, 1), ((0, 0), (side,...]
    all_to_all x0 -> x2, starting transfers between devices: none -> 24.1 us  [the longest x1 18.1 us: shards(): whole = lax.all_to_all(jnp.broadcast_to(part, (16, 224, 128)), PLANE, 0, 0)]
    conv_general_dilated x9 -> x0, local copies, waits for them, and re-layouts: 23.7 us -> none  [the longest x6 18.9 us: conv_inner(): lax.conv_general_dilated(inputs[None], kernel, (1, 1, 1), ((0, 0), (side,...]
    all_to_all x0 -> x1, blocking collectives: none -> 23 us  [shards(): part = lax.all_to_all(part, ('h', 'l'), 0, 0)]
  transfers between devices with their start and end apart: 10 -> 15, of which waited for: 9 -> 11; matrix products, arithmetic and copies ran while one was open for 16% -> 0% of each run, Pallas kernels for 0% -> 3%
where the time goes in v2:
time: 120 us
  starting transfers between devices  43.2 us (36%)
  waiting for transfers between devices  34.6 us (29%)
  blocking collectives  23 us (19%)
  Pallas kernels  14.3 us (12%)
  local copies, waits for them, and re-layouts  3.74 us (3%)
    all_to_all x1, blocking collectives, shards(): part = lax.all_to_all(part, ('h', 'l'), 0, 0)  23 us
    all_to_all x1, starting transfers between devices, shards(): whole = lax.all_to_all(jnp.broadcast_to(part, (16, 224, 128)), PLANE, 0, 0)  18.1 us
    ppermute x6, waiting for transfers between devices, spread(): lax.ppermute(pieces[k], 'l', turns[k])  16.4 us
    pallas_call x9, Pallas kernels, call(): pl.pallas_call(kernel, out_shape=outs, in_specs=[smem if k in scalars els...  14.3 us
    ppermute x1, waiting for transfers between devices, shards(): from_next = lax.ppermute(to_prev, near, down)  8.87 us
    ppermute x6, starting transfers between devices, spread(): lax.ppermute(pieces[k], 'l', turns[k])  7.16 us
    all_to_all x1, starting transfers between devices, shards(): received = lax.all_to_all(pieces, CHAN, 0, 0)  5.91 us
    ppermute x1, starting transfers between devices, shards(): before = lax.ppermute(field, near, up)  3.48 us
  transfers between devices with their start and end apart: 15, of which 11 were waited for; matrix products, arithmetic and copies ran while one was open for 0% of the time, Pallas kernels for 3%

profile of v2, /device:TPU:8, one launch (start us, length us, event | category | flops | bytes accessed | tf_op | source)
XLA Modules:
  0.0 119.8 jit_solution(4024910155283239410)
XLA Ops:
  0.7 0.1 stack.41.place
  0.8 0.9 copy-done
  1.7 0.9 copy-done.1
  2.6 1.9 %shard_map.101 = bf16[8,168,128]{2,1,0:T(8,128)(2,1)} custom-call(s32[5]{0:T(128)S(1)} %stack.41.place, bf16[8,64,128]{2,1,0:T(8,128)(2,1)S(1)} %bitcast.36, bf16[8,64,128]{2,1,0:T(8,128)(2,1)S(1)} %bitcast.37), custom_call_target="tpu_custom_call" | custom-call | bytes 606228 | tf_op jit(solution)/shard_map/pallas_call | solution.py:323
  4.5 5.9 %all-to-all-start = ((bf16[8,168,128]{2,1,0:T(8,128)(2,1)}), bf16[8,168,128]{2,1,0:T(8,128)(2,1)S(1)}, u32[]{:S(2)}, u32[]{:S(2)}) async-start(bf16[8,168,128]{2,1,0:T(8,128)(2,1)} %shard_map.101), calls=%async_computation | async-start | bytes 688128 | tf_op jit(solution)/shard_map/all_to_all | solution.py:390
  10.4 0.6 shard_map.103
  11.0 3.9 %collective-permute-start.4 = (bf16[224,128]{1,0:T(8,128)(2,1)S(1)}, bf16[224,128]{1,0:T(8,128)(2,1)S(1)}, u32[]{:S(2)}, u32[]{:S(2)}) collective-permute-start(bf16[224,128]{1,0:T(8,128)(2,1)S(1)} %shard_map.103), channel_id=1, source_target_pairs={{0,6},{2,0},{4,2},{6,4},{1,7},{3,1},{5,3},{7,5},{8,14},{10,8},{12,... | collective-permute-start | bytes 172040 | tf_op jit(solution)/shard_map/ppermute | solution.py:356
  14.9 0.0 collective-permute-start.3
  14.9 1.1 collective-permute-start.2
  16.1 2.4 %collective-permute-done.4 = bf16[224,128]{1,0:T(8,128)(2,1)S(1)} collective-permute-done((bf16[224,128]{1,0:T(8,128)(2,1)S(1)}, bf16[224,128]{1,0:T(8,128)(2,1)S(1)}, u32[]{:S(2)}, u32[]{:S(2)}) %collective-permute-start.4) | collective-permute-done | bytes 57376 | tf_op jit(solution)/shard_map/ppermute | solution.py:356
  18.4 8.4 %collective-permute-done.3 = bf16[224,128]{1,0:T(8,128)(2,1)S(1)} collective-permute-done((bf16[224,128]{1,0:T(8,128)(2,1)S(1)}, bf16[224,128]{1,0:T(8,128)(2,1)S(1)}, u32[]{:S(2)}, u32[]{:S(2)}) %collective-permute-start.3) | collective-permute-done | bytes 57376 | tf_op jit(solution)/shard_map/ppermute | solution.py:356
  26.8 0.0 collective-permute-done.2
  26.8 0.1 collective-permute-start.5
  26.9 0.0 all-to-all-done.received
  26.9 0.1 shard_map.102
  27.0 2.4 %collective-permute-start.1 = (bf16[11,64,128]{2,1,0:T(8,128)(2,1)S(1)}, bf16[11,64,128]{2,1,0:T(8,128)(2,1)S(1)}, u32[]{:S(2)}, u32[]{:S(2)}) collective-permute-start(bf16[11,64,128]{2,1,0:T(8,128)(2,1)S(1)} %get-tuple-element.24.own), channel_id=1, source_target_pairs={{8,0},{10,2},{12,4},{14,6},{16,8},{18,10},{20,12},{22,14},{24,16},... | collective-permute-start | bytes 540680 | tf_op jit(solution)/shard_map/ppermute | solution.py:395
  29.4 3.5 %collective-permute-start = (bf16[11,64,128]{2,1,0:T(8,128)(2,1)S(1)}, bf16[11,64,128]{2,1,0:T(8,128)(2,1)S(1)}, u32[]{:S(2)}, u32[]{:S(2)}) collective-permute-start(bf16[11,64,128]{2,1,0:T(8,128)(2,1)S(1)} %get-tuple-element.24.own), channel_id=1, source_target_pairs={{0,8},{2,10},{4,12},{6,14},{8,16},{10,18},{12,20},{14,22},{16,24},... | collective-permute-start | bytes 540680 | tf_op jit(solution)/shard_map/ppermute | solution.py:394
  32.9 0.0 collective-permute-done.5.other
  32.9 1.1 shard_map.104
  33.9 1.9 %collective-permute-done.1.after = bf16[11,64,128]{2,1,0:T(8,128)(2,1)S(1)} collective-permute-done((bf16[11,64,128]{2,1,0:T(8,128)(2,1)S(1)}, bf16[11,64,128]{2,1,0:T(8,128)(2,1)S(1)}, u32[]{:S(2)}, u32[]{:S(2)}) %collective-permute-start.1) | collective-permute-done | bytes 180256 | tf_op jit(solution)/shard_map/ppermute | solution.py:395
  35.8 2.1 %collective-permute-done.before = bf16[11,64,128]{2,1,0:T(8,128)(2,1)S(1)} collective-permute-done((bf16[11,64,128]{2,1,0:T(8,128)(2,1)S(1)}, bf16[11,64,128]{2,1,0:T(8,128)(2,1)S(1)}, u32[]{:S(2)}, u32[]{:S(2)}) %collective-permute-start) | collective-permute-done | bytes 180256 | tf_op jit(solution)/shard_map/ppermute | solution.py:394
  37.9 5.9 %shard_map.105 = (bf16[192,1536]{1,0:T(8,128)(2,1)S(1)}, bf16[192,2816]{1,0:T(8,128)(2,1)S(1)}, bf16[10,64,128]{2,1,0:T(8,128)(2,1)S(1)}, bf16[4,2,64,128]{3,2,1...) custom-call(s32[5]{0:T(128)S(1)} %stack.41.place, ...), custom_call_target="tpu_custom_call" | custom-call | flops 849346560 | bytes 3342356 | tf_op jit(solution)/shard_map/pallas_call | solution.py:323
  43.8 3.5 %collective-permute-start.10 = (bf16[5,64,128]{2,1,0:T(8,128)(2,1)S(1)}, bf16[5,64,128]{2,1,0:T(8,128)(2,1)S(1)}, u32[]{:S(2)}, u32[]{:S(2)}) collective-permute-start(bf16[5,64,128]{2,1,0:T(8,128)(2,1)S(1)} %get-tuple-element.30), channel_id=1, source_target_pairs={{0,8},{2,10},{4,12},{6,14},{8,16},{10,18},{12,20},{14,22},{16,24},... | collective-permute-start | bytes 245768 | tf_op jit(solution)/shard_map/ppermute | solution.py:419
  47.3 2.4 %collective-permute-start.11 = (bf16[5,64,128]{2,1,0:T(8,128)(2,1)S(1)}, bf16[5,64,128]{2,1,0:T(8,128)(2,1)S(1)}, u32[]{:S(2)}, u32[]{:S(2)}) collective-permute-start(bf16[5,64,128]{2,1,0:T(8,128)(2,1)S(1)} %get-tuple-element.31), channel_id=1, source_target_pairs={{8,0},{10,2},{12,4},{14,6},{16,8},{18,10},{20,12},{22,14},{24,16},... | collective-permute-start | bytes 245768 | tf_op jit(solution)/shard_map/ppermute | solution.py:418
  49.7 0.6 shard_map.107
  50.3 0.0 collective-permute-done.10.from_prev
  50.3 8.9 %collective-permute-done.11.from_next = bf16[5,64,128]{2,1,0:T(8,128)(2,1)S(1)} collective-permute-done((bf16[5,64,128]{2,1,0:T(8,128)(2,1)S(1)}, bf16[5,64,128]{2,1,0:T(8,128)(2,1)S(1)}, u32[]{:S(2)}, u32[]{:S(2)}) %collective-permute-start.11) | collective-permute-done | bytes 81952 | tf_op jit(solution)/shard_map/ppermute | solution.py:418
  59.2 1.9 %shard_map.108 = (bf16[4,224,128]{2,1,0:T(8,128)(2,1)S(1)}, bf16[4,224,128]{2,1,0:T(8,128)(2,1)S(1)}) custom-call(s32[5]{0:T(128)S(1)} %stack.41.place, bf16[10,64,128]{2,1,0:T(8,128)(2,1)S(1)} %get-tuple-element.29.delta, bf16[5,64,128]{2,1,0:T(8,128)(2,1)S(1)} %collective-permute-done.10.from_prev, ...), custom_call_target="tpu_custom_call" | custom-call | flops 452984832 | bytes 2564116 | tf_op jit(solution)/shard_map/pallas_call | solution.py:323
  61.1 0.1 collective-permute-start.12
  61.2 1.5 %collective-permute-done.12 = bf16[4,224,128]{2,1,0:T(8,128)(2,1)S(1)} collective-permute-done((bf16[4,224,128]{2,1,0:T(8,128)(2,1)S(1)}, bf16[4,224,128]{2,1,0:T(8,128)(2,1)S(1)}, u32[]{:S(2)}, u32[]{:S(2)}) %collective-permute-start.12) | collective-permute-done | bytes 229408 | tf_op jit(solution)/shard_map/ppermute | solution.py:446
  62.6 0.1 add_convert_fusion
  62.7 0.1 broadcast_in_dim.4
  62.8 23.0 %all_to_all.15 = bf16[8,224,128]{2,1,0:T(8,128)(2,1)S(1)} all-to-all(bf16[8,224,128]{2,1,0:T(8,128)(2,1)S(1)} %bitcast.40), channel_id=1, replica_groups=mesh['x'=4,'h'=2,'y'=4,'l'=4,'c'=2] {'h','l'}, dimensions={0} | all-to-all | bytes 917504 | tf_op jit(solution)/shard_map/all_to_all | solution.py:448
  85.8 0.1 reduce_sum.12
  85.9 1.1 broadcast_in_dim.10
  86.9 18.1 %all-to-all-start.2 = ((bf16[16,224,128]{2,1,0:T(8,128)(2,1)}), bf16[16,224,128]{2,1,0:T(8,128)(2,1)S(1)}, u32[]{:S(2)}, u32[]{:S(2)}) async-start(bf16[16,224,128]{2,1,0:T(8,128)(2,1)} %broadcast_in_dim.10), calls=%async_computation.2 | async-start | bytes 1835008 | tf_op jit(solution)/shard_map/all_to_all | solution.py:450
  105.1 0.4 collective-permute-start.8
  105.5 1.7 %collective-permute-start.7 = (bf16[2,64,128]{2,1,0:T(8,128)(2,1)S(1)}, bf16[2,64,128]{2,1,0:T(8,128)(2,1)S(1)}, u32[]{:S(2)}, u32[]{:S(2)}) collective-permute-start(bf16[2,64,128]{2,1,0:T(8,128)(2,1)S(1)} %get-tuple-element.46), channel_id=1, source_target_pairs={{0,4},{2,6},{4,0},{6,2},{1,5},{3,7},{5,1},{7,3},{8,12},{10,14},{12... | collective-permute-start | bytes 98312 | tf_op jit(solution)/shard_map/ppermute | solution.py:356
  107.2 0.0 collective-permute-start.6
  107.2 2.1 %collective-permute-done.8.refs_3_ = bf16[2,64,128]{2,1,0:T(8,128)(2,1)S(1)} collective-permute-done((bf16[2,64,128]{2,1,0:T(8,128)(2,1)S(1)}, bf16[2,64,128]{2,1,0:T(8,128)(2,1)S(1)}, u32[]{:S(2)}, u32[]{:S(2)}) %collective-permute-start.8) | collective-permute-done | bytes 32800 | tf_op jit(solution)/shard_map/ppermute | solution.py:356
  109.3 1.0 collective-permute-done.7.refs_2_
  110.3 2.6 %collective-permute-done.6.refs_1_ = bf16[2,64,128]{2,1,0:T(8,128)(2,1)S(1)} collective-permute-done((bf16[2,64,128]{2,1,0:T(8,128)(2,1)S(1)}, bf16[2,64,128]{2,1,0:T(8,128)(2,1)S(1)}, u32[]{:S(2)}, u32[]{:S(2)}) %collective-permute-start.6) | collective-permute-done | bytes 32800 | tf_op jit(solution)/shard_map/ppermute | solution.py:356
  112.9 0.1 collective-permute-start.9
  113.0 1.2 %collective-permute-done.9.refs_4_ = bf16[4,64,128]{2,1,0:T(8,128)(2,1)S(1)} collective-permute-done((bf16[4,64,128]{2,1,0:T(8,128)(2,1)S(1)}, bf16[4,64,128]{2,1,0:T(8,128)(2,1)S(1)}, u32[]{:S(2)}, u32[]{:S(2)}) %collective-permute-start.9) | collective-permute-done | bytes 65568 | tf_op jit(solution)/shard_map/ppermute | solution.py:462
  114.3 1.4 %shard_map.106 = bf16[8,64,128]{2,1,0:T(8,128)(2,1)} custom-call(s32[5]{0:T(128)S(1)} %stack.41.place, bf16[2,64,128]{2,1,0:T(8,128)(2,1)S(1)} %get-tuple-element.48.refs_0_, bf16[2,64,128]{2,1,0:T(8,128)(2,1)S(1)} %collective-permute-done.6.refs_1_, bf16[2,64,128]{2,1,0:T(8,128)(2,1)S(1)} %collective-permute-done.7.refs_2_, ...), custom_call_target="tpu_custom_call" | custom-call | bytes 327700 | tf_op jit(solution)/shard_map/pallas_call | solution.py:323
  115.7 2.6 %all-to-all-done.2.whole = bf16[16,224,128]{2,1,0:T(8,128)(2,1)S(1)} async-done(((bf16[16,224,128]{2,1,0:T(8,128)(2,1)}), bf16[16,224,128]{2,1,0:T(8,128)(2,1)S(1)}, u32[]{:S(2)}, u32[]{:S(2)}) %all-to-all-start.2) | async-done | bytes 917536 | tf_op jit(solution)/shard_map/all_to_all | solution.py:450
  118.3 0.9 shard_map.109
  119.1 0.7 slice_reduce_fusion
  (17 shorter events, 0.1 us)
Async XLA Ops:
  0.6 9.7 %copy-start.5 = (f32[8]{0:T(128)S(1)}, f32[8]{0:T(128)}, u32[]{:S(2)}) copy-start(f32[8]{0:T(128)} %bias_two.1) | copy-start | bytes 100
  0.6 9.7 %copy-start.4 = (f32[8]{0:T(128)S(1)}, f32[8]{0:T(128)}, u32[]{:S(2)}) copy-start(f32[8]{0:T(128)} %bias_one.1) | copy-start | bytes 100
  0.7 9.7 %copy-start.2 = (bf16[8,64,3,3,3]{1,0,4,3,2:T(8,128)(2,1)S(1)}, bf16[8,64,3,3,3]{1,0,4,3,2:T(8,128)(2,1)}, u32[]{:S(2)}) copy-start(bf16[8,64,3,3,3]{1,0,4,3,2:T(8,128)(2,1)} %param.7) | copy-start | bytes 82948
  0.8 0.9 copy-start
  1.7 0.9 copy-start.1
  2.6 7.8 %copy-start.3 = (bf16[8,64,3,3,3]{1,0,4,3,2:T(8,128)(2,1)S(1)}, bf16[8,64,3,3,3]{1,0,4,3,2:T(8,128)(2,1)}, u32[]{:S(2)}) copy-start(bf16[8,64,3,3,3]{1,0,4,3,2:T(8,128)(2,1)} %param.9) | copy-start | bytes 82948
  4.5 22.5 %all-to-all-start = ((bf16[8,168,128]{2,1,0:T(8,128)(2,1)}), bf16[8,168,128]{2,1,0:T(8,128)(2,1)S(1)}, u32[]{:S(2)}, u32[]{:S(2)}) async-start(bf16[8,168,128]{2,1,0:T(8,128)(2,1)} %shard_map.101), calls=%async_computation | async-start | bytes 688128 | tf_op jit(solution)/shard_map/all_to_all | solution.py:390
  11.0 7.4 %collective-permute-start.4 = (bf16[224,128]{1,0:T(8,128)(2,1)S(1)}, bf16[224,128]{1,0:T(8,128)(2,1)S(1)}, u32[]{:S(2)}, u32[]{:S(2)}) collective-permute-start(bf16[224,128]{1,0:T(8,128)(2,1)S(1)} %shard_map.103), channel_id=1, source_target_pairs={{0,6},{2,0},{4,2},{6,4},{1,7},{3,1},{5,3},{7,5},{8,14},{10,8},{12,... | collective-permute-start | bytes 172040 | tf_op jit(solution)/shard_map/ppermute | solution.py:356
  14.9 11.9 %collective-permute-start.3 = (bf16[224,128]{1,0:T(8,128)(2,1)S(1)}, bf16[224,128]{1,0:T(8,128)(2,1)S(1)}, u32[]{:S(2)}, u32[]{:S(2)}) collective-permute-start(bf16[224,128]{1,0:T(8,128)(2,1)S(1)} %shard_map.103), channel_id=1, source_target_pairs={{0,4},{2,6},{4,0},{6,2},{1,5},{3,7},{5,1},{7,3},{8,12},{10,14},{12... | collective-permute-start | bytes 172040 | tf_op jit(solution)/shard_map/ppermute | solution.py:356
  14.9 11.9 %collective-permute-start.2 = (bf16[224,128]{1,0:T(8,128)(2,1)S(1)}, bf16[224,128]{1,0:T(8,128)(2,1)S(1)}, u32[]{:S(2)}, u32[]{:S(2)}) collective-permute-start(bf16[224,128]{1,0:T(8,128)(2,1)S(1)} %shard_map.103), channel_id=1, source_target_pairs={{0,2},{2,4},{4,6},{6,0},{1,3},{3,5},{5,7},{7,1},{8,10},{10,12},{12... | collective-permute-start | bytes 172040 | tf_op jit(solution)/shard_map/ppermute | solution.py:356
  26.8 6.0 %collective-permute-start.5 = (bf16[4,224,128]{2,1,0:T(8,128)(2,1)S(1)}, bf16[4,224,128]{2,1,0:T(8,128)(2,1)S(1)}, u32[]{:S(2)}, u32[]{:S(2)}) collective-permute-start(bf16[4,224,128]{2,1,0:T(8,128)(2,1)S(1)} %pad_maximum_fusion.mine), channel_id=1, source_target_pairs={{0,1},{1,0},{2,3},{3,2},{4,5},{5,4},{6,7},{7,6},{8,9},{9,8},{10,11... | collective-permute-start | bytes 688136 | tf_op jit(solution)/shard_map/ppermute | solution.py:369
  27.0 8.8 %collective-permute-start.1 = (bf16[11,64,128]{2,1,0:T(8,128)(2,1)S(1)}, bf16[11,64,128]{2,1,0:T(8,128)(2,1)S(1)}, u32[]{:S(2)}, u32[]{:S(2)}) collective-permute-start(bf16[11,64,128]{2,1,0:T(8,128)(2,1)S(1)} %get-tuple-element.24.own), channel_id=1, source_target_pairs={{8,0},{10,2},{12,4},{14,6},{16,8},{18,10},{20,12},{22,14},{24,16},... | collective-permute-start | bytes 540680 | tf_op jit(solution)/shard_map/ppermute | solution.py:395
  29.4 8.6 %collective-permute-start = (bf16[11,64,128]{2,1,0:T(8,128)(2,1)S(1)}, bf16[11,64,128]{2,1,0:T(8,128)(2,1)S(1)}, u32[]{:S(2)}, u32[]{:S(2)}) collective-permute-start(bf16[11,64,128]{2,1,0:T(8,128)(2,1)S(1)} %get-tuple-element.24.own), channel_id=1, source_target_pairs={{0,8},{2,10},{4,12},{6,14},{8,16},{10,18},{12,20},{14,22},{16,24},... | collective-permute-start | bytes 540680 | tf_op jit(solution)/shard_map/ppermute | solution.py:394
  43.8 6.5 %collective-permute-start.10 = (bf16[5,64,128]{2,1,0:T(8,128)(2,1)S(1)}, bf16[5,64,128]{2,1,0:T(8,128)(2,1)S(1)}, u32[]{:S(2)}, u32[]{:S(2)}) collective-permute-start(bf16[5,64,128]{2,1,0:T(8,128)(2,1)S(1)} %get-tuple-element.30), channel_id=1, source_target_pairs={{0,8},{2,10},{4,12},{6,14},{8,16},{10,18},{12,20},{14,22},{16,24},... | collective-permute-start | bytes 245768 | tf_op jit(solution)/shard_map/ppermute | solution.py:419
  47.3 11.9 %collective-permute-start.11 = (bf16[5,64,128]{2,1,0:T(8,128)(2,1)S(1)}, bf16[5,64,128]{2,1,0:T(8,128)(2,1)S(1)}, u32[]{:S(2)}, u32[]{:S(2)}) collective-permute-start(bf16[5,64,128]{2,1,0:T(8,128)(2,1)S(1)} %get-tuple-element.31), channel_id=1, source_target_pairs={{8,0},{10,2},{12,4},{14,6},{16,8},{18,10},{20,12},{22,14},{24,16},... | collective-permute-start | bytes 245768 | tf_op jit(solution)/shard_map/ppermute | solution.py:418
  61.1 1.6 %collective-permute-start.12 = (bf16[4,224,128]{2,1,0:T(8,128)(2,1)S(1)}, bf16[4,224,128]{2,1,0:T(8,128)(2,1)S(1)}, u32[]{:S(2)}, u32[]{:S(2)}) collective-permute-start(bf16[4,224,128]{2,1,0:T(8,128)(2,1)S(1)} %get-tuple-element.39), channel_id=1, source_target_pairs={{0,1},{1,0},{2,3},{3,2},{4,5},{5,4},{6,7},{7,6},{8,9},{9,8},{10,11... | collective-permute-start | bytes 688136 | tf_op jit(solution)/shard_map/ppermute | solution.py:446
  86.9 31.4 %all-to-all-start.2 = ((bf16[16,224,128]{2,1,0:T(8,128)(2,1)}), bf16[16,224,128]{2,1,0:T(8,128)(2,1)S(1)}, u32[]{:S(2)}, u32[]{:S(2)}) async-start(bf16[16,224,128]{2,1,0:T(8,128)(2,1)} %broadcast_in_dim.10), calls=%async_computation.2 | async-start | bytes 1835008 | tf_op jit(solution)/shard_map/all_to_all | solution.py:450
  105.1 4.2 %collective-permute-start.8 = (bf16[2,64,128]{2,1,0:T(8,128)(2,1)S(1)}, bf16[2,64,128]{2,1,0:T(8,128)(2,1)S(1)}, u32[]{:S(2)}, u32[]{:S(2)}) collective-permute-start(bf16[2,64,128]{2,1,0:T(8,128)(2,1)S(1)} %get-tuple-element.45), channel_id=1, source_target_pairs={{0,6},{2,0},{4,2},{6,4},{1,7},{3,1},{5,3},{7,5},{8,14},{10,8},{12,... | collective-permute-start | bytes 98312 | tf_op jit(solution)/shard_map/ppermute | solution.py:356
  105.5 4.8 %collective-permute-start.7 = (bf16[2,64,128]{2,1,0:T(8,128)(2,1)S(1)}, bf16[2,64,128]{2,1,0:T(8,128)(2,1)S(1)}, u32[]{:S(2)}, u32[]{:S(2)}) collective-permute-start(bf16[2,64,128]{2,1,0:T(8,128)(2,1)S(1)} %get-tuple-element.46), channel_id=1, source_target_pairs={{0,4},{2,6},{4,0},{6,2},{1,5},{3,7},{5,1},{7,3},{8,12},{10,14},{12... | collective-permute-start | bytes 98312 | tf_op jit(solution)/shard_map/ppermute | solution.py:356
  107.2 5.7 %collective-permute-start.6 = (bf16[2,64,128]{2,1,0:T(8,128)(2,1)S(1)}, bf16[2,64,128]{2,1,0:T(8,128)(2,1)S(1)}, u32[]{:S(2)}, u32[]{:S(2)}) collective-permute-start(bf16[2,64,128]{2,1,0:T(8,128)(2,1)S(1)} %get-tuple-element.47), channel_id=1, source_target_pairs={{0,2},{2,4},{4,6},{6,0},{1,3},{3,5},{5,7},{7,1},{8,10},{10,12},{12... | collective-permute-start | bytes 98312 | tf_op jit(solution)/shard_map/ppermute | solution.py:356
  112.9 1.3 %collective-permute-start.9 = (bf16[4,64,128]{2,1,0:T(8,128)(2,1)S(1)}, bf16[4,64,128]{2,1,0:T(8,128)(2,1)S(1)}, u32[]{:S(2)}, u32[]{:S(2)}) collective-permute-start(bf16[4,64,128]{2,1,0:T(8,128)(2,1)S(1)} %pad_maximum_fusion.1), channel_id=1, source_target_pairs={{0,1},{1,0},{2,3},{3,2},{4,5},{5,4},{6,7},{7,6},{8,9},{9,8},{10,11... | collective-permute-start | bytes 196616 | tf_op jit(solution)/shard_map/ppermute | solution.py:462

commit v3 on v2

--- a/solution.py
+++ b/solution.py
@@ -60,10 +60,18 @@
     )
 
 
-def weight_prepare_kernel(weight_one, bias_one, weight_two, bias_two, units):
+def weight_prepare_kernel(weight_one, bias_one, weight_two, bias_two, units, held, arrived):
+    copies = [
+        pltpu.make_async_copy(ref, held.at[k], arrived.at[k])
+        for k, ref in enumerate((weight_one, weight_two))
+    ]
+    for copy in copies:
+        copy.start()
     row = lax.broadcasted_iota(jnp.int32, (8, 128), 0)
     lane = lanes((8, 128))
 
+    for copy in copies:
+        copy.wait()
     rows = []
     for t in range(9):
         for dy in range(3):
@@ -71,7 +79,7 @@
             for half in range(2):
                 layer, k = divmod(2 * t + half, 9)
                 dz, dx = divmod(k, 3)
-                halves.append((weight_two if layer else weight_one)[dx * 9 + dy * 3 + dz].astype(F32))
+                halves.append(held[layer, dx * 9 + dy * 3 + dz].astype(F32))
             rows.append(jnp.concatenate(halves, axis=1))
     packed = jnp.zeros((8, 128), F32)
     for layer, bias in enumerate((bias_one, bias_two)):
@@ -144,13 +152,15 @@
 
 
 def forward_kernel(
-    place, own, before, after, cotangent, weights, bias, act, wide, delta, feats, to_prev, to_next, post
+    place, own, even, odd, cotangent, weights, bias, act, wide, delta, feats, to_even, to_odd, post
 ):
+    upper = lax.rem(place[0], 2) == 1
     lane = lanes((64, 128))
     low = lane < 64
 
     for j in range(11):
-        p, o, n = (ref[j].astype(F32) for ref in (before, own, after))
+        o, x, y = (ref[j].astype(F32) for ref in (own, even, odd))
+        p, n = (jnp.where(upper, x, y), jnp.where(upper, y, x))
         turned = pltpu.roll(o, 64, 1)
         for half in range(2):
             if half == 0:
@@ -202,8 +212,10 @@
             delta[row] = grad
             grads.append(grad.astype(F32))
             post[row] = leaky(value)
-        to_prev[m] = jnp.where(front, grads[0], pltpu.roll(grads[1], 32, 1)).astype(BF16)
-        to_next[m] = jnp.where(front, pltpu.roll(grads[0], 96, 1), grads[1]).astype(BF16)
+        to_prev = jnp.where(front, grads[0], pltpu.roll(grads[1], 32, 1))
+        to_next = jnp.where(front, pltpu.roll(grads[0], 96, 1), grads[1])
+        to_even[m] = jnp.where(upper, to_prev, to_next).astype(BF16)
+        to_odd[m] = jnp.where(upper, to_next, to_prev).astype(BF16)
 
     for block in range(8):
         turn = lax.rem(block // 2 + 4 - place[4], 4)
@@ -239,12 +251,14 @@
 
 
 def backward_kernel(
-    place, delta, from_prev, from_next, weights, act, narrow, grad_two, total_two, keep, send, stacked, own, both
+    place, delta, from_even, from_odd, weights, act, narrow, grad_two, total_two, keep, send, stacked, own, both
 ):
     lane = lanes((64, 128))
+    upper = lax.rem(place[0], 2) == 1
     front = lane % 64 < 32
     for m in range(5):
-        prev, after = (from_prev[m].astype(F32), from_next[m].astype(F32))
+        x, y = (from_even[m].astype(F32), from_odd[m].astype(F32))
+        prev, after = (jnp.where(upper, x, y), jnp.where(upper, y, x))
         for half in range(2):
             row = 2 * m + half
             value = delta[row].astype(F32)
@@ -280,12 +294,18 @@
     first = place[2] == 0
     for group in range(4):
         even, odd = (block(2 * group), block(2 * group + 1))
-        keep[group] = jnp.where(first, even, odd).astype(BF16)
-        send[group] = jnp.where(first, odd, even).astype(BF16)
-
-
-def finish_kernel(factor, whole, kernel_two, kernel_one, offsets):
-    total = sum(whole[k].astype(F32) for k in range(16)) * factor
+        turn = lax.rem(group + 4 - place[4], 4)
+        keep[turn] = jnp.where(first, even, odd).astype(BF16)
+        send[turn] = jnp.where(first, odd, even).astype(BF16)
+
+
+def sum_of_four(parts):
+    parts = [part.astype(F32) for part in parts]
+    return (parts[0] + parts[2]) + (parts[1] + parts[3])
+
+
+def finish_kernel(factor, first, second, third, fourth, kernel_two, kernel_one, offsets):
+    total = sum_of_four([first[...], second[...], third[...], fourth[...]]) * factor
     units = [total[8 * u : 8 * u + 8] for u in range(28)]
     for dy in range(3):
         for column in range(9):
@@ -332,12 +352,17 @@
 
 
 def neighbours():
-    pairs = []
-    for here in range(31):
-        there = here + 1
-        turn = (here // 4) % 2 != (there // 4) % 2
-        pairs += [(here * 4 + l, there * 4 + (3 - l if turn else l)) for l in range(4)]
-    return pairs, [(b, a) for a, b in pairs]
+    both = []
+    for start in range(2):
+        pairs = []
+        for here in range(start, 31, 2):
+            there = here + 1
+            turn = (here // 4) % 2 != (there // 4) % 2
+            for l in range(4):
+                pair = (here * 4 + l, there * 4 + (3 - l if turn else l))
+                pairs += [pair, pair[::-1]]
+        both.append(pairs)
+    return both
 
 
 def shards(volume, weight_one, bias_one, weight_two, bias_two, cotangent):
@@ -347,25 +372,45 @@
     block = 2 * jnp.where(mirrored, 3 - l, l) + c
     place = [lax.axis_index(SPACE), block, c, h, l]
     place = jnp.stack(place).astype(jnp.int32)
-    up, down = neighbours()
+    even, odd = neighbours()
     near = SPACE + ("l",)
     swap = [(0, 1), (1, 0)]
 
-    def spread(pieces):
+    def spread(pieces, axis="l"):
         turns = [[(i, (i + k) % 4) for i in range(4)] for k in range(4)]
-        return [pieces[0]] + [lax.ppermute(pieces[k], "l", turns[k]) for k in range(1, 4)]
+        return [pieces[0]] + [lax.ppermute(pieces[k], axis, turns[k]) for k in range(1, 4)]
 
     (units,) = call(
         weight_prepare_kernel,
         [((224, 128), BF16)],
-        [],
+        [((2, 27, 8, 64), BF16), pltpu.SemaphoreType.DMA((2,))],
         jnp.transpose(weight_one, (2, 3, 4, 0, 1)).reshape(27, 8, 64),
         bias_one,
         jnp.transpose(weight_two, (2, 3, 4, 0, 1)).reshape(27, 8, 64),
         bias_two,
         scalars=(1, 3),
-    )
-    mine = jnp.stack(spread([units] * 4))
+        far=(0, 2),
+    )
+    mine = spread([units] * 4)
+
+    (pieces,) = call(
+        prepare_kernel,
+        [((8, 168, 128), BF16)],
+        [((2, 8, 64, 128), BF16), ((1072, 128), F32), pltpu.SemaphoreType.DMA((2,))],
+        place,
+        volume.reshape(8, 64, 128),
+        cotangent.reshape(8, 64, 128),
+        scalars=(0,),
+        far=(1, 2),
+    )
+    received = lax.all_to_all(pieces, CHAN, 0, 0)
+    field, cots = call(
+        unpack_kernel, [((11, 64, 128), BF16), ((10, 64, 128), BF16)], [], received
+    )
+    near_even = lax.ppermute(field, near, even)
+    near_odd = lax.ppermute(field, near, odd)
+    mine, near_even = lax.optimization_barrier((mine, near_even))
+    mine = jnp.stack(mine)
     other = lax.ppermute(mine, "c", swap)
     weights, weights_back, bias = call(
         weights_kernel,
@@ -377,24 +422,7 @@
         scalars=(0,),
     )
 
-    (pieces,) = call(
-        prepare_kernel,
-        [((8, 168, 128), BF16)],
-        [((2, 8, 64, 128), BF16), ((1072, 128), F32), pltpu.SemaphoreType.DMA((2,))],
-        place,
-        volume.reshape(8, 64, 128),
-        cotangent.reshape(8, 64, 128),
-        scalars=(0,),
-        far=(1, 2),
-    )
-    received = lax.all_to_all(pieces, CHAN, 0, 0)
-    field, cots = call(
-        unpack_kernel, [((11, 64, 128), BF16), ((10, 64, 128), BF16)], [], received
-    )
-    before = lax.ppermute(field, near, up)
-    after = lax.ppermute(field, near, down)
-
-    act, wide, delta, feats, to_prev, to_next = call(
+    act, wide, delta, feats, to_even, to_odd = call(
         forward_kernel,
         [
             ((192, 1536), BF16),
@@ -407,16 +435,16 @@
         [((10, 64, 128), F32)],
         place,
         field,
-        before,
-        after,
+        near_even,
+        near_odd,
         cots,
         weights,
         bias,
         scalars=(0,),
         flops=2 * 192 * 576 * 128 * 30,
     )
-    from_next = lax.ppermute(to_prev, near, down)
-    from_prev = lax.ppermute(to_next, near, up)
+    from_even = lax.ppermute(to_even, near, even)
+    from_odd = lax.ppermute(to_odd, near, odd)
     grad_two, total_two, narrow = call(
         second_grad_kernel,
         [((192, 576), F32), ((64, 128), F32), ((192, 1280), BF16)],
@@ -432,8 +460,8 @@
         [((192, 1280), BF16), ((192, 1024), BF16), ((192, 1152), F32)],
         place,
         delta,
-        from_prev,
-        from_next,
+        from_even,
+        from_odd,
         weights_back,
         act,
         narrow,
@@ -443,16 +471,18 @@
         flops=4 * 192 * 576 * 1024,
     )
 
-    part = keep.astype(F32) + lax.ppermute(send, "c", swap).astype(F32)
-    part = jnp.broadcast_to(part.astype(BF16)[None], (2, 4, 224, 128)).reshape(8, 224, 128)
-    part = lax.all_to_all(part, ("h", "l"), 0, 0)
-    part = jnp.sum(part.astype(F32), axis=0).astype(BF16)
-    whole = lax.all_to_all(jnp.broadcast_to(part, (16, 224, 128)), PLANE, 0, 0)
+    other = lax.ppermute(send, "c", swap)
+    parts = [(keep[k].astype(F32) + other[k].astype(F32)).astype(BF16) for k in range(4)]
+    part = sum_of_four(spread(parts)).astype(BF16)
+    other = lax.ppermute(part, "h", swap)
+    part = (part.astype(F32) + other.astype(F32)).astype(BF16)
+    part = sum_of_four(spread([part] * 4, "y")).astype(BF16)
+    parts = spread([part] * 4, "x")
     kernel_two, kernel_one, offsets = call(
         functools.partial(finish_kernel, factor),
         [((27, 8, 64), F32), ((27, 8, 64), F32), ((8, 128), F32)],
         [],
-        whole,
+        *parts,
     )
     kernel_one, kernel_two = (
         jnp.transpose(k.reshape(3, 3, 3, 8, 64), (3, 4, 0, 1, 2)) for k in (kernel_one, kernel_two)

time: 120 us -> 103 us (0.86)
  waiting for transfers between devices: 34.6 us -> 22.2 us
  blocking collectives: 23 us -> 17.2 us
  starting transfers between devices: 43.2 us -> 45.7 us
    ppermute x11 -> x21, starting transfers between devices: 18.9 us -> 45.5 us  [the longest x15 23.6 us: spread(): lax.ppermute(pieces[k], axis, turns[k])]
    all_to_all x2 -> x0, starting transfers between devices: 24.1 us -> none  [the longest x1 18.1 us: shards(): whole = lax.all_to_all(jnp.broadcast_to(part, (16, 224, 128)), PLANE, 0, 0)]
    ppermute x11 -> x21, waiting for transfers between devices: 30.7 us -> 22.2 us  [the longest x15 12.2 us: spread(): lax.ppermute(pieces[k], axis, turns[k])]
    all_to_all x1, blocking collectives: 23 us -> 17.2 us  [shards(): received = lax.all_to_all(pieces, CHAN, 0, 0)]
    all_to_all x2 -> x0, waiting for transfers between devices: 2.6 us -> none  [the longest x1 2.6 us: shards(): whole = lax.all_to_all(jnp.broadcast_to(part, (16, 224, 128)), PLANE, 0, 0)]
    ppermute x1, waiting for transfers between devices: 1.24 us -> 0.01 us  [shards(): other = lax.ppermute(jnp.stack([piece[1] for piece in feats]), 'c', swap)]
  transfers between devices with their start and end apart: 15 -> 23, of which waited for: 11 -> 12; matrix products, arithmetic and copies ran while one was open for 0% -> 0% of each run, Pallas kernels for 3% -> 4%
where the time goes in v3:
time: 103 us; the launch traced here: 102 us
  starting transfers between devices  45.7 us (44%)
  waiting for transfers between devices  22.2 us (22%)
  blocking collectives  17.2 us (17%)
  Pallas kernels  13.2 us (13%)
  local copies, waits for them, and re-layouts  2.62 us (3%)
    ppermute x15, starting transfers between devices, spread(): lax.ppermute(pieces[k], axis, turns[k])  23.6 us
    all_to_all x1, blocking collectives, shards(): received = lax.all_to_all(pieces, CHAN, 0, 0)  17.2 us
    pallas_call x9, Pallas kernels, call(): pl.pallas_call(kernel, out_shape=outs, in_specs=[smem if k in scalars els...  13.2 us
    ppermute x15, waiting for transfers between devices, spread(): lax.ppermute(pieces[k], axis, turns[k])  12.2 us
    ppermute x1, starting transfers between devices, shards(): from_odd = lax.ppermute(to_odd, near, odd)  11.4 us
    ppermute x1, starting transfers between devices, shards(): other = lax.ppermute(part, 'h', swap)  5.48 us
    ppermute x1, starting transfers between devices, shards(): near_odd = lax.ppermute(field, near, odd)  4.32 us
    ppermute x1, waiting for transfers between devices, shards(): near_odd = lax.ppermute(field, near, odd)  4.12 us
  transfers between devices with their start and end apart: 23, of which 12 were waited for; matrix products, arithmetic and copies ran while one was open for 0% of the time, Pallas kernels for 4%

profile of v3, /device:TPU:8, one launch (start us, length us, event | category | flops | bytes accessed | tf_op | source)
XLA Modules:
  0.0 102.0 jit_solution(6851202957246261916)
XLA Ops:
  0.7 0.1 stack.41.place
  0.8 0.9 copy-done
  1.7 0.9 copy-done.1
  2.6 1.2 %shard_map.101 = bf16[8,168,128]{2,1,0:T(8,128)(2,1)S(1)} custom-call(s32[5]{0:T(128)S(1)} %stack.41.place, bf16[8,64,128]{2,1,0:T(8,128)(2,1)S(1)} %bitcast.46, bf16[8,64,128]{2,1,0:T(8,128)(2,1)S(1)} %bitcast.47), custom_call_target="tpu_custom_call" | custom-call | bytes 606228 | tf_op jit(solution)/shard_map/pallas_call | solution.py:343
  3.7 17.2 %all_to_all.5.received = bf16[8,168,128]{2,1,0:T(8,128)(2,1)S(1)} all-to-all(bf16[8,168,128]{2,1,0:T(8,128)(2,1)S(1)} %shard_map.101), channel_id=1, replica_groups=mesh['x'=4,'h'=2,'y'=4,'l'=4,'c'=2] {'l','c'}, dimensions={0} | all-to-all | bytes 688128 | tf_op jit(solution)/shard_map/all_to_all | solution.py:406
  20.9 0.1 shard_map.102
  21.0 0.5 collective-permute-start.3
  21.6 0.8 shard_map.103
  22.3 1.3 %collective-permute-start.2 = (bf16[224,128]{1,0:T(8,128)(2,1)S(1)}, bf16[224,128]{1,0:T(8,128)(2,1)S(1)}, u32[]{:S(2)}, u32[]{:S(2)}) collective-permute-start(bf16[224,128]{1,0:T(8,128)(2,1)S(1)} %shard_map.103), channel_id=1, source_target_pairs={{0,6},{2,0},{4,2},{6,4},{1,7},{3,1},{5,3},{7,5},{8,14},{10,8},{12,... | collective-permute-start | bytes 172040 | tf_op jit(solution)/shard_map/ppermute | solution.py:381
  23.7 0.5 collective-permute-start.1
  24.2 0.3 collective-permute-start
  24.5 2.1 %collective-permute-done.2 = bf16[224,128]{1,0:T(8,128)(2,1)S(1)} collective-permute-done((bf16[224,128]{1,0:T(8,128)(2,1)S(1)}, bf16[224,128]{1,0:T(8,128)(2,1)S(1)}, u32[]{:S(2)}, u32[]{:S(2)}) %collective-permute-start.2) | collective-permute-done | bytes 57376 | tf_op jit(solution)/shard_map/ppermute | solution.py:381
  26.6 3.0 %collective-permute-done.1 = bf16[224,128]{1,0:T(8,128)(2,1)S(1)} collective-permute-done((bf16[224,128]{1,0:T(8,128)(2,1)S(1)}, bf16[224,128]{1,0:T(8,128)(2,1)S(1)}, u32[]{:S(2)}, u32[]{:S(2)}) %collective-permute-start.1) | collective-permute-done | bytes 57376 | tf_op jit(solution)/shard_map/ppermute | solution.py:381
  29.6 0.6 collective-permute-done
  30.3 0.1 collective-permute-start.5
  30.4 4.3 %collective-permute-start.4 = (bf16[11,64,128]{2,1,0:T(8,128)(2,1)S(1)}, bf16[11,64,128]{2,1,0:T(8,128)(2,1)S(1)}, u32[]{:S(2)}, u32[]{:S(2)}) collective-permute-start(bf16[11,64,128]{2,1,0:T(8,128)(2,1)S(1)} %get-tuple-element.29.own), channel_id=1, source_target_pairs={{8,16},{16,8},{10,18},{18,10},{12,20},{20,12},{14,22},{22,14},{24,... | collective-permute-start | bytes 540680 | tf_op jit(solution)/shard_map/ppermute | solution.py:411
  34.7 1.1 %shard_map.104 = (bf16[192,1152]{1,0:T(8,128)(2,1)S(1)}, bf16[192,576]{1,0:T(8,128)(2,1)S(1)}, f32[2,64,128]{2,1,0:T(8,128)S(1)}) custom-call(s32[5]{0:T(128)S(1)} %stack.41.place, bf16[4,224,128]{2,1,0:T(8,128)(2,1)S(1)} %pad_maximum_fusion.mine, bf16[4,224,128]{2,1,0:T(8,128)(2,1)S(1)} %collective-permute-done.5.other), custom_call_target="tpu_custom_call" | custom-call | bytes 1187860 | tf_op jit(solution)/shard_map/pallas_call | solution.py:343
  35.8 4.1 %collective-permute-done.4.odd = bf16[11,64,128]{2,1,0:T(8,128)(2,1)S(1)} collective-permute-done((bf16[11,64,128]{2,1,0:T(8,128)(2,1)S(1)}, bf16[11,64,128]{2,1,0:T(8,128)(2,1)S(1)}, u32[]{:S(2)}, u32[]{:S(2)}) %collective-permute-start.4) | collective-permute-done | bytes 180256 | tf_op jit(solution)/shard_map/ppermute | solution.py:411
  39.9 5.4 %shard_map.105 = (bf16[192,1536]{1,0:T(8,128)(2,1)S(1)}, bf16[192,2816]{1,0:T(8,128)(2,1)S(1)}, bf16[10,64,128]{2,1,0:T(8,128)(2,1)S(1)}, bf16[4,2,64,128]{3,2,1...) custom-call(s32[5]{0:T(128)S(1)} %stack.41.place, ...), custom_call_target="tpu_custom_call" | custom-call | flops 849346560 | bytes 3342356 | tf_op jit(solution)/shard_map/pallas_call | solution.py:343
  45.3 0.1 collective-permute-start.10
  45.4 11.4 %collective-permute-start.11 = (bf16[5,64,128]{2,1,0:T(8,128)(2,1)S(1)}, bf16[5,64,128]{2,1,0:T(8,128)(2,1)S(1)}, u32[]{:S(2)}, u32[]{:S(2)}) collective-permute-start(bf16[5,64,128]{2,1,0:T(8,128)(2,1)S(1)} %get-tuple-element.41), channel_id=1, source_target_pairs={{8,16},{16,8},{10,18},{18,10},{12,20},{20,12},{14,22},{22,14},{24,... | collective-permute-start | bytes 245768 | tf_op jit(solution)/shard_map/ppermute | solution.py:447
  56.8 0.6 shard_map.107
  57.4 1.8 %collective-permute-done.11.from_odd = bf16[5,64,128]{2,1,0:T(8,128)(2,1)S(1)} collective-permute-done((bf16[5,64,128]{2,1,0:T(8,128)(2,1)S(1)}, bf16[5,64,128]{2,1,0:T(8,128)(2,1)S(1)}, u32[]{:S(2)}, u32[]{:S(2)}) %collective-permute-start.11) | collective-permute-done | bytes 81952 | tf_op jit(solution)/shard_map/ppermute | solution.py:447
  59.2 1.9 %shard_map.108 = (bf16[4,224,128]{2,1,0:T(8,128)(2,1)S(1)}, bf16[4,224,128]{2,1,0:T(8,128)(2,1)S(1)}) custom-call(s32[5]{0:T(128)S(1)} %stack.41.place, bf16[10,64,128]{2,1,0:T(8,128)(2,1)S(1)} %get-tuple-element.39.delta, bf16[5,64,128]{2,1,0:T(8,128)(2,1)S(1)} %collective-permute-done.10.from_even, ...), custom_call_target="tpu_custom_call" | custom-call | flops 452984832 | bytes 2564116 | tf_op jit(solution)/shard_map/pallas_call | solution.py:343
  61.1 0.1 collective-permute-start.12
  61.2 1.5 %collective-permute-done.12 = bf16[4,224,128]{2,1,0:T(8,128)(2,1)S(1)} collective-permute-done((bf16[4,224,128]{2,1,0:T(8,128)(2,1)S(1)}, bf16[4,224,128]{2,1,0:T(8,128)(2,1)S(1)}, u32[]{:S(2)}, u32[]{:S(2)}) %collective-permute-start.12) | collective-permute-done | bytes 229408 | tf_op jit(solution)/shard_map/ppermute | solution.py:474
  62.7 0.1 collective-permute-start.13
  62.8 1.4 %collective-permute-start.15 = (bf16[224,128]{1,0:T(8,128)(2,1)S(1)}, bf16[224,128]{1,0:T(8,128)(2,1)S(1)}, u32[]{:S(2)}, u32[]{:S(2)}) collective-permute-start(bf16[224,128]{1,0:T(8,128)(2,1)S(1)} %get-tuple-element.56), channel_id=1, source_target_pairs={{0,6},{2,0},{4,2},{6,4},{1,7},{3,1},{5,3},{7,5},{8,14},{10,8},{12,... | collective-permute-start | bytes 172040 | tf_op jit(solution)/shard_map/ppermute | solution.py:381
  64.2 0.7 collective-permute-start.14
  64.9 3.2 %collective-permute-start.8 = (bf16[2,64,128]{2,1,0:T(8,128)(2,1)S(1)}, bf16[2,64,128]{2,1,0:T(8,128)(2,1)S(1)}, u32[]{:S(2)}, u32[]{:S(2)}) collective-permute-start(bf16[2,64,128]{2,1,0:T(8,128)(2,1)S(1)} %get-tuple-element.58), channel_id=1, source_target_pairs={{0,6},{2,0},{4,2},{6,4},{1,7},{3,1},{5,3},{7,5},{8,14},{10,8},{12,... | collective-permute-start | bytes 98312 | tf_op jit(solution)/shard_map/ppermute | solution.py:381
  68.1 0.1 collective-permute-start.7
  68.3 0.1 collective-permute-done.13
  68.4 1.5 %collective-permute-start.6 = (bf16[2,64,128]{2,1,0:T(8,128)(2,1)S(1)}, bf16[2,64,128]{2,1,0:T(8,128)(2,1)S(1)}, u32[]{:S(2)}, u32[]{:S(2)}) collective-permute-start(bf16[2,64,128]{2,1,0:T(8,128)(2,1)S(1)} %get-tuple-element.60), channel_id=1, source_target_pairs={{0,2},{2,4},{4,6},{6,0},{1,3},{3,5},{5,7},{7,1},{8,10},{10,12},{12... | collective-permute-start | bytes 98312 | tf_op jit(solution)/shard_map/ppermute | solution.py:381
  69.8 1.3 %collective-permute-done.14 = bf16[224,128]{1,0:T(8,128)(2,1)S(1)} collective-permute-done((bf16[224,128]{1,0:T(8,128)(2,1)S(1)}, bf16[224,128]{1,0:T(8,128)(2,1)S(1)}, u32[]{:S(2)}, u32[]{:S(2)}) %collective-permute-start.14) | collective-permute-done | bytes 57376 | tf_op jit(solution)/shard_map/ppermute | solution.py:381
  71.2 5.5 %collective-permute-start.16 = (bf16[224,128]{1,0:T(8,128)(2,1)S(1)}, bf16[224,128]{1,0:T(8,128)(2,1)S(1)}, u32[]{:S(2)}, u32[]{:S(2)}) collective-permute-start(bf16[224,128]{1,0:T(8,128)(2,1)S(1)} %fusion.1), channel_id=1, source_target_pairs={{0,32},{32,0},{1,33},{33,1},{2,34},{34,2},{3,35},{35,3},{4,36},{36... | collective-permute-start | bytes 172040 | tf_op jit(solution)/shard_map/ppermute | solution.py:477
  76.7 2.6 %collective-permute-done.16 = bf16[224,128]{1,0:T(8,128)(2,1)S(1)} collective-permute-done((bf16[224,128]{1,0:T(8,128)(2,1)S(1)}, bf16[224,128]{1,0:T(8,128)(2,1)S(1)}, u32[]{:S(2)}, u32[]{:S(2)}) %collective-permute-start.16) | collective-permute-done | bytes 57376 | tf_op jit(solution)/shard_map/ppermute | solution.py:477
  79.4 2.8 %collective-permute-start.19 = (bf16[224,128]{1,0:T(8,128)(2,1)S(1)}, bf16[224,128]{1,0:T(8,128)(2,1)S(1)}, u32[]{:S(2)}, u32[]{:S(2)}) collective-permute-start(bf16[224,128]{1,0:T(8,128)(2,1)S(1)} %add_convert_fusion.1), channel_id=1, source_target_pairs={{0,24},{8,0},{16,8},{24,16},{1,25},{9,1},{17,9},{25,17},{2,26},{10... | collective-permute-start | bytes 172040 | tf_op jit(solution)/shard_map/ppermute | solution.py:381
  82.2 6.1 %collective-permute-start.17 = (bf16[224,128]{1,0:T(8,128)(2,1)S(1)}, bf16[224,128]{1,0:T(8,128)(2,1)S(1)}, u32[]{:S(2)}, u32[]{:S(2)}) collective-permute-start(bf16[224,128]{1,0:T(8,128)(2,1)S(1)} %add_convert_fusion.1), channel_id=1, source_target_pairs={{0,16},{8,24},{16,0},{24,8},{1,17},{9,25},{17,1},{25,9},{2,18},{10... | collective-permute-start | bytes 172040 | tf_op jit(solution)/shard_map/ppermute | solution.py:381
  88.3 0.1 collective-permute-start.9
  88.4 2.0 %collective-permute-done.17 = bf16[224,128]{1,0:T(8,128)(2,1)S(1)} collective-permute-done((bf16[224,128]{1,0:T(8,128)(2,1)S(1)}, bf16[224,128]{1,0:T(8,128)(2,1)S(1)}, u32[]{:S(2)}, u32[]{:S(2)}) %collective-permute-start.17) | collective-permute-done | bytes 57376 | tf_op jit(solution)/shard_map/ppermute | solution.py:381
  90.4 3.8 %collective-permute-start.22 = (bf16[224,128]{1,0:T(8,128)(2,1)S(1)}, bf16[224,128]{1,0:T(8,128)(2,1)S(1)}, u32[]{:S(2)}, u32[]{:S(2)}) collective-permute-start(bf16[224,128]{1,0:T(8,128)(2,1)S(1)} %add_convert_fusion.first), channel_id=1, source_target_pairs={{0,192},{64,0},{128,64},{192,128},{1,193},{65,1},{129,65},{193,129... | collective-permute-start | bytes 172040 | tf_op jit(solution)/shard_map/ppermute | solution.py:381
  94.2 0.8 collective-permute-start.21
  95.1 0.9 collective-permute-start.20
  95.9 1.4 %shard_map.106 = bf16[8,64,128]{2,1,0:T(8,128)(2,1)} custom-call(s32[5]{0:T(128)S(1)} %stack.41.place, bf16[2,64,128]{2,1,0:T(8,128)(2,1)S(1)} %get-tuple-element.61.refs_0_, bf16[2,64,128]{2,1,0:T(8,128)(2,1)S(1)} %collective-permute-done.6.refs_1_, bf16[2,64,128]{2,1,0:T(8,128)(2,1)S(1)} %collective-permute-done.7.refs_2_, ...), custom_call_target="tpu_custom_call" | custom-call | bytes 327700 | tf_op jit(solution)/shard_map/pallas_call | solution.py:343
  97.4 2.6 %collective-permute-done.21.third = bf16[224,128]{1,0:T(8,128)(2,1)S(1)} collective-permute-done((bf16[224,128]{1,0:T(8,128)(2,1)S(1)}, bf16[224,128]{1,0:T(8,128)(2,1)S(1)}, u32[]{:S(2)}, u32[]{:S(2)}) %collective-permute-start.21) | collective-permute-done | bytes 57376 | tf_op jit(solution)/shard_map/ppermute | solution.py:381
  99.9 0.6 collective-permute-done.20.second
  100.5 0.8 shard_map.109
  101.3 0.7 slice_reduce_fusion
  (33 shorter events, 0.3 us)
Async XLA Ops:
  0.6 20.9 %copy-start.5 = (f32[8]{0:T(128)S(1)}, f32[8]{0:T(128)}, u32[]{:S(2)}) copy-start(f32[8]{0:T(128)} %bias_two.1) | copy-start | bytes 100
  0.6 20.9 %copy-start.4 = (f32[8]{0:T(128)S(1)}, f32[8]{0:T(128)}, u32[]{:S(2)}) copy-start(f32[8]{0:T(128)} %bias_one.1) | copy-start | bytes 100
  0.7 20.9 %copy-start.2 = (bf16[8,64,3,3,3]{1,0,4,3,2:T(8,128)(2,1)S(1)}, bf16[8,64,3,3,3]{1,0,4,3,2:T(8,128)(2,1)}, u32[]{:S(2)}) copy-start(bf16[8,64,3,3,3]{1,0,4,3,2:T(8,128)(2,1)} %param.7) | copy-start | bytes 82948
  0.8 0.9 copy-start
  1.7 0.9 copy-start.1
  2.6 19.0 %copy-start.3 = (bf16[8,64,3,3,3]{1,0,4,3,2:T(8,128)(2,1)S(1)}, bf16[8,64,3,3,3]{1,0,4,3,2:T(8,128)(2,1)}, u32[]{:S(2)}) copy-start(bf16[8,64,3,3,3]{1,0,4,3,2:T(8,128)(2,1)} %param.9) | copy-start | bytes 82948
  21.0 9.2 %collective-permute-start.3 = (bf16[11,64,128]{2,1,0:T(8,128)(2,1)S(1)}, bf16[11,64,128]{2,1,0:T(8,128)(2,1)S(1)}, u32[]{:S(2)}, u32[]{:S(2)}) collective-permute-start(bf16[11,64,128]{2,1,0:T(8,128)(2,1)S(1)} %get-tuple-element.29.own), channel_id=1, source_target_pairs={{0,8},{8,0},{2,10},{10,2},{4,12},{12,4},{6,14},{14,6},{16,24},{24,... | collective-permute-start | bytes 540680 | tf_op jit(solution)/shard_map/ppermute | solution.py:410
  22.3 4.3 %collective-permute-start.2 = (bf16[224,128]{1,0:T(8,128)(2,1)S(1)}, bf16[224,128]{1,0:T(8,128)(2,1)S(1)}, u32[]{:S(2)}, u32[]{:S(2)}) collective-permute-start(bf16[224,128]{1,0:T(8,128)(2,1)S(1)} %shard_map.103), channel_id=1, source_target_pairs={{0,6},{2,0},{4,2},{6,4},{1,7},{3,1},{5,3},{7,5},{8,14},{10,8},{12,... | collective-permute-start | bytes 172040 | tf_op jit(solution)/shard_map/ppermute | solution.py:381
  23.7 5.9 %collective-permute-start.1 = (bf16[224,128]{1,0:T(8,128)(2,1)S(1)}, bf16[224,128]{1,0:T(8,128)(2,1)S(1)}, u32[]{:S(2)}, u32[]{:S(2)}) collective-permute-start(bf16[224,128]{1,0:T(8,128)(2,1)S(1)} %shard_map.103), channel_id=1, source_target_pairs={{0,4},{2,6},{4,0},{6,2},{1,5},{3,7},{5,1},{7,3},{8,12},{10,14},{12... | collective-permute-start | bytes 172040 | tf_op jit(solution)/shard_map/ppermute | solution.py:381
  24.2 6.0 %collective-permute-start = (bf16[224,128]{1,0:T(8,128)(2,1)S(1)}, bf16[224,128]{1,0:T(8,128)(2,1)S(1)}, u32[]{:S(2)}, u32[]{:S(2)}) collective-permute-start(bf16[224,128]{1,0:T(8,128)(2,1)S(1)} %shard_map.103), channel_id=1, source_target_pairs={{0,2},{2,4},{4,6},{6,0},{1,3},{3,5},{5,7},{7,1},{8,10},{10,12},{12... | collective-permute-start | bytes 172040 | tf_op jit(solution)/shard_map/ppermute | solution.py:381
  30.3 4.4 %collective-permute-start.5 = (bf16[4,224,128]{2,1,0:T(8,128)(2,1)S(1)}, bf16[4,224,128]{2,1,0:T(8,128)(2,1)S(1)}, u32[]{:S(2)}, u32[]{:S(2)}) collective-permute-start(bf16[4,224,128]{2,1,0:T(8,128)(2,1)S(1)} %pad_maximum_fusion.mine), channel_id=1, source_target_pairs={{0,1},{1,0},{2,3},{3,2},{4,5},{5,4},{6,7},{7,6},{8,9},{9,8},{10,11... | collective-permute-start | bytes 688136 | tf_op jit(solution)/shard_map/ppermute | solution.py:414
  30.4 9.5 %collective-permute-start.4 = (bf16[11,64,128]{2,1,0:T(8,128)(2,1)S(1)}, bf16[11,64,128]{2,1,0:T(8,128)(2,1)S(1)}, u32[]{:S(2)}, u32[]{:S(2)}) collective-permute-start(bf16[11,64,128]{2,1,0:T(8,128)(2,1)S(1)} %get-tuple-element.29.own), channel_id=1, source_target_pairs={{8,16},{16,8},{10,18},{18,10},{12,20},{20,12},{14,22},{22,14},{24,... | collective-permute-start | bytes 540680 | tf_op jit(solution)/shard_map/ppermute | solution.py:411
  45.3 12.1 %collective-permute-start.10 = (bf16[5,64,128]{2,1,0:T(8,128)(2,1)S(1)}, bf16[5,64,128]{2,1,0:T(8,128)(2,1)S(1)}, u32[]{:S(2)}, u32[]{:S(2)}) collective-permute-start(bf16[5,64,128]{2,1,0:T(8,128)(2,1)S(1)} %get-tuple-element.40), channel_id=1, source_target_pairs={{0,8},{8,0},{2,10},{10,2},{4,12},{12,4},{6,14},{14,6},{16,24},{24,... | collective-permute-start | bytes 245768 | tf_op jit(solution)/shard_map/ppermute | solution.py:446
  45.4 13.8 %collective-permute-start.11 = (bf16[5,64,128]{2,1,0:T(8,128)(2,1)S(1)}, bf16[5,64,128]{2,1,0:T(8,128)(2,1)S(1)}, u32[]{:S(2)}, u32[]{:S(2)}) collective-permute-start(bf16[5,64,128]{2,1,0:T(8,128)(2,1)S(1)} %get-tuple-element.41), channel_id=1, source_target_pairs={{8,16},{16,8},{10,18},{18,10},{12,20},{20,12},{14,22},{22,14},{24,... | collective-permute-start | bytes 245768 | tf_op jit(solution)/shard_map/ppermute | solution.py:447
  61.1 1.6 %collective-permute-start.12 = (bf16[4,224,128]{2,1,0:T(8,128)(2,1)S(1)}, bf16[4,224,128]{2,1,0:T(8,128)(2,1)S(1)}, u32[]{:S(2)}, u32[]{:S(2)}) collective-permute-start(bf16[4,224,128]{2,1,0:T(8,128)(2,1)S(1)} %get-tuple-element.49), channel_id=1, source_target_pairs={{0,1},{1,0},{2,3},{3,2},{4,5},{5,4},{6,7},{7,6},{8,9},{9,8},{10,11... | collective-permute-start | bytes 688136 | tf_op jit(solution)/shard_map/ppermute | solution.py:474
  62.7 5.7 %collective-permute-start.13 = (bf16[224,128]{1,0:T(8,128)(2,1)S(1)}, bf16[224,128]{1,0:T(8,128)(2,1)S(1)}, u32[]{:S(2)}, u32[]{:S(2)}) collective-permute-start(bf16[224,128]{1,0:T(8,128)(2,1)S(1)} %get-tuple-element.55), channel_id=1, source_target_pairs={{0,4},{2,6},{4,0},{6,2},{1,5},{3,7},{5,1},{7,3},{8,12},{10,14},{12... | collective-permute-start | bytes 172040 | tf_op jit(solution)/shard_map/ppermute | solution.py:381
  62.8 7.1 %collective-permute-start.15 = (bf16[224,128]{1,0:T(8,128)(2,1)S(1)}, bf16[224,128]{1,0:T(8,128)(2,1)S(1)}, u32[]{:S(2)}, u32[]{:S(2)}) collective-permute-start(bf16[224,128]{1,0:T(8,128)(2,1)S(1)} %get-tuple-element.56), channel_id=1, source_target_pairs={{0,6},{2,0},{4,2},{6,4},{1,7},{3,1},{5,3},{7,5},{8,14},{10,8},{12,... | collective-permute-start | bytes 172040 | tf_op jit(solution)/shard_map/ppermute | solution.py:381
  64.2 6.9 %collective-permute-start.14 = (bf16[224,128]{1,0:T(8,128)(2,1)S(1)}, bf16[224,128]{1,0:T(8,128)(2,1)S(1)}, u32[]{:S(2)}, u32[]{:S(2)}) collective-permute-start(bf16[224,128]{1,0:T(8,128)(2,1)S(1)} %get-tuple-element.57), channel_id=1, source_target_pairs={{0,2},{2,4},{4,6},{6,0},{1,3},{3,5},{5,7},{7,1},{8,10},{10,12},{12... | collective-permute-start | bytes 172040 | tf_op jit(solution)/shard_map/ppermute | solution.py:381
  64.9 11.7 %collective-permute-start.8 = (bf16[2,64,128]{2,1,0:T(8,128)(2,1)S(1)}, bf16[2,64,128]{2,1,0:T(8,128)(2,1)S(1)}, u32[]{:S(2)}, u32[]{:S(2)}) collective-permute-start(bf16[2,64,128]{2,1,0:T(8,128)(2,1)S(1)} %get-tuple-element.58), channel_id=1, source_target_pairs={{0,6},{2,0},{4,2},{6,4},{1,7},{3,1},{5,3},{7,5},{8,14},{10,8},{12,... | collective-permute-start | bytes 98312 | tf_op jit(solution)/shard_map/ppermute | solution.py:381
  68.1 8.5 %collective-permute-start.7 = (bf16[2,64,128]{2,1,0:T(8,128)(2,1)S(1)}, bf16[2,64,128]{2,1,0:T(8,128)(2,1)S(1)}, u32[]{:S(2)}, u32[]{:S(2)}) collective-permute-start(bf16[2,64,128]{2,1,0:T(8,128)(2,1)S(1)} %get-tuple-element.59), channel_id=1, source_target_pairs={{0,4},{2,6},{4,0},{6,2},{1,5},{3,7},{5,1},{7,3},{8,12},{10,14},{12... | collective-permute-start | bytes 98312 | tf_op jit(solution)/shard_map/ppermute | solution.py:381
  68.4 8.3 %collective-permute-start.6 = (bf16[2,64,128]{2,1,0:T(8,128)(2,1)S(1)}, bf16[2,64,128]{2,1,0:T(8,128)(2,1)S(1)}, u32[]{:S(2)}, u32[]{:S(2)}) collective-permute-start(bf16[2,64,128]{2,1,0:T(8,128)(2,1)S(1)} %get-tuple-element.60), channel_id=1, source_target_pairs={{0,2},{2,4},{4,6},{6,0},{1,3},{3,5},{5,7},{7,1},{8,10},{10,12},{12... | collective-permute-start | bytes 98312 | tf_op jit(solution)/shard_map/ppermute | solution.py:381
  71.2 8.2 %collective-permute-start.16 = (bf16[224,128]{1,0:T(8,128)(2,1)S(1)}, bf16[224,128]{1,0:T(8,128)(2,1)S(1)}, u32[]{:S(2)}, u32[]{:S(2)}) collective-permute-start(bf16[224,128]{1,0:T(8,128)(2,1)S(1)} %fusion.1), channel_id=1, source_target_pairs={{0,32},{32,0},{1,33},{33,1},{2,34},{34,2},{3,35},{35,3},{4,36},{36... | collective-permute-start | bytes 172040 | tf_op jit(solution)/shard_map/ppermute | solution.py:477
  79.4 9.0 %collective-permute-start.19 = (bf16[224,128]{1,0:T(8,128)(2,1)S(1)}, bf16[224,128]{1,0:T(8,128)(2,1)S(1)}, u32[]{:S(2)}, u32[]{:S(2)}) collective-permute-start(bf16[224,128]{1,0:T(8,128)(2,1)S(1)} %add_convert_fusion.1), channel_id=1, source_target_pairs={{0,24},{8,0},{16,8},{24,16},{1,25},{9,1},{17,9},{25,17},{2,26},{10... | collective-permute-start | bytes 172040 | tf_op jit(solution)/shard_map/ppermute | solution.py:381
  82.2 6.2 %collective-permute-start.18 = (bf16[224,128]{1,0:T(8,128)(2,1)S(1)}, bf16[224,128]{1,0:T(8,128)(2,1)S(1)}, u32[]{:S(2)}, u32[]{:S(2)}) collective-permute-start(bf16[224,128]{1,0:T(8,128)(2,1)S(1)} %add_convert_fusion.1), channel_id=1, source_target_pairs={{0,8},{8,16},{16,24},{24,0},{1,9},{9,17},{17,25},{25,1},{2,10},{10... | collective-permute-start | bytes 172040 | tf_op jit(solution)/shard_map/ppermute | solution.py:381
  82.2 8.2 %collective-permute-start.17 = (bf16[224,128]{1,0:T(8,128)(2,1)S(1)}, bf16[224,128]{1,0:T(8,128)(2,1)S(1)}, u32[]{:S(2)}, u32[]{:S(2)}) collective-permute-start(bf16[224,128]{1,0:T(8,128)(2,1)S(1)} %add_convert_fusion.1), channel_id=1, source_target_pairs={{0,16},{8,24},{16,0},{24,8},{1,17},{9,25},{17,1},{25,9},{2,18},{10... | collective-permute-start | bytes 172040 | tf_op jit(solution)/shard_map/ppermute | solution.py:381
  88.3 7.7 %collective-permute-start.9 = (bf16[4,64,128]{2,1,0:T(8,128)(2,1)S(1)}, bf16[4,64,128]{2,1,0:T(8,128)(2,1)S(1)}, u32[]{:S(2)}, u32[]{:S(2)}) collective-permute-start(bf16[4,64,128]{2,1,0:T(8,128)(2,1)S(1)} %pad_maximum_fusion.1), channel_id=1, source_target_pairs={{0,1},{1,0},{2,3},{3,2},{4,5},{5,4},{6,7},{7,6},{8,9},{9,8},{10,11... | collective-permute-start | bytes 196616 | tf_op jit(solution)/shard_map/ppermute | solution.py:492
  90.4 6.9 %collective-permute-start.22 = (bf16[224,128]{1,0:T(8,128)(2,1)S(1)}, bf16[224,128]{1,0:T(8,128)(2,1)S(1)}, u32[]{:S(2)}, u32[]{:S(2)}) collective-permute-start(bf16[224,128]{1,0:T(8,128)(2,1)S(1)} %add_convert_fusion.first), channel_id=1, source_target_pairs={{0,192},{64,0},{128,64},{192,128},{1,193},{65,1},{129,65},{193,129... | collective-permute-start | bytes 172040 | tf_op jit(solution)/shard_map/ppermute | solution.py:381
  94.2 5.7 %collective-permute-start.21 = (bf16[224,128]{1,0:T(8,128)(2,1)S(1)}, bf16[224,128]{1,0:T(8,128)(2,1)S(1)}, u32[]{:S(2)}, u32[]{:S(2)}) collective-permute-start(bf16[224,128]{1,0:T(8,128)(2,1)S(1)} %add_convert_fusion.first), channel_id=1, source_target_pairs={{0,128},{64,192},{128,0},{192,64},{1,129},{65,193},{129,1},{193,65... | collective-permute-start | bytes 172040 | tf_op jit(solution)/shard_map/ppermute | solution.py:381
  95.1 5.5 %collective-permute-start.20 = (bf16[224,128]{1,0:T(8,128)(2,1)S(1)}, bf16[224,128]{1,0:T(8,128)(2,1)S(1)}, u32[]{:S(2)}, u32[]{:S(2)}) collective-permute-start(bf16[224,128]{1,0:T(8,128)(2,1)S(1)} %add_convert_fusion.first), channel_id=1, source_target_pairs={{0,64},{64,128},{128,192},{192,0},{1,65},{65,129},{129,193},{193,1... | collective-permute-start | bytes 172040 | tf_op jit(solution)/shard_map/ppermute | solution.py:381

commit v4 on v3

--- a/solution.py
+++ b/solution.py
@@ -15,6 +15,7 @@
 CHAN = ("l", "c")
 CONTRACT_LAST = (((1,), (1,)), ((), ()))
 VMEM_LIMIT = 48 * 1024 * 1024
+FULL_LIMIT = 63 * 1024 * 1024
 
 
 def leaky(value):
@@ -60,18 +61,68 @@
     )
 
 
-def weight_prepare_kernel(weight_one, bias_one, weight_two, bias_two, units, held, arrived):
+def turn_field(place, held, turned):
+    turned[0:24] = jnp.zeros((24, 128), F32)
+    turned[1048:1072] = jnp.zeros((24, 128), F32)
+    for ch in range(8):
+        value = held[ch].astype(F32)
+        turned[pl.ds(24 + ch, 128, stride=8), :] = jnp.concatenate([value, value], axis=0).T
+
+
+def target_of(place, block):
+    chip = jnp.where(place[3] == 1, 3 - block // 2, block // 2)
+    return lax.rem(chip + 4 - place[4], 4), jnp.where(place[2] == block % 2, 0, 1)
+
+
+def volume_kernel(place, volume, out, held, turned, arrived):
+    copy = pltpu.make_async_copy(volume, held, arrived)
+    copy.start()
+    low = lanes((88, 128)) < 64
+    copy.wait()
+    turn_field(place, held, turned)
+    for block in range(8):
+        turn, same = target_of(place, block)
+        rows = turned[block * 128 : block * 128 + 176].reshape(11, 2, 8, 128)
+        even, odd = (rows[:, k].reshape(88, 128) for k in range(2))
+        out[turn, same] = jnp.where(low, even, odd).astype(BF16)
+
+
+def rest_kernel(
+    place,
+    cotangent,
+    weight_one,
+    bias_one,
+    weight_two,
+    bias_two,
+    first,
+    second,
+    third,
+    fourth,
+    held,
+    turned,
+    kernels,
+    biases,
+    arrived,
+):
     copies = [
-        pltpu.make_async_copy(ref, held.at[k], arrived.at[k])
-        for k, ref in enumerate((weight_one, weight_two))
+        pltpu.make_async_copy(ref, to, arrived.at[k])
+        for k, (ref, to) in enumerate(
+            (
+                (cotangent, held),
+                (weight_one, kernels.at[0]),
+                (weight_two, kernels.at[1]),
+                (bias_one, biases.at[0]),
+                (bias_two, biases.at[1]),
+            )
+        )
     ]
     for copy in copies:
         copy.start()
+    for copy in copies:
+        copy.wait()
+
     row = lax.broadcasted_iota(jnp.int32, (8, 128), 0)
     lane = lanes((8, 128))
-
-    for copy in copies:
-        copy.wait()
     rows = []
     for t in range(9):
         for dy in range(3):
@@ -79,61 +130,68 @@
             for half in range(2):
                 layer, k = divmod(2 * t + half, 9)
                 dz, dx = divmod(k, 3)
-                halves.append(held[layer, dx * 9 + dy * 3 + dz].astype(F32))
+                halves.append(kernels[layer, dx * 9 + dy * 3 + dz].astype(F32))
             rows.append(jnp.concatenate(halves, axis=1))
     packed = jnp.zeros((8, 128), F32)
-    for layer, bias in enumerate((bias_one, bias_two)):
-        value = sum(jnp.where(row == o, bias[o], 0.0) for o in range(8))
+    for layer in range(2):
+        value = sum(jnp.where(row == o, biases[layer, o], 0.0) for o in range(8))
         for part in range(3):
             rounded = value.astype(BF16).astype(F32)
             packed = jnp.where(lane == 3 * layer + part, rounded, packed)
             value = value - rounded
     rows.append(packed)
-    units[...] = jnp.concatenate(rows, axis=0).astype(BF16)
-
-
-def prepare_kernel(place, volume, cotangent, out, held, turned, arrived):
-    copies = [
-        pltpu.make_async_copy(ref, held.at[k], arrived.at[k])
-        for k, ref in enumerate((volume, cotangent))
-    ]
-    for copy in copies:
-        copy.start()
-    low = lanes((88, 128)) < 64
-    turned[0:24] = jnp.zeros((24, 128), F32)
-    turned[1048:1072] = jnp.zeros((24, 128), F32)
-    for copy in copies:
-        copy.wait()
-    for ch in range(8):
-        both = jnp.concatenate([held[0, ch], held[1, ch]], axis=0).astype(F32)
-        turned[pl.ds(24 + ch, 128, stride=8), :] = both.T
-    for block in range(8):
-        target = jnp.where(place[3] == 1, 6 - 2 * (block // 2) + block % 2, block)
-        rows = turned[block * 128 : block * 128 + 176].reshape(11, 2, 8, 128)
-        even, odd = (rows[:, k].reshape(88, 128) for k in range(2))
-        field = jnp.where(low, even, pltpu.roll(odd, 64, 1))
-        left = turned[block * 128 + 16 : block * 128 + 96]
-        right = turned[block * 128 + 80 : block * 128 + 160]
-        cots = jnp.where(low[:80], pltpu.roll(left, 64, 1), right)
-        out[target] = jnp.concatenate([field, cots], axis=0).astype(BF16)
-
-
-def unpack_kernel(received, field, cots):
-    pieces = [received[src].astype(F32) for src in range(8)]
-    for j in range(21):
-        both = jnp.concatenate([piece[8 * j : 8 * j + 8] for piece in pieces], axis=0).astype(BF16)
-        if j < 11:
-            field[j] = both
-        else:
-            cots[j - 11] = both
-
-
-def weights_kernel(place, mine, other, out, back, bias):
+    turn_field(place, held, turned)
+    low = lanes((80, 128)) < 64
+    for k, out in enumerate((first, second, third, fourth)):
+        chip = lax.rem(place[4] + k, 4)
+        chip = jnp.where(place[3] == 1, 3 - chip, chip)
+        pieces = []
+        for same in range(2):
+            block = 2 * chip + (1 - place[2] if same else place[2])
+            start = pl.multiple_of(block * 128, 128)
+            pieces.append(jnp.where(low, turned[pl.ds(start + 16, 80)], turned[pl.ds(start + 80, 80)]))
+        out[...] = jnp.concatenate(pieces + rows, axis=0).astype(BF16)
+
+
+def channel_order(place, ours, theirs):
+    first = place[2] == 0
+    pieces = [None] * 8
+    pairs = [(jnp.where(first, a, b), jnp.where(first, b, a)) for a, b in zip(ours, theirs)]
+    for chip in range(4):
+        turn = lax.rem(place[4] + 4 - chip, 4)
+        for core in range(2):
+            value = pairs[3][core]
+            for k in range(3):
+                value = jnp.where(turn == k, pairs[k][core], value)
+            pieces[2 * chip + core] = value
+    return pieces
+
+
+def unpack_kernel(place, *refs):
+    ours, theirs, field = (refs[:4], refs[4:8], refs[8])
+    ours = [ref[0].astype(F32) for ref in ours]
+    theirs = [ref[1].astype(F32) for ref in theirs]
+    pieces = channel_order(place, ours, theirs)
+    for j in range(11):
+        both = jnp.concatenate([piece[8 * j : 8 * j + 8] for piece in pieces], axis=0)
+        field[j] = both.astype(BF16)
+
+
+def weights_kernel(place, *refs):
+    ours, theirs = (refs[:4], refs[4:8])
+    out, back, bias, cots = refs[8:]
+    pieces = channel_order(
+        place, [ref[0:80].astype(F32) for ref in ours], [ref[80:160].astype(F32) for ref in theirs]
+    )
+    for j in range(10):
+        both = jnp.concatenate([piece[8 * j : 8 * j + 8] for piece in pieces], axis=0)
+        cots[j] = both.astype(BF16)
+
     first = place[2] == 0
     for k in range(4):
         group = lax.rem(place[4] + 4 - k, 4)
-        ours, theirs = (ref[k].astype(F32) for ref in (mine, other))
-        pair = (jnp.where(first, ours, theirs), jnp.where(first, theirs, ours))
+        mine, other = (ref[160:384].astype(F32) for ref in (ours[k], theirs[k]))
+        pair = (jnp.where(first, mine, other), jnp.where(first, other, mine))
         rows = pl.ds(pl.multiple_of(48 * group, 16), 48)
         for t in range(9):
             block = jnp.concatenate([x[24 * t : 24 * t + 24] for x in pair], axis=0)
@@ -319,12 +377,12 @@
 
 
 def features_kernel(place, *refs):
-    pieces, other, out, turned = (refs[:4], refs[4], refs[5], refs[6])
+    pieces, other, out, turned = (refs[:4], refs[4:8], refs[8], refs[9])
     for k in range(4):
         group = lax.rem(place[4] + 4 - k, 4)
         group = jnp.where(place[3] == 1, 3 - group, group)
         for same in range(2):
-            value = (pieces[k][0] if same == 0 else other[k]).astype(F32)
+            value = (other[k][1] if same else pieces[k][0]).astype(F32)
             core = place[2] if same == 0 else 1 - place[2]
             start = pl.multiple_of(128 * (2 * group + core), 128)
             turned[pl.ds(start, 64), :] = value
@@ -333,10 +391,10 @@
         out[o] = turned[pl.ds(o, 128, stride=8), :].T[0:64].astype(BF16)
 
 
-def call(kernel, out_shapes, scratch, *args, scalars=(), far=(), flops=0):
+def call(kernel, out_shapes, scratch, *args, scalars=(), far=(), flops=0, limit=VMEM_LIMIT):
     vmem = pl.BlockSpec(memory_space=pltpu.VMEM)
     smem = pl.BlockSpec(memory_space=pltpu.SMEM)
-    anywhere = pl.BlockSpec(memory_space=pl.ANY)
+    anywhere = pl.BlockSpec(memory_space=pltpu.HBM)
     outs = [jax.ShapeDtypeStruct(shape, dtype) for shape, dtype in out_shapes]
     size = sum(a.size * a.dtype.itemsize for a in args)
     size += sum(o.size * o.dtype.itemsize for o in outs)
@@ -346,7 +404,7 @@
         in_specs=[smem if k in scalars else anywhere if k in far else vmem for k in range(len(args))],
         out_specs=[vmem] * len(outs),
         scratch_shapes=[pltpu.VMEM(*x) if isinstance(x, tuple) else x for x in scratch],
-        compiler_params=pltpu.CompilerParams(vmem_limit_bytes=VMEM_LIMIT),
+        compiler_params=pltpu.CompilerParams(vmem_limit_bytes=limit),
         cost_estimate=pl.CostEstimate(flops=flops, bytes_accessed=size, transcendentals=0),
     )(*args)
 
@@ -380,45 +438,59 @@
         turns = [[(i, (i + k) % 4) for i in range(4)] for k in range(4)]
         return [pieces[0]] + [lax.ppermute(pieces[k], axis, turns[k]) for k in range(1, 4)]
 
-    (units,) = call(
-        weight_prepare_kernel,
-        [((224, 128), BF16)],
-        [((2, 27, 8, 64), BF16), pltpu.SemaphoreType.DMA((2,))],
+    def cross(pieces):
+        return [lax.ppermute(piece, "c", swap) for piece in pieces]
+
+    (pieces,) = call(
+        volume_kernel,
+        [((4, 2, 88, 128), BF16)],
+        [((8, 64, 128), BF16), ((1072, 128), F32), pltpu.SemaphoreType.DMA(())],
+        place,
+        volume.reshape(8, 64, 128),
+        scalars=(0,),
+        far=(1,),
+    )
+    pieces = spread([pieces[k] for k in range(4)])
+    (field,) = call(
+        unpack_kernel,
+        [((11, 64, 128), BF16)],
+        [],
+        place,
+        *pieces,
+        *cross(pieces),
+        scalars=(0,),
+    )
+    near_even = lax.ppermute(field, near, even)
+    near_odd = lax.ppermute(field, near, odd)
+
+    rest = call(
+        rest_kernel,
+        [((384, 128), BF16)] * 4,
+        [
+            ((8, 64, 128), BF16),
+            ((1072, 128), F32),
+            ((2, 27, 8, 64), BF16),
+            pltpu.SMEM((2, 8), F32),
+            pltpu.SemaphoreType.DMA((5,)),
+        ],
+        place,
+        cotangent.reshape(8, 64, 128),
         jnp.transpose(weight_one, (2, 3, 4, 0, 1)).reshape(27, 8, 64),
         bias_one,
         jnp.transpose(weight_two, (2, 3, 4, 0, 1)).reshape(27, 8, 64),
         bias_two,
-        scalars=(1, 3),
-        far=(0, 2),
-    )
-    mine = spread([units] * 4)
-
-    (pieces,) = call(
-        prepare_kernel,
-        [((8, 168, 128), BF16)],
-        [((2, 8, 64, 128), BF16), ((1072, 128), F32), pltpu.SemaphoreType.DMA((2,))],
-        place,
-        volume.reshape(8, 64, 128),
-        cotangent.reshape(8, 64, 128),
-        scalars=(0,),
-        far=(1, 2),
-    )
-    received = lax.all_to_all(pieces, CHAN, 0, 0)
-    field, cots = call(
-        unpack_kernel, [((11, 64, 128), BF16), ((10, 64, 128), BF16)], [], received
-    )
-    near_even = lax.ppermute(field, near, even)
-    near_odd = lax.ppermute(field, near, odd)
-    mine, near_even = lax.optimization_barrier((mine, near_even))
-    mine = jnp.stack(mine)
-    other = lax.ppermute(mine, "c", swap)
-    weights, weights_back, bias = call(
+        scalars=(0,),
+        far=(1, 2, 3, 4, 5),
+        limit=FULL_LIMIT,
+    )
+    rest = spread(rest)
+    weights, weights_back, bias, cots = call(
         weights_kernel,
-        [((192, 1152), BF16), ((192, 576), BF16), ((2, 64, 128), F32)],
+        [((192, 1152), BF16), ((192, 576), BF16), ((2, 64, 128), F32), ((10, 64, 128), BF16)],
         [],
         place,
-        mine,
-        other,
+        *rest,
+        *cross(rest),
         scalars=(0,),
     )
 
@@ -489,14 +561,13 @@
     )
 
     feats = spread([feats[k] for k in range(4)])
-    other = lax.ppermute(jnp.stack([piece[1] for piece in feats]), "c", swap)
     (features,) = call(
         features_kernel,
         [((8, 64, 128), BF16)],
         [((1024, 128), F32)],
         place,
         *feats,
-        other,
+        *cross(feats),
         scalars=(0,),
     )
     return features.reshape(8, 2, 32, 128), kernel_one, offsets[:, 1], kernel_two, offsets[:, 0]

time: 103 us -> 95.5 us (0.927)
  blocking collectives: 17.2 us -> 0 us
  starting transfers between devices: 45.7 us -> 53.6 us
  Pallas kernels: 13.2 us -> 15.3 us
    all_to_all x1 -> x0, blocking collectives: 17.2 us -> none  [shards(): received = lax.all_to_all(pieces, CHAN, 0, 0)]
    ppermute x15 -> x18, starting transfers between devices: 23.6 us -> 31 us  [spread(): lax.ppermute(pieces[k], axis, turns[k])]
    ppermute x1, waiting for transfers between devices: 4.12 us -> 0.72 us  [shards(): near_odd = lax.ppermute(field, near, odd)]
    ppermute x2 -> x12, starting transfers between devices: 0.19 us -> 2.4 us  [cross(): return [lax.ppermute(piece, 'c', swap) for piece in pieces]]
    pallas_call x9, Pallas kernels: 13.2 us -> 15.3 us  [call(): pl.pallas_call(kernel, out_shape=outs, in_specs=[smem if k in scalars els...]
    ppermute x2 -> x12, waiting for transfers between devices: 0.01 us -> 1.91 us  [cross(): return [lax.ppermute(piece, 'c', swap) for piece in pieces]]
    ppermute x1, waiting for transfers between devices: 0.01 us -> 1.42 us  [shards(): near_even = lax.ppermute(field, near, even)]
    ppermute x1, starting transfers between devices: 11.4 us -> 10.2 us  [shards(): from_odd = lax.ppermute(to_odd, near, odd)]
  transfers between devices with their start and end apart: 23 -> 36, of which waited for: 12 -> 16; matrix products, arithmetic and copies ran while one was open for 0% -> 0% of each run, Pallas kernels for 4% -> 7%
where the time goes in v4:
time: 95.5 us; the launch traced here: 95.3 us
  starting transfers between devices  53.6 us (56%)
  waiting for transfers between devices  22.2 us (23%)
  Pallas kernels  15.3 us (16%)
  local copies, waits for them, and re-layouts  3.26 us (3%)
    ppermute x18, starting transfers between devices, spread(): lax.ppermute(pieces[k], axis, turns[k])  31 us
    pallas_call x9, Pallas kernels, call(): pl.pallas_call(kernel, out_shape=outs, in_specs=[smem if k in scalars els...  15.3 us
    ppermute x18, waiting for transfers between devices, spread(): lax.ppermute(pieces[k], axis, turns[k])  12.7 us
    ppermute x1, starting transfers between devices, shards(): from_odd = lax.ppermute(to_odd, near, odd)  10.2 us
    ppermute x1, starting transfers between devices, shards(): other = lax.ppermute(part, 'h', swap)  5.91 us
    ppermute x1, starting transfers between devices, shards(): near_odd = lax.ppermute(field, near, odd)  3.48 us
    unnamed x8, local copies, waits for them, and re-layouts  2.45 us
    ppermute x12, starting transfers between devices, cross(): return [lax.ppermute(piece, 'c', swap) for piece in pieces]  2.4 us
  transfers between devices with their start and end apart: 36, of which 16 were waited for; matrix products, arithmetic and copies ran while one was open for 0% of the time, Pallas kernels for 7%

profile of v4, /device:TPU:8, one launch (start us, length us, event | category | flops | bytes accessed | tf_op | source)
XLA Modules:
  0.0 95.3 jit_solution(1215963517916382747)
XLA Ops:
  0.7 0.9 copy-done
  1.6 0.9 shard_map.101
  2.6 4.7 %collective-permute-start.2 = (bf16[2,88,128]{2,1,0:T(8,128)(2,1)S(1)}, bf16[2,88,128]{2,1,0:T(8,128)(2,1)S(1)}, u32[]{:S(2)}, u32[]{:S(2)}) collective-permute-start(bf16[2,88,128]{2,1,0:T(8,128)(2,1)S(1)} %get-tuple-element.54), channel_id=1, source_target_pairs={{0,6},{2,0},{4,2},{6,4},{1,7},{3,1},{5,3},{7,5},{8,14},{10,8},{12,... | collective-permute-start | bytes 135176 | tf_op jit(solution)/shard_map/ppermute | solution.py:439
  7.3 2.5 %shard_map.103 = (bf16[384,128]{1,0:T(8,128)(2,1)}, bf16[384,128]{1,0:T(8,128)(2,1)}, bf16[384,128]{1,0:T(8,128)(2,1)}, bf16[384,128]{1,0:T(8,128)(2,1)}) custom-call(s32[5]{0:T(128)} %copy-done.2, bf16[8,64,128]{2,1,0:T(8,128)(2,1)} %bitcast.49, bf16[27,8,64]{2,1,0:T(8,128)(2,1)} %bitcast.50, f32[8]{0:T(128)} %bias_one.1, bf16[27,8,64]{2,1,0:T(8,128)(2,1)} %bitcast.51, ...), custom_call_target="tpu_custom_call" | custom-call | bytes 579668 | tf_op jit(solution)/shard_map/pallas_call | solution.py:401
  9.8 0.7 collective-permute-start.9
  10.6 2.8 %collective-permute-start = (bf16[2,88,128]{2,1,0:T(8,128)(2,1)S(1)}, bf16[2,88,128]{2,1,0:T(8,128)(2,1)S(1)}, u32[]{:S(2)}, u32[]{:S(2)}) collective-permute-start(bf16[2,88,128]{2,1,0:T(8,128)(2,1)S(1)} %get-tuple-element.56), channel_id=1, source_target_pairs={{0,2},{2,4},{4,6},{6,0},{1,3},{3,5},{5,7},{7,1},{8,10},{10,12},{12... | collective-permute-start | bytes 135176 | tf_op jit(solution)/shard_map/ppermute | solution.py:439
  13.4 0.5 collective-permute-start.6
  14.0 3.1 %collective-permute-done.refs_1_ = bf16[2,88,128]{2,1,0:T(8,128)(2,1)S(1)} collective-permute-done((bf16[2,88,128]{2,1,0:T(8,128)(2,1)S(1)}, bf16[2,88,128]{2,1,0:T(8,128)(2,1)S(1)}, u32[]{:S(2)}, u32[]{:S(2)}) %collective-permute-start) | collective-permute-done | bytes 45088 | tf_op jit(solution)/shard_map/ppermute | solution.py:439
  17.1 1.0 %collective-permute-start.10 = (bf16[384,128]{1,0:T(8,128)(2,1)}, bf16[384,128]{1,0:T(8,128)(2,1)S(1)}, u32[]{:S(2)}, u32[]{:S(2)}) collective-permute-start(bf16[384,128]{1,0:T(8,128)(2,1)} %get-tuple-element.29), channel_id=1, source_target_pairs={{0,4},{2,6},{4,0},{6,2},{1,5},{3,7},{5,1},{7,3},{8,12},{10,14},{12... | collective-permute-start | bytes 294920 | tf_op jit(solution)/shard_map/ppermute | solution.py:439
  18.1 1.7 %collective-permute-start.11 = (bf16[384,128]{1,0:T(8,128)(2,1)}, bf16[384,128]{1,0:T(8,128)(2,1)S(1)}, u32[]{:S(2)}, u32[]{:S(2)}) collective-permute-start(bf16[384,128]{1,0:T(8,128)(2,1)} %get-tuple-element.30), channel_id=1, source_target_pairs={{0,6},{2,0},{4,2},{6,4},{1,7},{3,1},{5,3},{7,5},{8,14},{10,8},{12,... | collective-permute-start | bytes 294920 | tf_op jit(solution)/shard_map/ppermute | solution.py:439
  19.8 0.6 copy-done.3
  20.5 0.6 shard_map.102.own
  21.1 3.5 %collective-permute-start.8 = (bf16[11,64,128]{2,1,0:T(8,128)(2,1)S(1)}, bf16[11,64,128]{2,1,0:T(8,128)(2,1)S(1)}, u32[]{:S(2)}, u32[]{:S(2)}) collective-permute-start(bf16[11,64,128]{2,1,0:T(8,128)(2,1)S(1)} %shard_map.102.own), channel_id=1, source_target_pairs={{8,16},{16,8},{10,18},{18,10},{12,20},{20,12},{14,22},{22,14},{24,... | collective-permute-start | bytes 540680 | tf_op jit(solution)/shard_map/ppermute | solution.py:464
  24.7 0.7 collective-permute-done.10.refs_2_
  25.4 0.5 collective-permute-start.14
  26.2 0.5 collective-permute-done.13.refs_5_
  26.8 0.4 collective-permute-done.15.refs_7_
  27.2 0.9 copy-done.1
  28.1 1.1 %shard_map.104 = (bf16[192,1152]{1,0:T(8,128)(2,1)S(1)}, bf16[192,576]{1,0:T(8,128)(2,1)S(1)}, f32[2,64,128]{2,1,0:T(8,128)S(1)}, bf16[10,64,128]{2,1,0:T(8,128)(2,1)S(1)}) custom-call(s32[5]{0:T(128)S(1)} %copy-done.3, bf16[384,128]{1,0:T(8,128)(2,1)S(1)} %copy-done.1, bf16[384,128]{1,0:T(8,128)(2,1)S(1)} %collective-permute-done.9.refs_1_, ...), custom_call_target="tpu_custom_call" | custom-call | bytes 1679380 | tf_op jit(solution)/shard_map/pallas_call | solution.py:401
  29.2 0.7 collective-permute-done.8.odd
  29.9 1.4 %collective-permute-done.7.even = bf16[11,64,128]{2,1,0:T(8,128)(2,1)S(1)} collective-permute-done((bf16[11,64,128]{2,1,0:T(8,128)(2,1)S(1)}, bf16[11,64,128]{2,1,0:T(8,128)(2,1)S(1)}, u32[]{:S(2)}, u32[]{:S(2)}) %collective-permute-start.7) | collective-permute-done | bytes 180256 | tf_op jit(solution)/shard_map/ppermute | solution.py:463
  31.4 5.4 %shard_map.105 = (bf16[192,1536]{1,0:T(8,128)(2,1)S(1)}, bf16[192,2816]{1,0:T(8,128)(2,1)S(1)}, bf16[10,64,128]{2,1,0:T(8,128)(2,1)S(1)}, bf16[4,2,64,128]{3,2,1...) custom-call(s32[5]{0:T(128)S(1)} %copy-done.3, ...), custom_call_target="tpu_custom_call" | custom-call | flops 849346560 | bytes 3342356 | tf_op jit(solution)/shard_map/pallas_call | solution.py:401
  36.8 0.4 collective-permute-start.23
  37.1 10.2 %collective-permute-start.24 = (bf16[5,64,128]{2,1,0:T(8,128)(2,1)S(1)}, bf16[5,64,128]{2,1,0:T(8,128)(2,1)S(1)}, u32[]{:S(2)}, u32[]{:S(2)}) collective-permute-start(bf16[5,64,128]{2,1,0:T(8,128)(2,1)S(1)} %get-tuple-element.37), channel_id=1, source_target_pairs={{8,16},{16,8},{10,18},{18,10},{12,20},{20,12},{14,22},{22,14},{24,... | collective-permute-start | bytes 245768 | tf_op jit(solution)/shard_map/ppermute | solution.py:519
  47.4 0.6 shard_map.107
  48.0 1.8 %collective-permute-done.24.from_odd = bf16[5,64,128]{2,1,0:T(8,128)(2,1)S(1)} collective-permute-done((bf16[5,64,128]{2,1,0:T(8,128)(2,1)S(1)}, bf16[5,64,128]{2,1,0:T(8,128)(2,1)S(1)}, u32[]{:S(2)}, u32[]{:S(2)}) %collective-permute-start.24) | collective-permute-done | bytes 81952 | tf_op jit(solution)/shard_map/ppermute | solution.py:519
  49.8 1.9 %shard_map.108 = (bf16[4,224,128]{2,1,0:T(8,128)(2,1)S(1)}, bf16[4,224,128]{2,1,0:T(8,128)(2,1)S(1)}) custom-call(s32[5]{0:T(128)S(1)} %copy-done.3, bf16[10,64,128]{2,1,0:T(8,128)(2,1)S(1)} %get-tuple-element.35.delta, bf16[5,64,128]{2,1,0:T(8,128)(2,1)S(1)} %collective-permute-done.23.from_even, bf16[5,64,128]{2,1,0:T(8,128)(2,1)S(1)} %collective-permute-done.24.from_odd, ...), custom_call_target="tpu_custom_call" | custom-call | flops 452984832 | bytes 2564116 | tf_op jit(solution)/shard_map/pallas_call | solution.py:401
  51.8 1.5 %collective-permute-done.25 = bf16[4,224,128]{2,1,0:T(8,128)(2,1)S(1)} collective-permute-done((bf16[4,224,128]{2,1,0:T(8,128)(2,1)S(1)}, bf16[4,224,128]{2,1,0:T(8,128)(2,1)S(1)}, u32[]{:S(2)}, u32[]{:S(2)}) %collective-permute-start.25) | collective-permute-done | bytes 229408 | tf_op jit(solution)/shard_map/ppermute | solution.py:546
  53.4 1.8 %collective-permute-start.28 = (bf16[224,128]{1,0:T(8,128)(2,1)S(1)}, bf16[224,128]{1,0:T(8,128)(2,1)S(1)}, u32[]{:S(2)}, u32[]{:S(2)}) collective-permute-start(bf16[224,128]{1,0:T(8,128)(2,1)S(1)} %get-tuple-element.52), channel_id=1, source_target_pairs={{0,6},{2,0},{4,2},{6,4},{1,7},{3,1},{5,3},{7,5},{8,14},{10,8},{12,... | collective-permute-start | bytes 172040 | tf_op jit(solution)/shard_map/ppermute | solution.py:439
  55.2 0.5 collective-permute-start.27
  55.7 3.4 %collective-permute-done.26 = bf16[224,128]{1,0:T(8,128)(2,1)S(1)} collective-permute-done((bf16[224,128]{1,0:T(8,128)(2,1)S(1)}, bf16[224,128]{1,0:T(8,128)(2,1)S(1)}, u32[]{:S(2)}, u32[]{:S(2)}) %collective-permute-start.26) | collective-permute-done | bytes 57376 | tf_op jit(solution)/shard_map/ppermute | solution.py:439
  59.0 2.1 %collective-permute-done.27 = bf16[224,128]{1,0:T(8,128)(2,1)S(1)} collective-permute-done((bf16[224,128]{1,0:T(8,128)(2,1)S(1)}, bf16[224,128]{1,0:T(8,128)(2,1)S(1)}, u32[]{:S(2)}, u32[]{:S(2)}) %collective-permute-start.27) | collective-permute-done | bytes 57376 | tf_op jit(solution)/shard_map/ppermute | solution.py:439
  61.2 5.9 %collective-permute-start.29 = (bf16[224,128]{1,0:T(8,128)(2,1)S(1)}, bf16[224,128]{1,0:T(8,128)(2,1)S(1)}, u32[]{:S(2)}, u32[]{:S(2)}) collective-permute-start(bf16[224,128]{1,0:T(8,128)(2,1)S(1)} %fusion.1), channel_id=1, source_target_pairs={{0,32},{32,0},{1,33},{33,1},{2,34},{34,2},{3,35},{35,3},{4,36},{36... | collective-permute-start | bytes 172040 | tf_op jit(solution)/shard_map/ppermute | solution.py:549
  67.1 2.3 %collective-permute-done.29 = bf16[224,128]{1,0:T(8,128)(2,1)S(1)} collective-permute-done((bf16[224,128]{1,0:T(8,128)(2,1)S(1)}, bf16[224,128]{1,0:T(8,128)(2,1)S(1)}, u32[]{:S(2)}, u32[]{:S(2)}) %collective-permute-start.29) | collective-permute-done | bytes 57376 | tf_op jit(solution)/shard_map/ppermute | solution.py:549
  69.4 2.4 %collective-permute-start.32 = (bf16[224,128]{1,0:T(8,128)(2,1)S(1)}, bf16[224,128]{1,0:T(8,128)(2,1)S(1)}, u32[]{:S(2)}, u32[]{:S(2)}) collective-permute-start(bf16[224,128]{1,0:T(8,128)(2,1)S(1)} %add_convert_fusion.1), channel_id=1, source_target_pairs={{0,24},{8,0},{16,8},{24,16},{1,25},{9,1},{17,9},{25,17},{2,26},{10... | collective-permute-start | bytes 172040 | tf_op jit(solution)/shard_map/ppermute | solution.py:439
  71.8 6.9 %collective-permute-start.30 = (bf16[224,128]{1,0:T(8,128)(2,1)S(1)}, bf16[224,128]{1,0:T(8,128)(2,1)S(1)}, u32[]{:S(2)}, u32[]{:S(2)}) collective-permute-start(bf16[224,128]{1,0:T(8,128)(2,1)S(1)} %add_convert_fusion.1), channel_id=1, source_target_pairs={{0,16},{8,24},{16,0},{24,8},{1,17},{9,25},{17,1},{25,9},{2,18},{10... | collective-permute-start | bytes 172040 | tf_op jit(solution)/shard_map/ppermute | solution.py:439
  78.7 1.7 %collective-permute-start.18 = (bf16[2,64,128]{2,1,0:T(8,128)(2,1)S(1)}, bf16[2,64,128]{2,1,0:T(8,128)(2,1)S(1)}, u32[]{:S(2)}, u32[]{:S(2)}) collective-permute-start(bf16[2,64,128]{2,1,0:T(8,128)(2,1)S(1)} %get-tuple-element.58), channel_id=1, source_target_pairs={{0,6},{2,0},{4,2},{6,4},{1,7},{3,1},{5,3},{7,5},{8,14},{10,8},{12,... | collective-permute-start | bytes 98312 | tf_op jit(solution)/shard_map/ppermute | solution.py:439
  80.5 2.3 %collective-permute-done.18.refs_3_ = bf16[2,64,128]{2,1,0:T(8,128)(2,1)S(1)} collective-permute-done((bf16[2,64,128]{2,1,0:T(8,128)(2,1)S(1)}, bf16[2,64,128]{2,1,0:T(8,128)(2,1)S(1)}, u32[]{:S(2)}, u32[]{:S(2)}) %collective-permute-start.18) | collective-permute-done | bytes 32800 | tf_op jit(solution)/shard_map/ppermute | solution.py:439
  82.8 0.5 collective-permute-start.22
  83.3 2.8 %collective-permute-start.35 = (bf16[224,128]{1,0:T(8,128)(2,1)S(1)}, bf16[224,128]{1,0:T(8,128)(2,1)S(1)}, u32[]{:S(2)}, u32[]{:S(2)}) collective-permute-start(bf16[224,128]{1,0:T(8,128)(2,1)S(1)} %add_convert_fusion.first), channel_id=1, source_target_pairs={{0,192},{64,0},{128,64},{192,128},{1,193},{65,1},{129,65},{193,129... | collective-permute-start | bytes 172040 | tf_op jit(solution)/shard_map/ppermute | solution.py:439
  86.1 2.4 %collective-permute-start.34 = (bf16[224,128]{1,0:T(8,128)(2,1)S(1)}, bf16[224,128]{1,0:T(8,128)(2,1)S(1)}, u32[]{:S(2)}, u32[]{:S(2)}) collective-permute-start(bf16[224,128]{1,0:T(8,128)(2,1)S(1)} %add_convert_fusion.first), channel_id=1, source_target_pairs={{0,128},{64,192},{128,0},{192,64},{1,129},{65,193},{129,1},{193,65... | collective-permute-start | bytes 172040 | tf_op jit(solution)/shard_map/ppermute | solution.py:439
  88.5 1.5 %collective-permute-start.33 = (bf16[224,128]{1,0:T(8,128)(2,1)S(1)}, bf16[224,128]{1,0:T(8,128)(2,1)S(1)}, u32[]{:S(2)}, u32[]{:S(2)}) collective-permute-start(bf16[224,128]{1,0:T(8,128)(2,1)S(1)} %add_convert_fusion.first), channel_id=1, source_target_pairs={{0,64},{64,128},{128,192},{192,0},{1,65},{65,129},{129,193},{193,1... | collective-permute-start | bytes 172040 | tf_op jit(solution)/shard_map/ppermute | solution.py:439
  90.0 0.5 collective-permute-start.20
  90.5 0.7 collective-permute-done.21.refs_6_
  91.3 1.4 %shard_map.106 = bf16[8,64,128]{2,1,0:T(8,128)(2,1)} custom-call(s32[5]{0:T(128)S(1)} %copy-done.3, bf16[2,64,128]{2,1,0:T(8,128)(2,1)S(1)} %get-tuple-element.61.refs_0_, bf16[2,64,128]{2,1,0:T(8,128)(2,1)S(1)} %collective-permute-done.16.refs_1_, bf16[2,64,128]{2,1,0:T(8,128)(2,1)S(1)} %collective-permute-done.17.refs_2_, ...), custom_call_target="tpu_custom_call" | custom-call | bytes 393236 | tf_op jit(solution)/shard_map/pallas_call | solution.py:401
  92.8 1.1 %collective-permute-done.33.second = bf16[224,128]{1,0:T(8,128)(2,1)S(1)} collective-permute-done((bf16[224,128]{1,0:T(8,128)(2,1)S(1)}, bf16[224,128]{1,0:T(8,128)(2,1)S(1)}, u32[]{:S(2)}, u32[]{:S(2)}) %collective-permute-start.33) | collective-permute-done | bytes 57376 | tf_op jit(solution)/shard_map/ppermute | solution.py:439
  93.8 0.8 shard_map.109
  94.6 0.7 slice_reduce_fusion
  (49 shorter events, 1.3 us)
Async XLA Ops:
  0.7 6.5 %copy-start.2 = (s32[5]{0:T(128)}, s32[5]{0:T(128)S(1)}, u32[]{:S(2)}) copy-start(s32[5]{0:T(128)S(1)} %stack.23.place) | copy-start | bytes 64
  0.7 0.9 copy-start
  2.6 10.8 %collective-permute-start.2 = (bf16[2,88,128]{2,1,0:T(8,128)(2,1)S(1)}, bf16[2,88,128]{2,1,0:T(8,128)(2,1)S(1)}, u32[]{:S(2)}, u32[]{:S(2)}) collective-permute-start(bf16[2,88,128]{2,1,0:T(8,128)(2,1)S(1)} %get-tuple-element.54), channel_id=1, source_target_pairs={{0,6},{2,0},{4,2},{6,4},{1,7},{3,1},{5,3},{7,5},{8,14},{10,8},{12,... | collective-permute-start | bytes 135176 | tf_op jit(solution)/shard_map/ppermute | solution.py:439
  7.3 6.6 %collective-permute-start.1 = (bf16[2,88,128]{2,1,0:T(8,128)(2,1)S(1)}, bf16[2,88,128]{2,1,0:T(8,128)(2,1)S(1)}, u32[]{:S(2)}, u32[]{:S(2)}) collective-permute-start(bf16[2,88,128]{2,1,0:T(8,128)(2,1)S(1)} %get-tuple-element.55), channel_id=1, source_target_pairs={{0,4},{2,6},{4,0},{6,2},{1,5},{3,7},{5,1},{7,3},{8,12},{10,14},{12... | collective-permute-start | bytes 135176 | tf_op jit(solution)/shard_map/ppermute | solution.py:439
  9.8 14.8 %collective-permute-start.9 = (bf16[384,128]{1,0:T(8,128)(2,1)}, bf16[384,128]{1,0:T(8,128)(2,1)S(1)}, u32[]{:S(2)}, u32[]{:S(2)}) collective-permute-start(bf16[384,128]{1,0:T(8,128)(2,1)} %get-tuple-element.28), channel_id=1, source_target_pairs={{0,2},{2,4},{4,6},{6,0},{1,3},{3,5},{5,7},{7,1},{8,10},{10,12},{12... | collective-permute-start | bytes 294920 | tf_op jit(solution)/shard_map/ppermute | solution.py:439
  10.6 6.6 %collective-permute-start = (bf16[2,88,128]{2,1,0:T(8,128)(2,1)S(1)}, bf16[2,88,128]{2,1,0:T(8,128)(2,1)S(1)}, u32[]{:S(2)}, u32[]{:S(2)}) collective-permute-start(bf16[2,88,128]{2,1,0:T(8,128)(2,1)S(1)} %get-tuple-element.56), channel_id=1, source_target_pairs={{0,2},{2,4},{4,6},{6,0},{1,3},{3,5},{5,7},{7,1},{8,10},{10,12},{12... | collective-permute-start | bytes 135176 | tf_op jit(solution)/shard_map/ppermute | solution.py:439
  13.4 3.7 %collective-permute-start.3 = (bf16[2,88,128]{2,1,0:T(8,128)(2,1)S(1)}, bf16[2,88,128]{2,1,0:T(8,128)(2,1)S(1)}, u32[]{:S(2)}, u32[]{:S(2)}) collective-permute-start(bf16[2,88,128]{2,1,0:T(8,128)(2,1)S(1)} %get-tuple-element.57.refs_0_), channel_id=1, source_target_pairs={{0,1},{1,0},{2,3},{3,2},{4,5},{5,4},{6,7},{7,6},{8,9},{9,8},{10,11... | collective-permute-start | bytes 135176 | tf_op jit(solution)/shard_map/ppermute | solution.py:442
  13.4 4.8 %collective-permute-start.6 = (bf16[2,88,128]{2,1,0:T(8,128)(2,1)S(1)}, bf16[2,88,128]{2,1,0:T(8,128)(2,1)S(1)}, u32[]{:S(2)}, u32[]{:S(2)}) collective-permute-start(bf16[2,88,128]{2,1,0:T(8,128)(2,1)S(1)} %collective-permute-done.2.refs_3_), channel_id=1, source_target_pairs={{0,1},{1,0},{2,3},{3,2},{4,5},{5,4},{6,7},{7,6},{8,9},{9,8},{10,11... | collective-permute-start | bytes 135176 | tf_op jit(solution)/shard_map/ppermute | solution.py:442
  13.9 5.9 %collective-permute-start.5 = (bf16[2,88,128]{2,1,0:T(8,128)(2,1)S(1)}, bf16[2,88,128]{2,1,0:T(8,128)(2,1)S(1)}, u32[]{:S(2)}, u32[]{:S(2)}) collective-permute-start(bf16[2,88,128]{2,1,0:T(8,128)(2,1)S(1)} %collective-permute-done.1.refs_2_), channel_id=1, source_target_pairs={{0,1},{1,0},{2,3},{3,2},{4,5},{5,4},{6,7},{7,6},{8,9},{9,8},{10,11... | collective-permute-start | bytes 135176 | tf_op jit(solution)/shard_map/ppermute | solution.py:442
  17.1 2.7 %collective-permute-start.4 = (bf16[2,88,128]{2,1,0:T(8,128)(2,1)S(1)}, bf16[2,88,128]{2,1,0:T(8,128)(2,1)S(1)}, u32[]{:S(2)}, u32[]{:S(2)}) collective-permute-start(bf16[2,88,128]{2,1,0:T(8,128)(2,1)S(1)} %collective-permute-done.refs_1_), channel_id=1, source_target_pairs={{0,1},{1,0},{2,3},{3,2},{4,5},{5,4},{6,7},{7,6},{8,9},{9,8},{10,11... | collective-permute-start | bytes 135176 | tf_op jit(solution)/shard_map/ppermute | solution.py:442
  17.1 8.3 %collective-permute-start.10 = (bf16[384,128]{1,0:T(8,128)(2,1)}, bf16[384,128]{1,0:T(8,128)(2,1)S(1)}, u32[]{:S(2)}, u32[]{:S(2)}) collective-permute-start(bf16[384,128]{1,0:T(8,128)(2,1)} %get-tuple-element.29), channel_id=1, source_target_pairs={{0,4},{2,6},{4,0},{6,2},{1,5},{3,7},{5,1},{7,3},{8,12},{10,14},{12... | collective-permute-start | bytes 294920 | tf_op jit(solution)/shard_map/ppermute | solution.py:439
  18.1 7.3 %collective-permute-start.11 = (bf16[384,128]{1,0:T(8,128)(2,1)}, bf16[384,128]{1,0:T(8,128)(2,1)S(1)}, u32[]{:S(2)}, u32[]{:S(2)}) collective-permute-start(bf16[384,128]{1,0:T(8,128)(2,1)} %get-tuple-element.30), channel_id=1, source_target_pairs={{0,6},{2,0},{4,2},{6,4},{1,7},{3,1},{5,3},{7,5},{8,14},{10,8},{12,... | collective-permute-start | bytes 294920 | tf_op jit(solution)/shard_map/ppermute | solution.py:439
  19.8 6.1 %collective-permute-start.12 = (bf16[384,128]{1,0:T(8,128)(2,1)}, bf16[384,128]{1,0:T(8,128)(2,1)S(1)}, u32[]{:S(2)}, u32[]{:S(2)}) collective-permute-start(bf16[384,128]{1,0:T(8,128)(2,1)} %get-tuple-element.27.refs_0_), channel_id=1, source_target_pairs={{0,1},{1,0},{2,3},{3,2},{4,5},{5,4},{6,7},{7,6},{8,9},{9,8},{10,11... | collective-permute-start | bytes 294920 | tf_op jit(solution)/shard_map/ppermute | solution.py:442
  19.8 0.7 copy-start.3
  21.1 8.9 %collective-permute-start.8 = (bf16[11,64,128]{2,1,0:T(8,128)(2,1)S(1)}, bf16[11,64,128]{2,1,0:T(8,128)(2,1)S(1)}, u32[]{:S(2)}, u32[]{:S(2)}) collective-permute-start(bf16[11,64,128]{2,1,0:T(8,128)(2,1)S(1)} %shard_map.102.own), channel_id=1, source_target_pairs={{8,16},{16,8},{10,18},{18,10},{12,20},{20,12},{14,22},{22,14},{24,... | collective-permute-start | bytes 540680 | tf_op jit(solution)/shard_map/ppermute | solution.py:464
  24.6 6.8 %collective-permute-start.7 = (bf16[11,64,128]{2,1,0:T(8,128)(2,1)S(1)}, bf16[11,64,128]{2,1,0:T(8,128)(2,1)S(1)}, u32[]{:S(2)}, u32[]{:S(2)}) collective-permute-start(bf16[11,64,128]{2,1,0:T(8,128)(2,1)S(1)} %shard_map.102.own), channel_id=1, source_target_pairs={{0,8},{8,0},{2,10},{10,2},{4,12},{12,4},{6,14},{14,6},{16,24},{24,... | collective-permute-start | bytes 540680 | tf_op jit(solution)/shard_map/ppermute | solution.py:463
  25.4 1.3 %collective-permute-start.13 = (bf16[384,128]{1,0:T(8,128)(2,1)S(1)}, bf16[384,128]{1,0:T(8,128)(2,1)S(1)}, u32[]{:S(2)}, u32[]{:S(2)}) collective-permute-start(bf16[384,128]{1,0:T(8,128)(2,1)S(1)} %collective-permute-done.9.refs_1_), channel_id=1, source_target_pairs={{0,1},{1,0},{2,3},{3,2},{4,5},{5,4},{6,7},{7,6},{8,9},{9,8},{10,11... | collective-permute-start | bytes 294920 | tf_op jit(solution)/shard_map/ppermute | solution.py:442
  25.4 1.4 %collective-permute-start.14 = (bf16[384,128]{1,0:T(8,128)(2,1)S(1)}, bf16[384,128]{1,0:T(8,128)(2,1)S(1)}, u32[]{:S(2)}, u32[]{:S(2)}) collective-permute-start(bf16[384,128]{1,0:T(8,128)(2,1)S(1)} %collective-permute-done.10.refs_2_), channel_id=1, source_target_pairs={{0,1},{1,0},{2,3},{3,2},{4,5},{5,4},{6,7},{7,6},{8,9},{9,8},{10,11... | collective-permute-start | bytes 294920 | tf_op jit(solution)/shard_map/ppermute | solution.py:442
  25.9 1.3 %collective-permute-start.15 = (bf16[384,128]{1,0:T(8,128)(2,1)S(1)}, bf16[384,128]{1,0:T(8,128)(2,1)S(1)}, u32[]{:S(2)}, u32[]{:S(2)}) collective-permute-start(bf16[384,128]{1,0:T(8,128)(2,1)S(1)} %collective-permute-done.11.refs_3_), channel_id=1, source_target_pairs={{0,1},{1,0},{2,3},{3,2},{4,5},{5,4},{6,7},{7,6},{8,9},{9,8},{10,11... | collective-permute-start | bytes 294920 | tf_op jit(solution)/shard_map/ppermute | solution.py:442
  27.2 0.9 copy-start.1
  36.8 11.3 %collective-permute-start.23 = (bf16[5,64,128]{2,1,0:T(8,128)(2,1)S(1)}, bf16[5,64,128]{2,1,0:T(8,128)(2,1)S(1)}, u32[]{:S(2)}, u32[]{:S(2)}) collective-permute-start(bf16[5,64,128]{2,1,0:T(8,128)(2,1)S(1)} %get-tuple-element.36), channel_id=1, source_target_pairs={{0,8},{8,0},{2,10},{10,2},{4,12},{12,4},{6,14},{14,6},{16,24},{24,... | collective-permute-start | bytes 245768 | tf_op jit(solution)/shard_map/ppermute | solution.py:518
  37.1 12.6 %collective-permute-start.24 = (bf16[5,64,128]{2,1,0:T(8,128)(2,1)S(1)}, bf16[5,64,128]{2,1,0:T(8,128)(2,1)S(1)}, u32[]{:S(2)}, u32[]{:S(2)}) collective-permute-start(bf16[5,64,128]{2,1,0:T(8,128)(2,1)S(1)} %get-tuple-element.37), channel_id=1, source_target_pairs={{8,16},{16,8},{10,18},{18,10},{12,20},{20,12},{14,22},{22,14},{24,... | collective-permute-start | bytes 245768 | tf_op jit(solution)/shard_map/ppermute | solution.py:519
  51.7 1.6 %collective-permute-start.25 = (bf16[4,224,128]{2,1,0:T(8,128)(2,1)S(1)}, bf16[4,224,128]{2,1,0:T(8,128)(2,1)S(1)}, u32[]{:S(2)}, u32[]{:S(2)}) collective-permute-start(bf16[4,224,128]{2,1,0:T(8,128)(2,1)S(1)} %get-tuple-element.45), channel_id=1, source_target_pairs={{0,1},{1,0},{2,3},{3,2},{4,5},{5,4},{6,7},{7,6},{8,9},{9,8},{10,11... | collective-permute-start | bytes 688136 | tf_op jit(solution)/shard_map/ppermute | solution.py:546
  53.3 5.7 %collective-permute-start.26 = (bf16[224,128]{1,0:T(8,128)(2,1)S(1)}, bf16[224,128]{1,0:T(8,128)(2,1)S(1)}, u32[]{:S(2)}, u32[]{:S(2)}) collective-permute-start(bf16[224,128]{1,0:T(8,128)(2,1)S(1)} %get-tuple-element.51), channel_id=1, source_target_pairs={{0,4},{2,6},{4,0},{6,2},{1,5},{3,7},{5,1},{7,3},{8,12},{10,14},{12... | collective-permute-start | bytes 172040 | tf_op jit(solution)/shard_map/ppermute | solution.py:439
  53.4 5.7 %collective-permute-start.28 = (bf16[224,128]{1,0:T(8,128)(2,1)S(1)}, bf16[224,128]{1,0:T(8,128)(2,1)S(1)}, u32[]{:S(2)}, u32[]{:S(2)}) collective-permute-start(bf16[224,128]{1,0:T(8,128)(2,1)S(1)} %get-tuple-element.52), channel_id=1, source_target_pairs={{0,6},{2,0},{4,2},{6,4},{1,7},{3,1},{5,3},{7,5},{8,14},{10,8},{12,... | collective-permute-start | bytes 172040 | tf_op jit(solution)/shard_map/ppermute | solution.py:439
  55.2 6.0 %collective-permute-start.27 = (bf16[224,128]{1,0:T(8,128)(2,1)S(1)}, bf16[224,128]{1,0:T(8,128)(2,1)S(1)}, u32[]{:S(2)}, u32[]{:S(2)}) collective-permute-start(bf16[224,128]{1,0:T(8,128)(2,1)S(1)} %get-tuple-element.53), channel_id=1, source_target_pairs={{0,2},{2,4},{4,6},{6,0},{1,3},{3,5},{5,7},{7,1},{8,10},{10,12},{12... | collective-permute-start | bytes 172040 | tf_op jit(solution)/shard_map/ppermute | solution.py:439
  61.2 8.2 %collective-permute-start.29 = (bf16[224,128]{1,0:T(8,128)(2,1)S(1)}, bf16[224,128]{1,0:T(8,128)(2,1)S(1)}, u32[]{:S(2)}, u32[]{:S(2)}) collective-permute-start(bf16[224,128]{1,0:T(8,128)(2,1)S(1)} %fusion.1), channel_id=1, source_target_pairs={{0,32},{32,0},{1,33},{33,1},{2,34},{34,2},{3,35},{35,3},{4,36},{36... | collective-permute-start | bytes 172040 | tf_op jit(solution)/shard_map/ppermute | solution.py:549
  69.4 13.4 %collective-permute-start.32 = (bf16[224,128]{1,0:T(8,128)(2,1)S(1)}, bf16[224,128]{1,0:T(8,128)(2,1)S(1)}, u32[]{:S(2)}, u32[]{:S(2)}) collective-permute-start(bf16[224,128]{1,0:T(8,128)(2,1)S(1)} %add_convert_fusion.1), channel_id=1, source_target_pairs={{0,24},{8,0},{16,8},{24,16},{1,25},{9,1},{17,9},{25,17},{2,26},{10... | collective-permute-start | bytes 172040 | tf_op jit(solution)/shard_map/ppermute | solution.py:439
  71.8 10.9 %collective-permute-start.31 = (bf16[224,128]{1,0:T(8,128)(2,1)S(1)}, bf16[224,128]{1,0:T(8,128)(2,1)S(1)}, u32[]{:S(2)}, u32[]{:S(2)}) collective-permute-start(bf16[224,128]{1,0:T(8,128)(2,1)S(1)} %add_convert_fusion.1), channel_id=1, source_target_pairs={{0,8},{8,16},{16,24},{24,0},{1,9},{9,17},{17,25},{25,1},{2,10},{10... | collective-permute-start | bytes 172040 | tf_op jit(solution)/shard_map/ppermute | solution.py:439
  71.8 11.4 %collective-permute-start.30 = (bf16[224,128]{1,0:T(8,128)(2,1)S(1)}, bf16[224,128]{1,0:T(8,128)(2,1)S(1)}, u32[]{:S(2)}, u32[]{:S(2)}) collective-permute-start(bf16[224,128]{1,0:T(8,128)(2,1)S(1)} %add_convert_fusion.1), channel_id=1, source_target_pairs={{0,16},{8,24},{16,0},{24,8},{1,17},{9,25},{17,1},{25,9},{2,18},{10... | collective-permute-start | bytes 172040 | tf_op jit(solution)/shard_map/ppermute | solution.py:439
  78.7 4.0 %collective-permute-start.18 = (bf16[2,64,128]{2,1,0:T(8,128)(2,1)S(1)}, bf16[2,64,128]{2,1,0:T(8,128)(2,1)S(1)}, u32[]{:S(2)}, u32[]{:S(2)}) collective-permute-start(bf16[2,64,128]{2,1,0:T(8,128)(2,1)S(1)} %get-tuple-element.58), channel_id=1, source_target_pairs={{0,6},{2,0},{4,2},{6,4},{1,7},{3,1},{5,3},{7,5},{8,14},{10,8},{12,... | collective-permute-start | bytes 98312 | tf_op jit(solution)/shard_map/ppermute | solution.py:439
  80.5 5.6 %collective-permute-start.17 = (bf16[2,64,128]{2,1,0:T(8,128)(2,1)S(1)}, bf16[2,64,128]{2,1,0:T(8,128)(2,1)S(1)}, u32[]{:S(2)}, u32[]{:S(2)}) collective-permute-start(bf16[2,64,128]{2,1,0:T(8,128)(2,1)S(1)} %get-tuple-element.59), channel_id=1, source_target_pairs={{0,4},{2,6},{4,0},{6,2},{1,5},{3,7},{5,1},{7,3},{8,12},{10,14},{12... | collective-permute-start | bytes 98312 | tf_op jit(solution)/shard_map/ppermute | solution.py:439
  82.7 5.7 %collective-permute-start.16 = (bf16[2,64,128]{2,1,0:T(8,128)(2,1)S(1)}, bf16[2,64,128]{2,1,0:T(8,128)(2,1)S(1)}, u32[]{:S(2)}, u32[]{:S(2)}) collective-permute-start(bf16[2,64,128]{2,1,0:T(8,128)(2,1)S(1)} %get-tuple-element.60), channel_id=1, source_target_pairs={{0,2},{2,4},{4,6},{6,0},{1,3},{3,5},{5,7},{7,1},{8,10},{10,12},{12... | collective-permute-start | bytes 98312 | tf_op jit(solution)/shard_map/ppermute | solution.py:439
  82.7 7.2 %collective-permute-start.19 = (bf16[2,64,128]{2,1,0:T(8,128)(2,1)S(1)}, bf16[2,64,128]{2,1,0:T(8,128)(2,1)S(1)}, u32[]{:S(2)}, u32[]{:S(2)}) collective-permute-start(bf16[2,64,128]{2,1,0:T(8,128)(2,1)S(1)} %get-tuple-element.61.refs_0_), channel_id=1, source_target_pairs={{0,1},{1,0},{2,3},{3,2},{4,5},{5,4},{6,7},{7,6},{8,9},{9,8},{10,11... | collective-permute-start | bytes 98312 | tf_op jit(solution)/shard_map/ppermute | solution.py:442
  82.8 7.2 %collective-permute-start.22 = (bf16[2,64,128]{2,1,0:T(8,128)(2,1)S(1)}, bf16[2,64,128]{2,1,0:T(8,128)(2,1)S(1)}, u32[]{:S(2)}, u32[]{:S(2)}) collective-permute-start(bf16[2,64,128]{2,1,0:T(8,128)(2,1)S(1)} %collective-permute-done.18.refs_3_), channel_id=1, source_target_pairs={{0,1},{1,0},{2,3},{3,2},{4,5},{5,4},{6,7},{7,6},{8,9},{9,8},{10,11... | collective-permute-start | bytes 98312 | tf_op jit(solution)/shard_map/ppermute | solution.py:442
  83.3 9.5 %collective-permute-start.35 = (bf16[224,128]{1,0:T(8,128)(2,1)S(1)}, bf16[224,128]{1,0:T(8,128)(2,1)S(1)}, u32[]{:S(2)}, u32[]{:S(2)}) collective-permute-start(bf16[224,128]{1,0:T(8,128)(2,1)S(1)} %add_convert_fusion.first), channel_id=1, source_target_pairs={{0,192},{64,0},{128,64},{192,128},{1,193},{65,1},{129,65},{193,129... | collective-permute-start | bytes 172040 | tf_op jit(solution)/shard_map/ppermute | solution.py:439
  86.1 6.7 %collective-permute-start.34 = (bf16[224,128]{1,0:T(8,128)(2,1)S(1)}, bf16[224,128]{1,0:T(8,128)(2,1)S(1)}, u32[]{:S(2)}, u32[]{:S(2)}) collective-permute-start(bf16[224,128]{1,0:T(8,128)(2,1)S(1)} %add_convert_fusion.first), channel_id=1, source_target_pairs={{0,128},{64,192},{128,0},{192,64},{1,129},{65,193},{129,1},{193,65... | collective-permute-start | bytes 172040 | tf_op jit(solution)/shard_map/ppermute | solution.py:439
  88.5 5.4 %collective-permute-start.33 = (bf16[224,128]{1,0:T(8,128)(2,1)S(1)}, bf16[224,128]{1,0:T(8,128)(2,1)S(1)}, u32[]{:S(2)}, u32[]{:S(2)}) collective-permute-start(bf16[224,128]{1,0:T(8,128)(2,1)S(1)} %add_convert_fusion.first), channel_id=1, source_target_pairs={{0,64},{64,128},{128,192},{192,0},{1,65},{65,129},{129,193},{193,1... | collective-permute-start | bytes 172040 | tf_op jit(solution)/shard_map/ppermute | solution.py:439
  90.0 1.2 %collective-permute-start.21 = (bf16[2,64,128]{2,1,0:T(8,128)(2,1)S(1)}, bf16[2,64,128]{2,1,0:T(8,128)(2,1)S(1)}, u32[]{:S(2)}, u32[]{:S(2)}) collective-permute-start(bf16[2,64,128]{2,1,0:T(8,128)(2,1)S(1)} %collective-permute-done.17.refs_2_), channel_id=1, source_target_pairs={{0,1},{1,0},{2,3},{3,2},{4,5},{5,4},{6,7},{7,6},{8,9},{9,8},{10,11... | collective-permute-start | bytes 98312 | tf_op jit(solution)/shard_map/ppermute | solution.py:442
  90.0 1.4 %collective-permute-start.20 = (bf16[2,64,128]{2,1,0:T(8,128)(2,1)S(1)}, bf16[2,64,128]{2,1,0:T(8,128)(2,1)S(1)}, u32[]{:S(2)}, u32[]{:S(2)}) collective-permute-start(bf16[2,64,128]{2,1,0:T(8,128)(2,1)S(1)} %collective-permute-done.16.refs_1_), channel_id=1, source_target_pairs={{0,1},{1,0},{2,3},{3,2},{4,5},{5,4},{6,7},{7,6},{8,9},{9,8},{10,11... | collective-permute-start | bytes 98312 | tf_op jit(solution)/shard_map/ppermute | solution.py:442

commit v5 on v4

--- a/solution.py
+++ b/solution.py
@@ -18,6 +18,13 @@
 FULL_LIMIT = 63 * 1024 * 1024
 
 
+def position():
+    h, l, c = (lax.axis_index(name) for name in ("h", "l", "c"))
+    space = (lax.axis_index("x") * 2 + h) * 4 + lax.axis_index("y")
+    block = 2 * jnp.where(h == 1, 3 - l, l) + c
+    return space, block, c, h, l
+
+
 def leaky(value):
     return jnp.maximum(value, SLOPE * value)
 
@@ -74,7 +81,8 @@
     return lax.rem(chip + 4 - place[4], 4), jnp.where(place[2] == block % 2, 0, 1)
 
 
-def volume_kernel(place, volume, out, held, turned, arrived):
+def volume_kernel(volume, out, held, turned, arrived):
+    place = position()
     copy = pltpu.make_async_copy(volume, held, arrived)
     copy.start()
     low = lanes((88, 128)) < 64
@@ -88,7 +96,6 @@
 
 
 def rest_kernel(
-    place,
     cotangent,
     weight_one,
     bias_one,
@@ -104,6 +111,7 @@
     biases,
     arrived,
 ):
+    place = position()
     copies = [
         pltpu.make_async_copy(ref, to, arrived.at[k])
         for k, (ref, to) in enumerate(
@@ -167,7 +175,8 @@
     return pieces
 
 
-def unpack_kernel(place, *refs):
+def unpack_kernel(*refs):
+    place = position()
     ours, theirs, field = (refs[:4], refs[4:8], refs[8])
     ours = [ref[0].astype(F32) for ref in ours]
     theirs = [ref[1].astype(F32) for ref in theirs]
@@ -177,7 +186,8 @@
         field[j] = both.astype(BF16)
 
 
-def weights_kernel(place, *refs):
+def weights_kernel(*refs):
+    place = position()
     ours, theirs = (refs[:4], refs[4:8])
     out, back, bias, cots = refs[8:]
     pieces = channel_order(
@@ -210,8 +220,9 @@
 
 
 def forward_kernel(
-    place, own, even, odd, cotangent, weights, bias, act, wide, delta, feats, to_even, to_odd, post
+    own, even, odd, cotangent, weights, bias, act, wide, delta, feats, to_even, to_odd, post
 ):
+    place = position()
     upper = lax.rem(place[0], 2) == 1
     lane = lanes((64, 128))
     low = lane < 64
@@ -309,8 +320,9 @@
 
 
 def backward_kernel(
-    place, delta, from_even, from_odd, weights, act, narrow, grad_two, total_two, keep, send, stacked, own, both
+    delta, from_even, from_odd, weights, act, narrow, grad_two, total_two, keep, send, stacked, own, both
 ):
+    place = position()
     lane = lanes((64, 128))
     upper = lax.rem(place[0], 2) == 1
     front = lane % 64 < 32
@@ -340,14 +352,14 @@
 
     both[:, 0:576] = grad_two[...]
     both[:, 576:1152] = kernel_grad(own, narrow, 0)
+    row = lax.broadcasted_iota(jnp.int32, (8, 64), 0)
     offsets = jnp.where(
-        lane == 0,
-        jnp.sum(total_two[...], axis=1, keepdims=True),
-        jnp.sum(total, axis=1, keepdims=True),
+        row == 0, jnp.sum(total_two[...].T, axis=0, keepdims=True), jnp.sum(total.T, axis=0, keepdims=True)
     )
     def block(index):
         rows = [both[24 * index + 8 * (u // 9) : 24 * index + 8 * (u // 9) + 8, tiles(u % 9)] for u in range(27)]
-        return jnp.concatenate(rows + [offsets[8 * index : 8 * index + 8]], axis=0)
+        last = jnp.concatenate([offsets[:, 8 * index : 8 * index + 8], jnp.zeros((8, 120), F32)], axis=1)
+        return jnp.concatenate(rows + [last], axis=0)
 
     first = place[2] == 0
     for group in range(4):
@@ -362,7 +374,7 @@
     return (parts[0] + parts[2]) + (parts[1] + parts[3])
 
 
-def finish_kernel(factor, first, second, third, fourth, kernel_two, kernel_one, offsets):
+def finish_kernel(factor, first, second, third, fourth, kernel_two, kernel_one, two, one):
     total = sum_of_four([first[...], second[...], third[...], fourth[...]]) * factor
     units = [total[8 * u : 8 * u + 8] for u in range(28)]
     for dy in range(3):
@@ -373,10 +385,12 @@
                 dz, dx = divmod(k, 3)
                 target = kernel_one if layer else kernel_two
                 target[dx * 9 + dy * 3 + dz] = value[:, 64 * half : 64 * half + 64]
-    offsets[...] = units[27]
-
-
-def features_kernel(place, *refs):
+    two[...] = units[27][0, 0:8]
+    one[...] = units[27][1, 0:8]
+
+
+def features_kernel(*refs):
+    place = position()
     pieces, other, out, turned = (refs[:4], refs[4:8], refs[8], refs[9])
     for k in range(4):
         group = lax.rem(place[4] + 4 - k, 4)
@@ -425,11 +439,7 @@
 
 def shards(volume, weight_one, bias_one, weight_two, bias_two, cotangent):
     factor = float(volume.shape[1] * 32 * volume.shape[2] * volume.shape[3]) ** (-0.5)
-    h, l, c = (lax.axis_index(name) for name in ("h", "l", "c"))
-    mirrored = h == 1
-    block = 2 * jnp.where(mirrored, 3 - l, l) + c
-    place = [lax.axis_index(SPACE), block, c, h, l]
-    place = jnp.stack(place).astype(jnp.int32)
+    c = lax.axis_index("c")
     even, odd = neighbours()
     near = SPACE + ("l",)
     swap = [(0, 1), (1, 0)]
@@ -445,20 +455,16 @@
         volume_kernel,
         [((4, 2, 88, 128), BF16)],
         [((8, 64, 128), BF16), ((1072, 128), F32), pltpu.SemaphoreType.DMA(())],
-        place,
         volume.reshape(8, 64, 128),
-        scalars=(0,),
-        far=(1,),
+        far=(0,),
     )
     pieces = spread([pieces[k] for k in range(4)])
     (field,) = call(
         unpack_kernel,
         [((11, 64, 128), BF16)],
         [],
-        place,
         *pieces,
         *cross(pieces),
-        scalars=(0,),
     )
     near_even = lax.ppermute(field, near, even)
     near_odd = lax.ppermute(field, near, odd)
@@ -473,14 +479,12 @@
             pltpu.SMEM((2, 8), F32),
             pltpu.SemaphoreType.DMA((5,)),
         ],
-        place,
         cotangent.reshape(8, 64, 128),
         jnp.transpose(weight_one, (2, 3, 4, 0, 1)).reshape(27, 8, 64),
         bias_one,
         jnp.transpose(weight_two, (2, 3, 4, 0, 1)).reshape(27, 8, 64),
         bias_two,
-        scalars=(0,),
-        far=(1, 2, 3, 4, 5),
+        far=(0, 1, 2, 3, 4),
         limit=FULL_LIMIT,
     )
     rest = spread(rest)
@@ -488,10 +492,8 @@
         weights_kernel,
         [((192, 1152), BF16), ((192, 576), BF16), ((2, 64, 128), F32), ((10, 64, 128), BF16)],
         [],
-        place,
         *rest,
         *cross(rest),
-        scalars=(0,),
     )
 
     act, wide, delta, feats, to_even, to_odd = call(
@@ -505,14 +507,12 @@
             ((5, 64, 128), BF16),
         ],
         [((10, 64, 128), F32)],
-        place,
         field,
         near_even,
         near_odd,
         cots,
         weights,
         bias,
-        scalars=(0,),
         flops=2 * 192 * 576 * 128 * 30,
     )
     from_even = lax.ppermute(to_even, near, even)
@@ -526,11 +526,11 @@
         wide,
         flops=2 * 192 * 576 * 1024,
     )
+    feats = spread([feats[k] for k in range(4)])
     keep, send = call(
         backward_kernel,
         [((4, 224, 128), BF16), ((4, 224, 128), BF16)],
         [((192, 1280), BF16), ((192, 1024), BF16), ((192, 1152), F32)],
-        place,
         delta,
         from_even,
         from_odd,
@@ -539,20 +539,23 @@
         narrow,
         grad_two,
         total_two,
-        scalars=(0,),
         flops=4 * 192 * 576 * 1024,
     )
 
+    send, feats = lax.optimization_barrier((send, feats))
     other = lax.ppermute(send, "c", swap)
     parts = [(keep[k].astype(F32) + other[k].astype(F32)).astype(BF16) for k in range(4)]
-    part = sum_of_four(spread(parts)).astype(BF16)
+    feats = feats + cross(feats)
+    parts = spread(parts)
+    parts, feats = lax.optimization_barrier((parts, feats))
+    part = sum_of_four(parts).astype(BF16)
     other = lax.ppermute(part, "h", swap)
     part = (part.astype(F32) + other.astype(F32)).astype(BF16)
     part = sum_of_four(spread([part] * 4, "y")).astype(BF16)
     parts = spread([part] * 4, "x")
-    kernel_two, kernel_one, offsets = call(
+    kernel_two, kernel_one, offset_two, offset_one = call(
         functools.partial(finish_kernel, factor),
-        [((27, 8, 64), F32), ((27, 8, 64), F32), ((8, 128), F32)],
+        [((27, 8, 64), F32), ((27, 8, 64), F32), ((8,), F32), ((8,), F32)],
         [],
         *parts,
     )
@@ -560,17 +563,13 @@
         jnp.transpose(k.reshape(3, 3, 3, 8, 64), (3, 4, 0, 1, 2)) for k in (kernel_one, kernel_two)
     )
 
-    feats = spread([feats[k] for k in range(4)])
     (features,) = call(
         features_kernel,
         [((8, 64, 128), BF16)],
         [((1024, 128), F32)],
-        place,
         *feats,
-        *cross(feats),
-        scalars=(0,),
-    )
-    return features.reshape(8, 2, 32, 128), kernel_one, offsets[:, 1], kernel_two, offsets[:, 0]
+    )
+    return features.reshape(8, 2, 32, 128), kernel_one, offset_one, kernel_two, offset_two
 
 
 def solution(mesh):

time: 95.5 us -> 90.1 us (0.943)
  Pallas kernels: 15.3 us -> 11.1 us
  waiting for transfers between devices: 22.2 us -> 24 us
  starting transfers between devices: 53.6 us -> 52 us
  local copies, waits for them, and re-layouts: 3.26 us -> 1.82 us
    ppermute x18, waiting for transfers between devices: 12.7 us -> 17.2 us  [spread(): lax.ppermute(pieces[k], axis, turns[k])]
    pallas_call x9, Pallas kernels: 15.3 us -> 11.1 us  [call(): pl.pallas_call(kernel, out_shape=outs, in_specs=[smem if k in scalars els...]
    ppermute x1, waiting for transfers between devices: 1.76 us -> 0.01 us  [shards(): from_odd = lax.ppermute(to_odd, near, odd)]
    ppermute x18, starting transfers between devices: 31 us -> 29.5 us  [spread(): lax.ppermute(pieces[k], axis, turns[k])]
    unnamed x8 -> x4, local copies, waits for them, and re-layouts: 2.45 us -> 1.79 us
  transfers between devices with their start and end apart: 36 -> 36, of which waited for: 16 -> 17; matrix products, arithmetic and copies ran while one was open for 0% -> 0% of each run, Pallas kernels for 7% -> 6%
where the time goes in v5:
time: 90.1 us; the launch traced here: 89.9 us
  starting transfers between devices  52 us (58%)
  waiting for transfers between devices  24 us (27%)
  Pallas kernels  11.1 us (12%)
  local copies, waits for them, and re-layouts  1.82 us (2%)
    ppermute x18, starting transfers between devices, spread(): lax.ppermute(pieces[k], axis, turns[k])  29.5 us
    ppermute x18, waiting for transfers between devices, spread(): lax.ppermute(pieces[k], axis, turns[k])  17.2 us
    pallas_call x9, Pallas kernels, call(): pl.pallas_call(kernel, out_shape=outs, in_specs=[smem if k in scalars els...  11.1 us
    ppermute x1, starting transfers between devices, shards(): from_odd = lax.ppermute(to_odd, near, odd)  10.2 us
    ppermute x1, starting transfers between devices, shards(): other = lax.ppermute(part, 'h', swap)  5.89 us
    ppermute x1, starting transfers between devices, shards(): near_odd = lax.ppermute(field, near, odd)  3.48 us
    ppermute x12, starting transfers between devices, cross(): return [lax.ppermute(piece, 'c', swap) for piece in pieces]  2.41 us
    ppermute x1, waiting for transfers between devices, shards(): other = lax.ppermute(part, 'h', swap)  2.28 us
  transfers between devices with their start and end apart: 36, of which 17 were waited for; matrix products, arithmetic and copies ran while one was open for 0% of the time, Pallas kernels for 6%

profile of v5, /device:TPU:8, one launch (start us, length us, event | category | flops | bytes accessed | tf_op | source)
XLA Modules:
  0.0 89.9 jit_solution(18258350082357438790)
XLA Ops:
  0.6 0.9 copy-done
  1.5 0.3 shard_map.101
  1.9 4.7 %collective-permute-start.2 = (bf16[2,88,128]{2,1,0:T(8,128)(2,1)S(1)}, bf16[2,88,128]{2,1,0:T(8,128)(2,1)S(1)}, u32[]{:S(2)}, u32[]{:S(2)}) collective-permute-start(bf16[2,88,128]{2,1,0:T(8,128)(2,1)S(1)} %get-tuple-element.89), channel_id=1, source_target_pairs={{0,6},{2,0},{4,2},{6,4},{1,7},{3,1},{5,3},{7,5},{8,14},{10,8},{12,... | collective-permute-start | bytes 135176 | tf_op jit(solution)/shard_map/ppermute | solution.py:449
  6.6 1.9 %shard_map.103 = (bf16[384,128]{1,0:T(8,128)(2,1)}, bf16[384,128]{1,0:T(8,128)(2,1)}, bf16[384,128]{1,0:T(8,128)(2,1)}, bf16[384,128]{1,0:T(8,128)(2,1)}) custom-call(bf16[8,64,128]{2,1,0:T(8,128)(2,1)} %bitcast.41, bf16[27,8,64]{2,1,0:T(8,128)(2,1)} %bitcast.42, f32[8]{0:T(128)} %bias_one.1, bf16[27,8,64]{2,1,0:T(8,128)(2,1)} %bitcast.43, f32[8]{0:T(128)} %bias_two.1), custom_call_target="tpu_custom_call" | custom-call | bytes 579648 | tf_op jit(solution)/shard_map/pallas_call | solution.py:415
  8.5 0.7 collective-permute-start.9
  9.2 2.8 %collective-permute-start = (bf16[2,88,128]{2,1,0:T(8,128)(2,1)S(1)}, bf16[2,88,128]{2,1,0:T(8,128)(2,1)S(1)}, u32[]{:S(2)}, u32[]{:S(2)}) collective-permute-start(bf16[2,88,128]{2,1,0:T(8,128)(2,1)S(1)} %get-tuple-element.91), channel_id=1, source_target_pairs={{0,2},{2,4},{4,6},{6,0},{1,3},{3,5},{5,7},{7,1},{8,10},{10,12},{12... | collective-permute-start | bytes 135176 | tf_op jit(solution)/shard_map/ppermute | solution.py:449
  12.1 0.5 collective-permute-start.6
  12.7 3.1 %collective-permute-done.refs_1_ = bf16[2,88,128]{2,1,0:T(8,128)(2,1)S(1)} collective-permute-done((bf16[2,88,128]{2,1,0:T(8,128)(2,1)S(1)}, bf16[2,88,128]{2,1,0:T(8,128)(2,1)S(1)}, u32[]{:S(2)}, u32[]{:S(2)}) %collective-permute-start) | collective-permute-done | bytes 45088 | tf_op jit(solution)/shard_map/ppermute | solution.py:449
  15.8 1.0 %collective-permute-start.10 = (bf16[384,128]{1,0:T(8,128)(2,1)}, bf16[384,128]{1,0:T(8,128)(2,1)S(1)}, u32[]{:S(2)}, u32[]{:S(2)}) collective-permute-start(bf16[384,128]{1,0:T(8,128)(2,1)} %get-tuple-element.47), channel_id=1, source_target_pairs={{0,4},{2,6},{4,0},{6,2},{1,5},{3,7},{5,1},{7,3},{8,12},{10,14},{12... | collective-permute-start | bytes 294920 | tf_op jit(solution)/shard_map/ppermute | solution.py:449
  16.8 1.7 %collective-permute-start.11 = (bf16[384,128]{1,0:T(8,128)(2,1)}, bf16[384,128]{1,0:T(8,128)(2,1)S(1)}, u32[]{:S(2)}, u32[]{:S(2)}) collective-permute-start(bf16[384,128]{1,0:T(8,128)(2,1)} %get-tuple-element.48), channel_id=1, source_target_pairs={{0,6},{2,0},{4,2},{6,4},{1,7},{3,1},{5,3},{7,5},{8,14},{10,8},{12,... | collective-permute-start | bytes 294920 | tf_op jit(solution)/shard_map/ppermute | solution.py:449
  18.6 3.5 %collective-permute-start.8 = (bf16[11,64,128]{2,1,0:T(8,128)(2,1)S(1)}, bf16[11,64,128]{2,1,0:T(8,128)(2,1)S(1)}, u32[]{:S(2)}, u32[]{:S(2)}) collective-permute-start(bf16[11,64,128]{2,1,0:T(8,128)(2,1)S(1)} %shard_map.102.own), channel_id=1, source_target_pairs={{8,16},{16,8},{10,18},{18,10},{12,20},{20,12},{14,22},{22,14},{24,... | collective-permute-start | bytes 540680 | tf_op jit(solution)/shard_map/ppermute | solution.py:470
  22.2 1.9 %collective-permute-done.10.refs_2_ = bf16[384,128]{1,0:T(8,128)(2,1)S(1)} collective-permute-done((bf16[384,128]{1,0:T(8,128)(2,1)}, bf16[384,128]{1,0:T(8,128)(2,1)S(1)}, u32[]{:S(2)}, u32[]{:S(2)}) %collective-permute-start.10) | collective-permute-done | bytes 98336 | tf_op jit(solution)/shard_map/ppermute | solution.py:449
  24.1 0.5 collective-permute-start.14
  24.8 0.5 collective-permute-done.13.refs_5_
  25.5 0.4 collective-permute-done.15.refs_7_
  25.9 0.9 copy-done.1
  26.8 0.6 shard_map.104
  27.4 1.4 %collective-permute-done.7.even = bf16[11,64,128]{2,1,0:T(8,128)(2,1)S(1)} collective-permute-done((bf16[11,64,128]{2,1,0:T(8,128)(2,1)S(1)}, bf16[11,64,128]{2,1,0:T(8,128)(2,1)S(1)}, u32[]{:S(2)}, u32[]{:S(2)}) %collective-permute-start.7) | collective-permute-done | bytes 180256 | tf_op jit(solution)/shard_map/ppermute | solution.py:469
  28.9 4.6 %shard_map.105 = (bf16[192,1536]{1,0:T(8,128)(2,1)S(1)}, bf16[192,2816]{1,0:T(8,128)(2,1)S(1)}, bf16[10,64,128]{2,1,0:T(8,128)(2,1)S(1)}, bf16[4,2,64,128]{3,2,1...) custom-call(bf16[11,64,128]{2,1,0:T(8,128)(2,1)S(1)} %shard_map.102.own, ...), custom_call_target="tpu_custom_call" | custom-call | flops 849346560 | bytes 3342336 | tf_op jit(solution)/shard_map/pallas_call | solution.py:415
  33.5 0.4 collective-permute-start.16
  33.8 10.2 %collective-permute-start.17 = (bf16[5,64,128]{2,1,0:T(8,128)(2,1)S(1)}, bf16[5,64,128]{2,1,0:T(8,128)(2,1)S(1)}, u32[]{:S(2)}, u32[]{:S(2)}) collective-permute-start(bf16[5,64,128]{2,1,0:T(8,128)(2,1)S(1)} %get-tuple-element.54), channel_id=1, source_target_pairs={{8,16},{16,8},{10,18},{18,10},{12,20},{20,12},{14,22},{22,14},{24,... | collective-permute-start | bytes 245768 | tf_op jit(solution)/shard_map/ppermute | solution.py:519
  44.1 1.8 %collective-permute-start.20 = (bf16[2,64,128]{2,1,0:T(8,128)(2,1)S(1)}, bf16[2,64,128]{2,1,0:T(8,128)(2,1)S(1)}, u32[]{:S(2)}, u32[]{:S(2)}) collective-permute-start(bf16[2,64,128]{2,1,0:T(8,128)(2,1)S(1)} %get-tuple-element.93), channel_id=1, source_target_pairs={{0,6},{2,0},{4,2},{6,4},{1,7},{3,1},{5,3},{7,5},{8,14},{10,8},{12,... | collective-permute-start | bytes 98312 | tf_op jit(solution)/shard_map/ppermute | solution.py:449
  45.9 0.7 collective-permute-start.18
  46.6 0.6 shard_map.106
  47.2 1.3 %shard_map.107 = (bf16[4,224,128]{2,1,0:T(8,128)(2,1)S(1)}, bf16[4,224,128]{2,1,0:T(8,128)(2,1)S(1)}) custom-call(bf16[10,64,128]{2,1,0:T(8,128)(2,1)S(1)} %get-tuple-element.52.delta, bf16[5,64,128]{2,1,0:T(8,128)(2,1)S(1)} %collective-permute-done.16.from_even, bf16[5,64,128]{2,1,0:T(8,128)(2,1)S(1)} %collective-permute-done.17.from_odd, ...), custom_call_target="tpu_custom_call" | custom-call | flops 452984832 | bytes 2564096 | tf_op jit(solution)/shard_map/pallas_call | solution.py:415
  48.5 2.3 %collective-permute-done.19.refs_2_ = bf16[2,64,128]{2,1,0:T(8,128)(2,1)S(1)} collective-permute-done((bf16[2,64,128]{2,1,0:T(8,128)(2,1)S(1)}, bf16[2,64,128]{2,1,0:T(8,128)(2,1)S(1)}, u32[]{:S(2)}, u32[]{:S(2)}) %collective-permute-start.19) | collective-permute-done | bytes 32800 | tf_op jit(solution)/shard_map/ppermute | solution.py:449
  50.8 0.8 collective-permute-done.18.refs_1_
  51.6 0.5 collective-permute-start.25
  52.1 1.0 %collective-permute-done.21 = bf16[4,224,128]{2,1,0:T(8,128)(2,1)S(1)} collective-permute-done((bf16[4,224,128]{2,1,0:T(8,128)(2,1)S(1)}, bf16[4,224,128]{2,1,0:T(8,128)(2,1)S(1)}, u32[]{:S(2)}, u32[]{:S(2)}) %collective-permute-start.21) | collective-permute-done | bytes 229408 | tf_op jit(solution)/shard_map/ppermute | solution.py:546
  53.2 0.9 %collective-permute-start.24 = (bf16[224,128]{1,0:T(8,128)(2,1)S(1)}, bf16[224,128]{1,0:T(8,128)(2,1)S(1)}, u32[]{:S(2)}, u32[]{:S(2)}) collective-permute-start(bf16[224,128]{1,0:T(8,128)(2,1)S(1)} %get-tuple-element.85), channel_id=1, source_target_pairs={{0,6},{2,0},{4,2},{6,4},{1,7},{3,1},{5,3},{7,5},{8,14},{10,8},{12,... | collective-permute-start | bytes 172040 | tf_op jit(solution)/shard_map/ppermute | solution.py:449
  54.1 0.4 collective-permute-start.23
  54.6 1.8 %collective-permute-start.22 = (bf16[224,128]{1,0:T(8,128)(2,1)S(1)}, bf16[224,128]{1,0:T(8,128)(2,1)S(1)}, u32[]{:S(2)}, u32[]{:S(2)}) collective-permute-start(bf16[224,128]{1,0:T(8,128)(2,1)S(1)} %get-tuple-element.87), channel_id=1, source_target_pairs={{0,2},{2,4},{4,6},{6,0},{1,3},{3,5},{5,7},{7,1},{8,10},{10,12},{12... | collective-permute-start | bytes 172040 | tf_op jit(solution)/shard_map/ppermute | solution.py:449
  56.4 0.5 collective-permute-start.28
  56.9 0.7 collective-permute-done.27.refs_6_
  57.6 0.3 collective-permute-done.28.refs_7_
  57.9 3.2 %collective-permute-done.23 = bf16[224,128]{1,0:T(8,128)(2,1)S(1)} collective-permute-done((bf16[224,128]{1,0:T(8,128)(2,1)S(1)}, bf16[224,128]{1,0:T(8,128)(2,1)S(1)}, u32[]{:S(2)}, u32[]{:S(2)}) %collective-permute-start.23) | collective-permute-done | bytes 57376 | tf_op jit(solution)/shard_map/ppermute | solution.py:449
  61.2 5.9 %collective-permute-start.29 = (bf16[224,128]{1,0:T(8,128)(2,1)S(1)}, bf16[224,128]{1,0:T(8,128)(2,1)S(1)}, u32[]{:S(2)}, u32[]{:S(2)}) collective-permute-start(bf16[224,128]{1,0:T(8,128)(2,1)S(1)} %add_convert_fusion.2), channel_id=1, source_target_pairs={{0,32},{32,0},{1,33},{33,1},{2,34},{34,2},{3,35},{35,3},{4,36},{36... | collective-permute-start | bytes 172040 | tf_op jit(solution)/shard_map/ppermute | solution.py:552
  67.1 2.3 %collective-permute-done.29 = bf16[224,128]{1,0:T(8,128)(2,1)S(1)} collective-permute-done((bf16[224,128]{1,0:T(8,128)(2,1)S(1)}, bf16[224,128]{1,0:T(8,128)(2,1)S(1)}, u32[]{:S(2)}, u32[]{:S(2)}) %collective-permute-start.29) | collective-permute-done | bytes 57376 | tf_op jit(solution)/shard_map/ppermute | solution.py:552
  69.5 2.0 %collective-permute-start.31 = (bf16[224,128]{1,0:T(8,128)(2,1)S(1)}, bf16[224,128]{1,0:T(8,128)(2,1)S(1)}, u32[]{:S(2)}, u32[]{:S(2)}) collective-permute-start(bf16[224,128]{1,0:T(8,128)(2,1)S(1)} %add_convert_fusion.1), channel_id=1, source_target_pairs={{0,8},{8,16},{16,24},{24,0},{1,9},{9,17},{17,25},{25,1},{2,10},{10... | collective-permute-start | bytes 172040 | tf_op jit(solution)/shard_map/ppermute | solution.py:449
  71.5 4.1 %collective-permute-start.30 = (bf16[224,128]{1,0:T(8,128)(2,1)S(1)}, bf16[224,128]{1,0:T(8,128)(2,1)S(1)}, u32[]{:S(2)}, u32[]{:S(2)}) collective-permute-start(bf16[224,128]{1,0:T(8,128)(2,1)S(1)} %add_convert_fusion.1), channel_id=1, source_target_pairs={{0,16},{8,24},{16,0},{24,8},{1,17},{9,25},{17,1},{25,9},{2,18},{10... | collective-permute-start | bytes 172040 | tf_op jit(solution)/shard_map/ppermute | solution.py:449
  75.7 2.1 %collective-permute-done.30 = bf16[224,128]{1,0:T(8,128)(2,1)S(1)} collective-permute-done((bf16[224,128]{1,0:T(8,128)(2,1)S(1)}, bf16[224,128]{1,0:T(8,128)(2,1)S(1)}, u32[]{:S(2)}, u32[]{:S(2)}) %collective-permute-start.30) | collective-permute-done | bytes 57376 | tf_op jit(solution)/shard_map/ppermute | solution.py:449
  77.8 5.0 %collective-permute-start.35 = (bf16[224,128]{1,0:T(8,128)(2,1)S(1)}, bf16[224,128]{1,0:T(8,128)(2,1)S(1)}, u32[]{:S(2)}, u32[]{:S(2)}) collective-permute-start(bf16[224,128]{1,0:T(8,128)(2,1)S(1)} %add_convert_fusion.first), channel_id=1, source_target_pairs={{0,192},{64,0},{128,64},{192,128},{1,193},{65,1},{129,65},{193,129... | collective-permute-start | bytes 172040 | tf_op jit(solution)/shard_map/ppermute | solution.py:449
  82.8 0.8 collective-permute-start.34
  83.6 0.9 collective-permute-start.33
  84.5 0.9 shard_map.108
  85.4 3.1 %collective-permute-done.34.third = bf16[224,128]{1,0:T(8,128)(2,1)S(1)} collective-permute-done((bf16[224,128]{1,0:T(8,128)(2,1)S(1)}, bf16[224,128]{1,0:T(8,128)(2,1)S(1)}, u32[]{:S(2)}, u32[]{:S(2)}) %collective-permute-start.34) | collective-permute-done | bytes 57376 | tf_op jit(solution)/shard_map/ppermute | solution.py:449
  88.5 0.6 collective-permute-done.33.second
  89.1 0.8 shard_map.109
  (43 shorter events, 1.2 us)
Async XLA Ops:
  0.6 0.9 %copy-start = (bf16[8,2,32,128]{3,2,1,0:T(8,128)(2,1)S(1)}, bf16[8,2,32,128]{3,2,1,0:T(8,128)(2,1)}, u32[]{:S(2)}) copy-start(bf16[8,2,32,128]{3,2,1,0:T(8,128)(2,1)} %param.6) | copy-start | bytes 393220
  1.9 10.2 %collective-permute-start.2 = (bf16[2,88,128]{2,1,0:T(8,128)(2,1)S(1)}, bf16[2,88,128]{2,1,0:T(8,128)(2,1)S(1)}, u32[]{:S(2)}, u32[]{:S(2)}) collective-permute-start(bf16[2,88,128]{2,1,0:T(8,128)(2,1)S(1)} %get-tuple-element.89), channel_id=1, source_target_pairs={{0,6},{2,0},{4,2},{6,4},{1,7},{3,1},{5,3},{7,5},{8,14},{10,8},{12,... | collective-permute-start | bytes 135176 | tf_op jit(solution)/shard_map/ppermute | solution.py:449
  6.6 6.0 %collective-permute-start.1 = (bf16[2,88,128]{2,1,0:T(8,128)(2,1)S(1)}, bf16[2,88,128]{2,1,0:T(8,128)(2,1)S(1)}, u32[]{:S(2)}, u32[]{:S(2)}) collective-permute-start(bf16[2,88,128]{2,1,0:T(8,128)(2,1)S(1)} %get-tuple-element.90), channel_id=1, source_target_pairs={{0,4},{2,6},{4,0},{6,2},{1,5},{3,7},{5,1},{7,3},{8,12},{10,14},{12... | collective-permute-start | bytes 135176 | tf_op jit(solution)/shard_map/ppermute | solution.py:449
  8.5 13.6 %collective-permute-start.9 = (bf16[384,128]{1,0:T(8,128)(2,1)}, bf16[384,128]{1,0:T(8,128)(2,1)S(1)}, u32[]{:S(2)}, u32[]{:S(2)}) collective-permute-start(bf16[384,128]{1,0:T(8,128)(2,1)} %get-tuple-element.46), channel_id=1, source_target_pairs={{0,2},{2,4},{4,6},{6,0},{1,3},{3,5},{5,7},{7,1},{8,10},{10,12},{12... | collective-permute-start | bytes 294920 | tf_op jit(solution)/shard_map/ppermute | solution.py:449
  9.2 6.6 %collective-permute-start = (bf16[2,88,128]{2,1,0:T(8,128)(2,1)S(1)}, bf16[2,88,128]{2,1,0:T(8,128)(2,1)S(1)}, u32[]{:S(2)}, u32[]{:S(2)}) collective-permute-start(bf16[2,88,128]{2,1,0:T(8,128)(2,1)S(1)} %get-tuple-element.91), channel_id=1, source_target_pairs={{0,2},{2,4},{4,6},{6,0},{1,3},{3,5},{5,7},{7,1},{8,10},{10,12},{12... | collective-permute-start | bytes 135176 | tf_op jit(solution)/shard_map/ppermute | solution.py:449
  12.0 3.7 %collective-permute-start.3 = (bf16[2,88,128]{2,1,0:T(8,128)(2,1)S(1)}, bf16[2,88,128]{2,1,0:T(8,128)(2,1)S(1)}, u32[]{:S(2)}, u32[]{:S(2)}) collective-permute-start(bf16[2,88,128]{2,1,0:T(8,128)(2,1)S(1)} %get-tuple-element.92.refs_0_), channel_id=1, source_target_pairs={{0,1},{1,0},{2,3},{3,2},{4,5},{5,4},{6,7},{7,6},{8,9},{9,8},{10,11... | collective-permute-start | bytes 135176 | tf_op jit(solution)/shard_map/ppermute | solution.py:452
  12.1 4.8 %collective-permute-start.6 = (bf16[2,88,128]{2,1,0:T(8,128)(2,1)S(1)}, bf16[2,88,128]{2,1,0:T(8,128)(2,1)S(1)}, u32[]{:S(2)}, u32[]{:S(2)}) collective-permute-start(bf16[2,88,128]{2,1,0:T(8,128)(2,1)S(1)} %collective-permute-done.2.refs_3_), channel_id=1, source_target_pairs={{0,1},{1,0},{2,3},{3,2},{4,5},{5,4},{6,7},{7,6},{8,9},{9,8},{10,11... | collective-permute-start | bytes 135176 | tf_op jit(solution)/shard_map/ppermute | solution.py:452
  12.6 5.9 %collective-permute-start.5 = (bf16[2,88,128]{2,1,0:T(8,128)(2,1)S(1)}, bf16[2,88,128]{2,1,0:T(8,128)(2,1)S(1)}, u32[]{:S(2)}, u32[]{:S(2)}) collective-permute-start(bf16[2,88,128]{2,1,0:T(8,128)(2,1)S(1)} %collective-permute-done.1.refs_2_), channel_id=1, source_target_pairs={{0,1},{1,0},{2,3},{3,2},{4,5},{5,4},{6,7},{7,6},{8,9},{9,8},{10,11... | collective-permute-start | bytes 135176 | tf_op jit(solution)/shard_map/ppermute | solution.py:452
  15.8 2.7 %collective-permute-start.4 = (bf16[2,88,128]{2,1,0:T(8,128)(2,1)S(1)}, bf16[2,88,128]{2,1,0:T(8,128)(2,1)S(1)}, u32[]{:S(2)}, u32[]{:S(2)}) collective-permute-start(bf16[2,88,128]{2,1,0:T(8,128)(2,1)S(1)} %collective-permute-done.refs_1_), channel_id=1, source_target_pairs={{0,1},{1,0},{2,3},{3,2},{4,5},{5,4},{6,7},{7,6},{8,9},{9,8},{10,11... | collective-permute-start | bytes 135176 | tf_op jit(solution)/shard_map/ppermute | solution.py:452
  15.8 8.3 %collective-permute-start.10 = (bf16[384,128]{1,0:T(8,128)(2,1)}, bf16[384,128]{1,0:T(8,128)(2,1)S(1)}, u32[]{:S(2)}, u32[]{:S(2)}) collective-permute-start(bf16[384,128]{1,0:T(8,128)(2,1)} %get-tuple-element.47), channel_id=1, source_target_pairs={{0,4},{2,6},{4,0},{6,2},{1,5},{3,7},{5,1},{7,3},{8,12},{10,14},{12... | collective-permute-start | bytes 294920 | tf_op jit(solution)/shard_map/ppermute | solution.py:449
  16.8 7.3 %collective-permute-start.11 = (bf16[384,128]{1,0:T(8,128)(2,1)}, bf16[384,128]{1,0:T(8,128)(2,1)S(1)}, u32[]{:S(2)}, u32[]{:S(2)}) collective-permute-start(bf16[384,128]{1,0:T(8,128)(2,1)} %get-tuple-element.48), channel_id=1, source_target_pairs={{0,6},{2,0},{4,2},{6,4},{1,7},{3,1},{5,3},{7,5},{8,14},{10,8},{12,... | collective-permute-start | bytes 294920 | tf_op jit(solution)/shard_map/ppermute | solution.py:449
  18.5 6.1 %collective-permute-start.12 = (bf16[384,128]{1,0:T(8,128)(2,1)}, bf16[384,128]{1,0:T(8,128)(2,1)S(1)}, u32[]{:S(2)}, u32[]{:S(2)}) collective-permute-start(bf16[384,128]{1,0:T(8,128)(2,1)} %get-tuple-element.45.refs_0_), channel_id=1, source_target_pairs={{0,1},{1,0},{2,3},{3,2},{4,5},{5,4},{6,7},{7,6},{8,9},{9,8},{10,11... | collective-permute-start | bytes 294920 | tf_op jit(solution)/shard_map/ppermute | solution.py:452
  18.6 8.9 %collective-permute-start.8 = (bf16[11,64,128]{2,1,0:T(8,128)(2,1)S(1)}, bf16[11,64,128]{2,1,0:T(8,128)(2,1)S(1)}, u32[]{:S(2)}, u32[]{:S(2)}) collective-permute-start(bf16[11,64,128]{2,1,0:T(8,128)(2,1)S(1)} %shard_map.102.own), channel_id=1, source_target_pairs={{8,16},{16,8},{10,18},{18,10},{12,20},{20,12},{14,22},{22,14},{24,... | collective-permute-start | bytes 540680 | tf_op jit(solution)/shard_map/ppermute | solution.py:470
  22.1 6.8 %collective-permute-start.7 = (bf16[11,64,128]{2,1,0:T(8,128)(2,1)S(1)}, bf16[11,64,128]{2,1,0:T(8,128)(2,1)S(1)}, u32[]{:S(2)}, u32[]{:S(2)}) collective-permute-start(bf16[11,64,128]{2,1,0:T(8,128)(2,1)S(1)} %shard_map.102.own), channel_id=1, source_target_pairs={{0,8},{8,0},{2,10},{10,2},{4,12},{12,4},{6,14},{14,6},{16,24},{24,... | collective-permute-start | bytes 540680 | tf_op jit(solution)/shard_map/ppermute | solution.py:469
  24.0 1.3 %collective-permute-start.13 = (bf16[384,128]{1,0:T(8,128)(2,1)S(1)}, bf16[384,128]{1,0:T(8,128)(2,1)S(1)}, u32[]{:S(2)}, u32[]{:S(2)}) collective-permute-start(bf16[384,128]{1,0:T(8,128)(2,1)S(1)} %collective-permute-done.9.refs_1_), channel_id=1, source_target_pairs={{0,1},{1,0},{2,3},{3,2},{4,5},{5,4},{6,7},{7,6},{8,9},{9,8},{10,11... | collective-permute-start | bytes 294920 | tf_op jit(solution)/shard_map/ppermute | solution.py:452
  24.1 1.4 %collective-permute-start.14 = (bf16[384,128]{1,0:T(8,128)(2,1)S(1)}, bf16[384,128]{1,0:T(8,128)(2,1)S(1)}, u32[]{:S(2)}, u32[]{:S(2)}) collective-permute-start(bf16[384,128]{1,0:T(8,128)(2,1)S(1)} %collective-permute-done.10.refs_2_), channel_id=1, source_target_pairs={{0,1},{1,0},{2,3},{3,2},{4,5},{5,4},{6,7},{7,6},{8,9},{9,8},{10,11... | collective-permute-start | bytes 294920 | tf_op jit(solution)/shard_map/ppermute | solution.py:452
  24.6 1.3 %collective-permute-start.15 = (bf16[384,128]{1,0:T(8,128)(2,1)S(1)}, bf16[384,128]{1,0:T(8,128)(2,1)S(1)}, u32[]{:S(2)}, u32[]{:S(2)}) collective-permute-start(bf16[384,128]{1,0:T(8,128)(2,1)S(1)} %collective-permute-done.11.refs_3_), channel_id=1, source_target_pairs={{0,1},{1,0},{2,3},{3,2},{4,5},{5,4},{6,7},{7,6},{8,9},{9,8},{10,11... | collective-permute-start | bytes 294920 | tf_op jit(solution)/shard_map/ppermute | solution.py:452
  25.9 0.9 copy-start.1
  33.5 13.7 %collective-permute-start.16 = (bf16[5,64,128]{2,1,0:T(8,128)(2,1)S(1)}, bf16[5,64,128]{2,1,0:T(8,128)(2,1)S(1)}, u32[]{:S(2)}, u32[]{:S(2)}) collective-permute-start(bf16[5,64,128]{2,1,0:T(8,128)(2,1)S(1)} %get-tuple-element.53), channel_id=1, source_target_pairs={{0,8},{8,0},{2,10},{10,2},{4,12},{12,4},{6,14},{14,6},{16,24},{24,... | collective-permute-start | bytes 245768 | tf_op jit(solution)/shard_map/ppermute | solution.py:518
  33.8 13.3 %collective-permute-start.17 = (bf16[5,64,128]{2,1,0:T(8,128)(2,1)S(1)}, bf16[5,64,128]{2,1,0:T(8,128)(2,1)S(1)}, u32[]{:S(2)}, u32[]{:S(2)}) collective-permute-start(bf16[5,64,128]{2,1,0:T(8,128)(2,1)S(1)} %get-tuple-element.54), channel_id=1, source_target_pairs={{8,16},{16,8},{10,18},{18,10},{12,20},{20,12},{14,22},{22,14},{24,... | collective-permute-start | bytes 245768 | tf_op jit(solution)/shard_map/ppermute | solution.py:519
  44.1 4.4 %collective-permute-start.20 = (bf16[2,64,128]{2,1,0:T(8,128)(2,1)S(1)}, bf16[2,64,128]{2,1,0:T(8,128)(2,1)S(1)}, u32[]{:S(2)}, u32[]{:S(2)}) collective-permute-start(bf16[2,64,128]{2,1,0:T(8,128)(2,1)S(1)} %get-tuple-element.93), channel_id=1, source_target_pairs={{0,6},{2,0},{4,2},{6,4},{1,7},{3,1},{5,3},{7,5},{8,14},{10,8},{12,... | collective-permute-start | bytes 98312 | tf_op jit(solution)/shard_map/ppermute | solution.py:449
  45.9 4.9 %collective-permute-start.19 = (bf16[2,64,128]{2,1,0:T(8,128)(2,1)S(1)}, bf16[2,64,128]{2,1,0:T(8,128)(2,1)S(1)}, u32[]{:S(2)}, u32[]{:S(2)}) collective-permute-start(bf16[2,64,128]{2,1,0:T(8,128)(2,1)S(1)} %get-tuple-element.94), channel_id=1, source_target_pairs={{0,4},{2,6},{4,0},{6,2},{1,5},{3,7},{5,1},{7,3},{8,12},{10,14},{12... | collective-permute-start | bytes 98312 | tf_op jit(solution)/shard_map/ppermute | solution.py:449
  45.9 5.7 %collective-permute-start.18 = (bf16[2,64,128]{2,1,0:T(8,128)(2,1)S(1)}, bf16[2,64,128]{2,1,0:T(8,128)(2,1)S(1)}, u32[]{:S(2)}, u32[]{:S(2)}) collective-permute-start(bf16[2,64,128]{2,1,0:T(8,128)(2,1)S(1)} %get-tuple-element.95), channel_id=1, source_target_pairs={{0,2},{2,4},{4,6},{6,0},{1,3},{3,5},{5,7},{7,1},{8,10},{10,12},{12... | collective-permute-start | bytes 98312 | tf_op jit(solution)/shard_map/ppermute | solution.py:449
  51.6 1.5 %collective-permute-start.21 = (bf16[4,224,128]{2,1,0:T(8,128)(2,1)S(1)}, bf16[4,224,128]{2,1,0:T(8,128)(2,1)S(1)}, u32[]{:S(2)}, u32[]{:S(2)}) collective-permute-start(bf16[4,224,128]{2,1,0:T(8,128)(2,1)S(1)} %get-tuple-element.64), channel_id=1, source_target_pairs={{0,1},{1,0},{2,3},{3,2},{4,5},{5,4},{6,7},{7,6},{8,9},{9,8},{10,11... | collective-permute-start | bytes 688136 | tf_op jit(solution)/shard_map/ppermute | solution.py:546
  51.6 4.8 %collective-permute-start.25 = (bf16[2,64,128]{2,1,0:T(8,128)(2,1)S(1)}, bf16[2,64,128]{2,1,0:T(8,128)(2,1)S(1)}, u32[]{:S(2)}, u32[]{:S(2)}) collective-permute-start(bf16[2,64,128]{2,1,0:T(8,128)(2,1)S(1)} %get-tuple-element.69.refs_0_), channel_id=1, source_target_pairs={{0,1},{1,0},{2,3},{3,2},{4,5},{5,4},{6,7},{7,6},{8,9},{9,8},{10,11... | collective-permute-start | bytes 98312 | tf_op jit(solution)/shard_map/ppermute | solution.py:452
  52.1 4.3 %collective-permute-start.26 = (bf16[2,64,128]{2,1,0:T(8,128)(2,1)S(1)}, bf16[2,64,128]{2,1,0:T(8,128)(2,1)S(1)}, u32[]{:S(2)}, u32[]{:S(2)}) collective-permute-start(bf16[2,64,128]{2,1,0:T(8,128)(2,1)S(1)} %collective-permute-done.18.refs_1_), channel_id=1, source_target_pairs={{0,1},{1,0},{2,3},{3,2},{4,5},{5,4},{6,7},{7,6},{8,9},{9,8},{10,11... | collective-permute-start | bytes 98312 | tf_op jit(solution)/shard_map/ppermute | solution.py:452
  53.2 4.8 %collective-permute-start.24 = (bf16[224,128]{1,0:T(8,128)(2,1)S(1)}, bf16[224,128]{1,0:T(8,128)(2,1)S(1)}, u32[]{:S(2)}, u32[]{:S(2)}) collective-permute-start(bf16[224,128]{1,0:T(8,128)(2,1)S(1)} %get-tuple-element.85), channel_id=1, source_target_pairs={{0,6},{2,0},{4,2},{6,4},{1,7},{3,1},{5,3},{7,5},{8,14},{10,8},{12,... | collective-permute-start | bytes 172040 | tf_op jit(solution)/shard_map/ppermute | solution.py:449
  54.1 7.0 %collective-permute-start.23 = (bf16[224,128]{1,0:T(8,128)(2,1)S(1)}, bf16[224,128]{1,0:T(8,128)(2,1)S(1)}, u32[]{:S(2)}, u32[]{:S(2)}) collective-permute-start(bf16[224,128]{1,0:T(8,128)(2,1)S(1)} %get-tuple-element.86), channel_id=1, source_target_pairs={{0,4},{2,6},{4,0},{6,2},{1,5},{3,7},{5,1},{7,3},{8,12},{10,14},{12... | collective-permute-start | bytes 172040 | tf_op jit(solution)/shard_map/ppermute | solution.py:449
  54.6 6.6 %collective-permute-start.22 = (bf16[224,128]{1,0:T(8,128)(2,1)S(1)}, bf16[224,128]{1,0:T(8,128)(2,1)S(1)}, u32[]{:S(2)}, u32[]{:S(2)}) collective-permute-start(bf16[224,128]{1,0:T(8,128)(2,1)S(1)} %get-tuple-element.87), channel_id=1, source_target_pairs={{0,2},{2,4},{4,6},{6,0},{1,3},{3,5},{5,7},{7,1},{8,10},{10,12},{12... | collective-permute-start | bytes 172040 | tf_op jit(solution)/shard_map/ppermute | solution.py:449
  56.4 1.2 %collective-permute-start.27 = (bf16[2,64,128]{2,1,0:T(8,128)(2,1)S(1)}, bf16[2,64,128]{2,1,0:T(8,128)(2,1)S(1)}, u32[]{:S(2)}, u32[]{:S(2)}) collective-permute-start(bf16[2,64,128]{2,1,0:T(8,128)(2,1)S(1)} %collective-permute-done.19.refs_2_), channel_id=1, source_target_pairs={{0,1},{1,0},{2,3},{3,2},{4,5},{5,4},{6,7},{7,6},{8,9},{9,8},{10,11... | collective-permute-start | bytes 98312 | tf_op jit(solution)/shard_map/ppermute | solution.py:452
  56.4 1.5 %collective-permute-start.28 = (bf16[2,64,128]{2,1,0:T(8,128)(2,1)S(1)}, bf16[2,64,128]{2,1,0:T(8,128)(2,1)S(1)}, u32[]{:S(2)}, u32[]{:S(2)}) collective-permute-start(bf16[2,64,128]{2,1,0:T(8,128)(2,1)S(1)} %collective-permute-done.20.refs_3_), channel_id=1, source_target_pairs={{0,1},{1,0},{2,3},{3,2},{4,5},{5,4},{6,7},{7,6},{8,9},{9,8},{10,11... | collective-permute-start | bytes 98312 | tf_op jit(solution)/shard_map/ppermute | solution.py:452
  61.2 8.2 %collective-permute-start.29 = (bf16[224,128]{1,0:T(8,128)(2,1)S(1)}, bf16[224,128]{1,0:T(8,128)(2,1)S(1)}, u32[]{:S(2)}, u32[]{:S(2)}) collective-permute-start(bf16[224,128]{1,0:T(8,128)(2,1)S(1)} %add_convert_fusion.2), channel_id=1, source_target_pairs={{0,32},{32,0},{1,33},{33,1},{2,34},{34,2},{3,35},{35,3},{4,36},{36... | collective-permute-start | bytes 172040 | tf_op jit(solution)/shard_map/ppermute | solution.py:552
  69.4 6.2 %collective-permute-start.32 = (bf16[224,128]{1,0:T(8,128)(2,1)S(1)}, bf16[224,128]{1,0:T(8,128)(2,1)S(1)}, u32[]{:S(2)}, u32[]{:S(2)}) collective-permute-start(bf16[224,128]{1,0:T(8,128)(2,1)S(1)} %add_convert_fusion.1), channel_id=1, source_target_pairs={{0,24},{8,0},{16,8},{24,16},{1,25},{9,1},{17,9},{25,17},{2,26},{10... | collective-permute-start | bytes 172040 | tf_op jit(solution)/shard_map/ppermute | solution.py:449
  69.5 6.2 %collective-permute-start.31 = (bf16[224,128]{1,0:T(8,128)(2,1)S(1)}, bf16[224,128]{1,0:T(8,128)(2,1)S(1)}, u32[]{:S(2)}, u32[]{:S(2)}) collective-permute-start(bf16[224,128]{1,0:T(8,128)(2,1)S(1)} %add_convert_fusion.1), channel_id=1, source_target_pairs={{0,8},{8,16},{16,24},{24,0},{1,9},{9,17},{17,25},{25,1},{2,10},{10... | collective-permute-start | bytes 172040 | tf_op jit(solution)/shard_map/ppermute | solution.py:449
  71.5 6.3 %collective-permute-start.30 = (bf16[224,128]{1,0:T(8,128)(2,1)S(1)}, bf16[224,128]{1,0:T(8,128)(2,1)S(1)}, u32[]{:S(2)}, u32[]{:S(2)}) collective-permute-start(bf16[224,128]{1,0:T(8,128)(2,1)S(1)} %add_convert_fusion.1), channel_id=1, source_target_pairs={{0,16},{8,24},{16,0},{24,8},{1,17},{9,25},{17,1},{25,9},{2,18},{10... | collective-permute-start | bytes 172040 | tf_op jit(solution)/shard_map/ppermute | solution.py:449
  77.8 7.6 %collective-permute-start.35 = (bf16[224,128]{1,0:T(8,128)(2,1)S(1)}, bf16[224,128]{1,0:T(8,128)(2,1)S(1)}, u32[]{:S(2)}, u32[]{:S(2)}) collective-permute-start(bf16[224,128]{1,0:T(8,128)(2,1)S(1)} %add_convert_fusion.first), channel_id=1, source_target_pairs={{0,192},{64,0},{128,64},{192,128},{1,193},{65,1},{129,65},{193,129... | collective-permute-start | bytes 172040 | tf_op jit(solution)/shard_map/ppermute | solution.py:449
  82.8 5.7 %collective-permute-start.34 = (bf16[224,128]{1,0:T(8,128)(2,1)S(1)}, bf16[224,128]{1,0:T(8,128)(2,1)S(1)}, u32[]{:S(2)}, u32[]{:S(2)}) collective-permute-start(bf16[224,128]{1,0:T(8,128)(2,1)S(1)} %add_convert_fusion.first), channel_id=1, source_target_pairs={{0,128},{64,192},{128,0},{192,64},{1,129},{65,193},{129,1},{193,65... | collective-permute-start | bytes 172040 | tf_op jit(solution)/shard_map/ppermute | solution.py:449
  83.6 5.5 %collective-permute-start.33 = (bf16[224,128]{1,0:T(8,128)(2,1)S(1)}, bf16[224,128]{1,0:T(8,128)(2,1)S(1)}, u32[]{:S(2)}, u32[]{:S(2)}) collective-permute-start(bf16[224,128]{1,0:T(8,128)(2,1)S(1)} %add_convert_fusion.first), channel_id=1, source_target_pairs={{0,64},{64,128},{128,192},{192,0},{1,65},{65,129},{129,193},{193,1... | collective-permute-start | bytes 172040 | tf_op jit(solution)/shard_map/ppermute | solution.py:449

commit v6 on v5

--- a/solution.py
+++ b/solution.py
@@ -410,8 +410,10 @@
     smem = pl.BlockSpec(memory_space=pltpu.SMEM)
     anywhere = pl.BlockSpec(memory_space=pltpu.HBM)
     outs = [jax.ShapeDtypeStruct(shape, dtype) for shape, dtype in out_shapes]
-    size = sum(a.size * a.dtype.itemsize for a in args)
-    size += sum(o.size * o.dtype.itemsize for o in outs)
+    size = 0
+    if flops:
+        size = sum(a.size * a.dtype.itemsize for a in args)
+        size += sum(o.size * o.dtype.itemsize for o in outs)
     return pl.pallas_call(
         kernel,
         out_shape=outs,
@@ -459,16 +461,6 @@
         far=(0,),
     )
     pieces = spread([pieces[k] for k in range(4)])
-    (field,) = call(
-        unpack_kernel,
-        [((11, 64, 128), BF16)],
-        [],
-        *pieces,
-        *cross(pieces),
-    )
-    near_even = lax.ppermute(field, near, even)
-    near_odd = lax.ppermute(field, near, odd)
-
     rest = call(
         rest_kernel,
         [((384, 128), BF16)] * 4,
@@ -487,6 +479,17 @@
         far=(0, 1, 2, 3, 4),
         limit=FULL_LIMIT,
     )
+    rest, pieces = lax.optimization_barrier((rest, pieces))
+    (field,) = call(
+        unpack_kernel,
+        [((11, 64, 128), BF16)],
+        [],
+        *pieces,
+        *cross(pieces),
+    )
+    near_even = lax.ppermute(field, near, even)
+    near_odd = lax.ppermute(field, near, odd)
+
     rest = spread(rest)
     weights, weights_back, bias, cots = call(
         weights_kernel,
@@ -542,14 +545,12 @@
         flops=4 * 192 * 576 * 1024,
     )
 
-    send, feats = lax.optimization_barrier((send, feats))
     other = lax.ppermute(send, "c", swap)
     parts = [(keep[k].astype(F32) + other[k].astype(F32)).astype(BF16) for k in range(4)]
     feats = feats + cross(feats)
-    parts = spread(parts)
-    parts, feats = lax.optimization_barrier((parts, feats))
-    part = sum_of_four(parts).astype(BF16)
+    part = sum_of_four(spread(parts)).astype(BF16)
     other = lax.ppermute(part, "h", swap)
+    other, feats = lax.optimization_barrier((other, feats))
     part = (part.astype(F32) + other.astype(F32)).astype(BF16)
     part = sum_of_four(spread([part] * 4, "y")).astype(BF16)
     parts = spread([part] * 4, "x")

time: 90.1 us -> 89.9 us (level)
  waiting for transfers between devices: 24 us -> 20.5 us
  starting transfers between devices: 52 us -> 54.8 us
    ppermute x18, waiting for transfers between devices: 17.2 us -> 13.4 us  [spread(): lax.ppermute(pieces[k], axis, turns[k])]
    ppermute x1, waiting for transfers between devices: 2.28 us -> 0.11 us  [shards(): other = lax.ppermute(part, 'h', swap)]
    ppermute x18, starting transfers between devices: 29.5 us -> 31.6 us  [spread(): lax.ppermute(pieces[k], axis, turns[k])]
    ppermute x1, waiting for transfers between devices: 0.01 us -> 1.79 us  [shards(): from_odd = lax.ppermute(to_odd, near, odd)]
  transfers between devices with their start and end apart: 36 -> 36, of which waited for: 17 -> 21; matrix products, arithmetic and copies ran while one was open for 0% -> 0% of each run, Pallas kernels for 6% -> 5%
where the time goes in v6:
time: 89.9 us; the launch traced here: 89.2 us
  starting transfers between devices  54.8 us (61%)
  waiting for transfers between devices  20.5 us (23%)
  Pallas kernels  11.1 us (12%)
  local copies, waits for them, and re-layouts  1.82 us (2%)
    ppermute x18, starting transfers between devices, spread(): lax.ppermute(pieces[k], axis, turns[k])  31.6 us
    ppermute x18, waiting for transfers between devices, spread(): lax.ppermute(pieces[k], axis, turns[k])  13.4 us
    pallas_call x9, Pallas kernels, call(): pl.pallas_call(kernel, out_shape=outs, in_specs=[smem if k in scalars els...  11.1 us
    ppermute x1, starting transfers between devices, shards(): from_odd = lax.ppermute(to_odd, near, odd)  10.2 us
    ppermute x1, starting transfers between devices, shards(): other = lax.ppermute(part, 'h', swap)  6.06 us
    ppermute x1, starting transfers between devices, shards(): near_odd = lax.ppermute(field, near, odd)  3.48 us
    ppermute x12, starting transfers between devices, cross(): return [lax.ppermute(piece, 'c', swap) for piece in pieces]  2.83 us
    ppermute x12, waiting for transfers between devices, cross(): return [lax.ppermute(piece, 'c', swap) for piece in pieces]  2.25 us
  transfers between devices with their start and end apart: 36, of which 21 were waited for; matrix products, arithmetic and copies ran while one was open for 0% of the time, Pallas kernels for 5%

profile of v6, /device:TPU:8, one launch (start us, length us, event | category | flops | bytes accessed | tf_op | source)
XLA Modules:
  0.0 89.2 jit_solution(14434667189415571484)
XLA Ops:
  0.6 0.9 %copy-done = bf16[8,2,32,128]{3,2,1,0:T(8,128)(2,1)S(1)} copy-done((bf16[8,2,32,128]{3,2,1,0:T(8,128)(2,1)S(1)}, bf16[8,2,32,128]{3,2,1,0:T(8,128)(2,1)}, u32[]{:S(2)}) %copy-start) | copy-done | bytes 131096
  1.5 0.3 shard_map.102
  1.9 4.7 %collective-permute-start.2 = (bf16[2,88,128]{2,1,0:T(8,128)(2,1)S(1)}, bf16[2,88,128]{2,1,0:T(8,128)(2,1)S(1)}, u32[]{:S(2)}, u32[]{:S(2)}) collective-permute-start(bf16[2,88,128]{2,1,0:T(8,128)(2,1)S(1)} %get-tuple-element.88), channel_id=1, source_target_pairs={{0,6},{2,0},{4,2},{6,4},{1,7},{3,1},{5,3},{7,5},{8,14},{10,8},{12,... | collective-permute-start | bytes 135176 | tf_op jit(solution)/shard_map/ppermute | solution.py:451
  6.6 0.7 collective-permute-start
  7.3 1.9 %shard_map.101 = (bf16[384,128]{1,0:T(8,128)(2,1)}, bf16[384,128]{1,0:T(8,128)(2,1)}, bf16[384,128]{1,0:T(8,128)(2,1)}, bf16[384,128]{1,0:T(8,128)(2,1)}) custom-call(bf16[8,64,128]{2,1,0:T(8,128)(2,1)} %bitcast.44, bf16[27,8,64]{2,1,0:T(8,128)(2,1)} %bitcast.45, f32[8]{0:T(128)} %bias_one.1, bf16[27,8,64]{2,1,0:T(8,128)(2,1)} %bitcast.46, f32[8]{0:T(128)} %bias_two.1), custom_call_target="tpu_custom_call" | custom-call | tf_op jit(solution)/shard_map/pallas_call | solution.py:417
  9.2 2.4 %collective-permute-done.1.refs_2_ = bf16[2,88,128]{2,1,0:T(8,128)(2,1)S(1)} collective-permute-done((bf16[2,88,128]{2,1,0:T(8,128)(2,1)S(1)}, bf16[2,88,128]{2,1,0:T(8,128)(2,1)S(1)}, u32[]{:S(2)}, u32[]{:S(2)}) %collective-permute-start.1) | collective-permute-done | bytes 45088 | tf_op jit(solution)/shard_map/ppermute | solution.py:451
  11.5 0.9 %collective-permute-done.refs_1_ = bf16[2,88,128]{2,1,0:T(8,128)(2,1)S(1)} collective-permute-done((bf16[2,88,128]{2,1,0:T(8,128)(2,1)S(1)}, bf16[2,88,128]{2,1,0:T(8,128)(2,1)S(1)}, u32[]{:S(2)}, u32[]{:S(2)}) %collective-permute-start) | collective-permute-done | bytes 45088 | tf_op jit(solution)/shard_map/ppermute | solution.py:451
  12.4 0.5 collective-permute-start.4
  13.0 0.5 collective-permute-start.6
  13.7 1.5 %collective-permute-start.10 = (bf16[384,128]{1,0:T(8,128)(2,1)}, bf16[384,128]{1,0:T(8,128)(2,1)S(1)}, u32[]{:S(2)}, u32[]{:S(2)}) collective-permute-start(bf16[384,128]{1,0:T(8,128)(2,1)} %get-tuple-element.55), channel_id=1, source_target_pairs={{0,4},{2,6},{4,0},{6,2},{1,5},{3,7},{5,1},{7,3},{8,12},{10,14},{12... | collective-permute-start | bytes 294920 | tf_op jit(solution)/shard_map/ppermute | solution.py:451
  15.2 2.6 %collective-permute-start.11 = (bf16[384,128]{1,0:T(8,128)(2,1)}, bf16[384,128]{1,0:T(8,128)(2,1)S(1)}, u32[]{:S(2)}, u32[]{:S(2)}) collective-permute-start(bf16[384,128]{1,0:T(8,128)(2,1)} %get-tuple-element.56), channel_id=1, source_target_pairs={{0,6},{2,0},{4,2},{6,4},{1,7},{3,1},{5,3},{7,5},{8,14},{10,8},{12,... | collective-permute-start | bytes 294920 | tf_op jit(solution)/shard_map/ppermute | solution.py:451
  17.8 3.5 %collective-permute-start.8 = (bf16[11,64,128]{2,1,0:T(8,128)(2,1)S(1)}, bf16[11,64,128]{2,1,0:T(8,128)(2,1)S(1)}, u32[]{:S(2)}, u32[]{:S(2)}) collective-permute-start(bf16[11,64,128]{2,1,0:T(8,128)(2,1)S(1)} %shard_map.103.own), channel_id=1, source_target_pairs={{8,16},{16,8},{10,18},{18,10},{12,20},{20,12},{14,22},{22,14},{24,... | collective-permute-start | bytes 540680 | tf_op jit(solution)/shard_map/ppermute | solution.py:491
  21.4 1.9 %collective-permute-done.10.refs_2_ = bf16[384,128]{1,0:T(8,128)(2,1)S(1)} collective-permute-done((bf16[384,128]{1,0:T(8,128)(2,1)}, bf16[384,128]{1,0:T(8,128)(2,1)S(1)}, u32[]{:S(2)}, u32[]{:S(2)}) %collective-permute-start.10) | collective-permute-done | bytes 98336 | tf_op jit(solution)/shard_map/ppermute | solution.py:451
  23.4 0.5 collective-permute-start.14
  24.1 0.5 collective-permute-done.13.refs_5_
  24.8 0.4 collective-permute-done.15.refs_7_
  25.2 0.9 copy-done.1
  26.1 0.6 shard_map.104
  26.7 1.4 %collective-permute-done.7.even = bf16[11,64,128]{2,1,0:T(8,128)(2,1)S(1)} collective-permute-done((bf16[11,64,128]{2,1,0:T(8,128)(2,1)S(1)}, bf16[11,64,128]{2,1,0:T(8,128)(2,1)S(1)}, u32[]{:S(2)}, u32[]{:S(2)}) %collective-permute-start.7) | collective-permute-done | bytes 180256 | tf_op jit(solution)/shard_map/ppermute | solution.py:490
  28.1 4.6 %shard_map.105 = (bf16[192,1536]{1,0:T(8,128)(2,1)S(1)}, bf16[192,2816]{1,0:T(8,128)(2,1)S(1)}, bf16[10,64,128]{2,1,0:T(8,128)(2,1)S(1)}, bf16[4,2,64,128]{3,2,1...) custom-call(bf16[11,64,128]{2,1,0:T(8,128)(2,1)S(1)} %shard_map.103.own, ...), custom_call_target="tpu_custom_call" | custom-call | flops 849346560 | bytes 3342336 | tf_op jit(solution)/shard_map/pallas_call | solution.py:417
  32.7 0.4 collective-permute-start.16
  33.1 10.2 %collective-permute-start.17 = (bf16[5,64,128]{2,1,0:T(8,128)(2,1)S(1)}, bf16[5,64,128]{2,1,0:T(8,128)(2,1)S(1)}, u32[]{:S(2)}, u32[]{:S(2)}) collective-permute-start(bf16[5,64,128]{2,1,0:T(8,128)(2,1)S(1)} %get-tuple-element.62), channel_id=1, source_target_pairs={{8,16},{16,8},{10,18},{18,10},{12,20},{20,12},{14,22},{22,14},{24,... | collective-permute-start | bytes 245768 | tf_op jit(solution)/shard_map/ppermute | solution.py:522
  43.3 0.6 shard_map.106
  44.0 1.8 %collective-permute-done.17.from_odd = bf16[5,64,128]{2,1,0:T(8,128)(2,1)S(1)} collective-permute-done((bf16[5,64,128]{2,1,0:T(8,128)(2,1)S(1)}, bf16[5,64,128]{2,1,0:T(8,128)(2,1)S(1)}, u32[]{:S(2)}, u32[]{:S(2)}) %collective-permute-start.17) | collective-permute-done | bytes 81952 | tf_op jit(solution)/shard_map/ppermute | solution.py:522
  45.7 1.3 %shard_map.107 = (bf16[4,224,128]{2,1,0:T(8,128)(2,1)S(1)}, bf16[4,224,128]{2,1,0:T(8,128)(2,1)S(1)}) custom-call(bf16[10,64,128]{2,1,0:T(8,128)(2,1)S(1)} %get-tuple-element.60.delta, bf16[5,64,128]{2,1,0:T(8,128)(2,1)S(1)} %collective-permute-done.16.from_even, bf16[5,64,128]{2,1,0:T(8,128)(2,1)S(1)} %collective-permute-done.17.from_odd, ...), custom_call_target="tpu_custom_call" | custom-call | flops 452984832 | bytes 2564096 | tf_op jit(solution)/shard_map/pallas_call | solution.py:417
  47.2 1.5 %collective-permute-done.18 = bf16[4,224,128]{2,1,0:T(8,128)(2,1)S(1)} collective-permute-done((bf16[4,224,128]{2,1,0:T(8,128)(2,1)S(1)}, bf16[4,224,128]{2,1,0:T(8,128)(2,1)S(1)}, u32[]{:S(2)}, u32[]{:S(2)}) %collective-permute-start.18) | collective-permute-done | bytes 229408 | tf_op jit(solution)/shard_map/ppermute | solution.py:548
  48.8 1.1 %collective-permute-start.21 = (bf16[224,128]{1,0:T(8,128)(2,1)S(1)}, bf16[224,128]{1,0:T(8,128)(2,1)S(1)}, u32[]{:S(2)}, u32[]{:S(2)}) collective-permute-start(bf16[224,128]{1,0:T(8,128)(2,1)S(1)} %get-tuple-element.86), channel_id=1, source_target_pairs={{0,6},{2,0},{4,2},{6,4},{1,7},{3,1},{5,3},{7,5},{8,14},{10,8},{12,... | collective-permute-start | bytes 172040 | tf_op jit(solution)/shard_map/ppermute | solution.py:451
  49.9 1.0 %collective-permute-start.20 = (bf16[224,128]{1,0:T(8,128)(2,1)S(1)}, bf16[224,128]{1,0:T(8,128)(2,1)S(1)}, u32[]{:S(2)}, u32[]{:S(2)}) collective-permute-start(bf16[224,128]{1,0:T(8,128)(2,1)S(1)} %get-tuple-element.87), channel_id=1, source_target_pairs={{0,2},{2,4},{4,6},{6,0},{1,3},{3,5},{5,7},{7,1},{8,10},{10,12},{12... | collective-permute-start | bytes 172040 | tf_op jit(solution)/shard_map/ppermute | solution.py:451
  50.9 2.9 %collective-permute-start.25 = (bf16[2,64,128]{2,1,0:T(8,128)(2,1)S(1)}, bf16[2,64,128]{2,1,0:T(8,128)(2,1)S(1)}, u32[]{:S(2)}, u32[]{:S(2)}) collective-permute-start(bf16[2,64,128]{2,1,0:T(8,128)(2,1)S(1)} %get-tuple-element.92), channel_id=1, source_target_pairs={{0,6},{2,0},{4,2},{6,4},{1,7},{3,1},{5,3},{7,5},{8,14},{10,8},{12,... | collective-permute-start | bytes 98312 | tf_op jit(solution)/shard_map/ppermute | solution.py:451
  53.9 1.1 %collective-permute-done.19 = bf16[224,128]{1,0:T(8,128)(2,1)S(1)} collective-permute-done((bf16[224,128]{1,0:T(8,128)(2,1)S(1)}, bf16[224,128]{1,0:T(8,128)(2,1)S(1)}, u32[]{:S(2)}, u32[]{:S(2)}) %collective-permute-start.19) | collective-permute-done | bytes 57376 | tf_op jit(solution)/shard_map/ppermute | solution.py:451
  55.1 0.8 collective-permute-start.23
  55.9 1.0 %collective-permute-done.20 = bf16[224,128]{1,0:T(8,128)(2,1)S(1)} collective-permute-done((bf16[224,128]{1,0:T(8,128)(2,1)S(1)}, bf16[224,128]{1,0:T(8,128)(2,1)S(1)}, u32[]{:S(2)}, u32[]{:S(2)}) %collective-permute-start.20) | collective-permute-done | bytes 57376 | tf_op jit(solution)/shard_map/ppermute | solution.py:451
  56.9 6.1 %collective-permute-start.22 = (bf16[224,128]{1,0:T(8,128)(2,1)S(1)}, bf16[224,128]{1,0:T(8,128)(2,1)S(1)}, u32[]{:S(2)}, u32[]{:S(2)}) collective-permute-start(bf16[224,128]{1,0:T(8,128)(2,1)S(1)} %fusion.1), channel_id=1, source_target_pairs={{0,32},{32,0},{1,33},{33,1},{2,34},{34,2},{3,35},{35,3},{4,36},{36... | collective-permute-start | bytes 172040 | tf_op jit(solution)/shard_map/ppermute | solution.py:552
  63.0 0.5 collective-permute-start.29
  63.5 0.3 collective-permute-start.28
  64.3 0.4 collective-permute-done.28.refs_6_
  64.7 0.3 collective-permute-done.27.refs_5_
  65.2 3.0 %collective-permute-start.32 = (bf16[224,128]{1,0:T(8,128)(2,1)S(1)}, bf16[224,128]{1,0:T(8,128)(2,1)S(1)}, u32[]{:S(2)}, u32[]{:S(2)}) collective-permute-start(bf16[224,128]{1,0:T(8,128)(2,1)S(1)} %add_convert_fusion.1), channel_id=1, source_target_pairs={{0,24},{8,0},{16,8},{24,16},{1,25},{9,1},{17,9},{25,17},{2,26},{10... | collective-permute-start | bytes 172040 | tf_op jit(solution)/shard_map/ppermute | solution.py:451
  68.2 6.9 %collective-permute-start.30 = (bf16[224,128]{1,0:T(8,128)(2,1)S(1)}, bf16[224,128]{1,0:T(8,128)(2,1)S(1)}, u32[]{:S(2)}, u32[]{:S(2)}) collective-permute-start(bf16[224,128]{1,0:T(8,128)(2,1)S(1)} %add_convert_fusion.1), channel_id=1, source_target_pairs={{0,16},{8,24},{16,0},{24,8},{1,17},{9,25},{17,1},{25,9},{2,18},{10... | collective-permute-start | bytes 172040 | tf_op jit(solution)/shard_map/ppermute | solution.py:451
  75.1 0.4 collective-permute-done.31
  75.5 1.7 %collective-permute-done.30 = bf16[224,128]{1,0:T(8,128)(2,1)S(1)} collective-permute-done((bf16[224,128]{1,0:T(8,128)(2,1)S(1)}, bf16[224,128]{1,0:T(8,128)(2,1)S(1)}, u32[]{:S(2)}, u32[]{:S(2)}) %collective-permute-start.30) | collective-permute-done | bytes 57376 | tf_op jit(solution)/shard_map/ppermute | solution.py:451
  77.2 4.9 %collective-permute-start.35 = (bf16[224,128]{1,0:T(8,128)(2,1)S(1)}, bf16[224,128]{1,0:T(8,128)(2,1)S(1)}, u32[]{:S(2)}, u32[]{:S(2)}) collective-permute-start(bf16[224,128]{1,0:T(8,128)(2,1)S(1)} %add_convert_fusion.first), channel_id=1, source_target_pairs={{0,192},{64,0},{128,64},{192,128},{1,193},{65,1},{129,65},{193,129... | collective-permute-start | bytes 172040 | tf_op jit(solution)/shard_map/ppermute | solution.py:451
  82.1 0.5 collective-permute-start.34
  82.6 0.9 %collective-permute-start.33 = (bf16[224,128]{1,0:T(8,128)(2,1)S(1)}, bf16[224,128]{1,0:T(8,128)(2,1)S(1)}, u32[]{:S(2)}, u32[]{:S(2)}) collective-permute-start(bf16[224,128]{1,0:T(8,128)(2,1)S(1)} %add_convert_fusion.first), channel_id=1, source_target_pairs={{0,64},{64,128},{128,192},{192,0},{1,65},{65,129},{129,193},{193,1... | collective-permute-start | bytes 172040 | tf_op jit(solution)/shard_map/ppermute | solution.py:451
  83.5 0.9 %shard_map.108 = bf16[8,64,128]{2,1,0:T(8,128)(2,1)} custom-call(bf16[2,64,128]{2,1,0:T(8,128)(2,1)S(1)} %get-tuple-element.72.refs_0_, bf16[2,64,128]{2,1,0:T(8,128)(2,1)S(1)} %collective-permute-done.23.refs_1_, bf16[2,64,128]{2,1,0:T(8,128)(2,1)S(1)} %collective-permute-done.24.refs_2_, bf16[2,64,128]{2,1,0:T(8,128)(2,1)S(1)} %collective-permute-done.25.refs_3_, ...), custom_call_target="tpu_custom_call" | custom-call | tf_op jit(solution)/shard_map/pallas_call | solution.py:417
  84.4 3.4 %collective-permute-done.34.third = bf16[224,128]{1,0:T(8,128)(2,1)S(1)} collective-permute-done((bf16[224,128]{1,0:T(8,128)(2,1)S(1)}, bf16[224,128]{1,0:T(8,128)(2,1)S(1)}, u32[]{:S(2)}, u32[]{:S(2)}) %collective-permute-start.34) | collective-permute-done | bytes 57376 | tf_op jit(solution)/shard_map/ppermute | solution.py:451
  87.8 0.6 collective-permute-done.33.second
  88.4 0.8 shard_map.109
  (43 shorter events, 2.0 us)
Async XLA Ops:
  0.6 0.9 %copy-start = (bf16[8,2,32,128]{3,2,1,0:T(8,128)(2,1)S(1)}, bf16[8,2,32,128]{3,2,1,0:T(8,128)(2,1)}, u32[]{:S(2)}) copy-start(bf16[8,2,32,128]{3,2,1,0:T(8,128)(2,1)} %param.6) | copy-start | bytes 393220
  1.9 7.3 %collective-permute-start.2 = (bf16[2,88,128]{2,1,0:T(8,128)(2,1)S(1)}, bf16[2,88,128]{2,1,0:T(8,128)(2,1)S(1)}, u32[]{:S(2)}, u32[]{:S(2)}) collective-permute-start(bf16[2,88,128]{2,1,0:T(8,128)(2,1)S(1)} %get-tuple-element.88), channel_id=1, source_target_pairs={{0,6},{2,0},{4,2},{6,4},{1,7},{3,1},{5,3},{7,5},{8,14},{10,8},{12,... | collective-permute-start | bytes 135176 | tf_op jit(solution)/shard_map/ppermute | solution.py:451
  6.6 4.9 %collective-permute-start.1 = (bf16[2,88,128]{2,1,0:T(8,128)(2,1)S(1)}, bf16[2,88,128]{2,1,0:T(8,128)(2,1)S(1)}, u32[]{:S(2)}, u32[]{:S(2)}) collective-permute-start(bf16[2,88,128]{2,1,0:T(8,128)(2,1)S(1)} %get-tuple-element.89), channel_id=1, source_target_pairs={{0,4},{2,6},{4,0},{6,2},{1,5},{3,7},{5,1},{7,3},{8,12},{10,14},{12... | collective-permute-start | bytes 135176 | tf_op jit(solution)/shard_map/ppermute | solution.py:451
  6.6 5.8 %collective-permute-start = (bf16[2,88,128]{2,1,0:T(8,128)(2,1)S(1)}, bf16[2,88,128]{2,1,0:T(8,128)(2,1)S(1)}, u32[]{:S(2)}, u32[]{:S(2)}) collective-permute-start(bf16[2,88,128]{2,1,0:T(8,128)(2,1)S(1)} %get-tuple-element.90), channel_id=1, source_target_pairs={{0,2},{2,4},{4,6},{6,0},{1,3},{3,5},{5,7},{7,1},{8,10},{10,12},{12... | collective-permute-start | bytes 135176 | tf_op jit(solution)/shard_map/ppermute | solution.py:451
  12.4 8.9 %collective-permute-start.9 = (bf16[384,128]{1,0:T(8,128)(2,1)}, bf16[384,128]{1,0:T(8,128)(2,1)S(1)}, u32[]{:S(2)}, u32[]{:S(2)}) collective-permute-start(bf16[384,128]{1,0:T(8,128)(2,1)} %get-tuple-element.54), channel_id=1, source_target_pairs={{0,2},{2,4},{4,6},{6,0},{1,3},{3,5},{5,7},{7,1},{8,10},{10,12},{12... | collective-permute-start | bytes 294920 | tf_op jit(solution)/shard_map/ppermute | solution.py:451
  12.4 1.2 %collective-permute-start.3 = (bf16[2,88,128]{2,1,0:T(8,128)(2,1)S(1)}, bf16[2,88,128]{2,1,0:T(8,128)(2,1)S(1)}, u32[]{:S(2)}, u32[]{:S(2)}) collective-permute-start(bf16[2,88,128]{2,1,0:T(8,128)(2,1)S(1)} %get-tuple-element.49.refs_0_), channel_id=1, source_target_pairs={{0,1},{1,0},{2,3},{3,2},{4,5},{5,4},{6,7},{7,6},{8,9},{9,8},{10,11... | collective-permute-start | bytes 135176 | tf_op jit(solution)/shard_map/ppermute | solution.py:454
  12.4 2.7 %collective-permute-start.4 = (bf16[2,88,128]{2,1,0:T(8,128)(2,1)S(1)}, bf16[2,88,128]{2,1,0:T(8,128)(2,1)S(1)}, u32[]{:S(2)}, u32[]{:S(2)}) collective-permute-start(bf16[2,88,128]{2,1,0:T(8,128)(2,1)S(1)} %collective-permute-done.refs_1_), channel_id=1, source_target_pairs={{0,1},{1,0},{2,3},{3,2},{4,5},{5,4},{6,7},{7,6},{8,9},{9,8},{10,11... | collective-permute-start | bytes 135176 | tf_op jit(solution)/shard_map/ppermute | solution.py:454
  13.0 4.8 %collective-permute-start.5 = (bf16[2,88,128]{2,1,0:T(8,128)(2,1)S(1)}, bf16[2,88,128]{2,1,0:T(8,128)(2,1)S(1)}, u32[]{:S(2)}, u32[]{:S(2)}) collective-permute-start(bf16[2,88,128]{2,1,0:T(8,128)(2,1)S(1)} %collective-permute-done.1.refs_2_), channel_id=1, source_target_pairs={{0,1},{1,0},{2,3},{3,2},{4,5},{5,4},{6,7},{7,6},{8,9},{9,8},{10,11... | collective-permute-start | bytes 135176 | tf_op jit(solution)/shard_map/ppermute | solution.py:454
  13.0 4.8 %collective-permute-start.6 = (bf16[2,88,128]{2,1,0:T(8,128)(2,1)S(1)}, bf16[2,88,128]{2,1,0:T(8,128)(2,1)S(1)}, u32[]{:S(2)}, u32[]{:S(2)}) collective-permute-start(bf16[2,88,128]{2,1,0:T(8,128)(2,1)S(1)} %collective-permute-done.2.refs_3_), channel_id=1, source_target_pairs={{0,1},{1,0},{2,3},{3,2},{4,5},{5,4},{6,7},{7,6},{8,9},{9,8},{10,11... | collective-permute-start | bytes 135176 | tf_op jit(solution)/shard_map/ppermute | solution.py:454
  13.7 9.7 %collective-permute-start.10 = (bf16[384,128]{1,0:T(8,128)(2,1)}, bf16[384,128]{1,0:T(8,128)(2,1)S(1)}, u32[]{:S(2)}, u32[]{:S(2)}) collective-permute-start(bf16[384,128]{1,0:T(8,128)(2,1)} %get-tuple-element.55), channel_id=1, source_target_pairs={{0,4},{2,6},{4,0},{6,2},{1,5},{3,7},{5,1},{7,3},{8,12},{10,14},{12... | collective-permute-start | bytes 294920 | tf_op jit(solution)/shard_map/ppermute | solution.py:451
  15.2 8.2 %collective-permute-start.11 = (bf16[384,128]{1,0:T(8,128)(2,1)}, bf16[384,128]{1,0:T(8,128)(2,1)S(1)}, u32[]{:S(2)}, u32[]{:S(2)}) collective-permute-start(bf16[384,128]{1,0:T(8,128)(2,1)} %get-tuple-element.56), channel_id=1, source_target_pairs={{0,6},{2,0},{4,2},{6,4},{1,7},{3,1},{5,3},{7,5},{8,14},{10,8},{12,... | collective-permute-start | bytes 294920 | tf_op jit(solution)/shard_map/ppermute | solution.py:451
  17.7 6.1 %collective-permute-start.12 = (bf16[384,128]{1,0:T(8,128)(2,1)}, bf16[384,128]{1,0:T(8,128)(2,1)S(1)}, u32[]{:S(2)}, u32[]{:S(2)}) collective-permute-start(bf16[384,128]{1,0:T(8,128)(2,1)} %get-tuple-element.53.refs_0_), channel_id=1, source_target_pairs={{0,1},{1,0},{2,3},{3,2},{4,5},{5,4},{6,7},{7,6},{8,9},{9,8},{10,11... | collective-permute-start | bytes 294920 | tf_op jit(solution)/shard_map/ppermute | solution.py:454
  17.8 8.9 %collective-permute-start.8 = (bf16[11,64,128]{2,1,0:T(8,128)(2,1)S(1)}, bf16[11,64,128]{2,1,0:T(8,128)(2,1)S(1)}, u32[]{:S(2)}, u32[]{:S(2)}) collective-permute-start(bf16[11,64,128]{2,1,0:T(8,128)(2,1)S(1)} %shard_map.103.own), channel_id=1, source_target_pairs={{8,16},{16,8},{10,18},{18,10},{12,20},{20,12},{14,22},{22,14},{24,... | collective-permute-start | bytes 540680 | tf_op jit(solution)/shard_map/ppermute | solution.py:491
  21.3 6.8 %collective-permute-start.7 = (bf16[11,64,128]{2,1,0:T(8,128)(2,1)S(1)}, bf16[11,64,128]{2,1,0:T(8,128)(2,1)S(1)}, u32[]{:S(2)}, u32[]{:S(2)}) collective-permute-start(bf16[11,64,128]{2,1,0:T(8,128)(2,1)S(1)} %shard_map.103.own), channel_id=1, source_target_pairs={{0,8},{8,0},{2,10},{10,2},{4,12},{12,4},{6,14},{14,6},{16,24},{24,... | collective-permute-start | bytes 540680 | tf_op jit(solution)/shard_map/ppermute | solution.py:490
  23.3 1.3 %collective-permute-start.13 = (bf16[384,128]{1,0:T(8,128)(2,1)S(1)}, bf16[384,128]{1,0:T(8,128)(2,1)S(1)}, u32[]{:S(2)}, u32[]{:S(2)}) collective-permute-start(bf16[384,128]{1,0:T(8,128)(2,1)S(1)} %collective-permute-done.9.refs_1_), channel_id=1, source_target_pairs={{0,1},{1,0},{2,3},{3,2},{4,5},{5,4},{6,7},{7,6},{8,9},{9,8},{10,11... | collective-permute-start | bytes 294920 | tf_op jit(solution)/shard_map/ppermute | solution.py:454
  23.4 1.5 %collective-permute-start.14 = (bf16[384,128]{1,0:T(8,128)(2,1)S(1)}, bf16[384,128]{1,0:T(8,128)(2,1)S(1)}, u32[]{:S(2)}, u32[]{:S(2)}) collective-permute-start(bf16[384,128]{1,0:T(8,128)(2,1)S(1)} %collective-permute-done.10.refs_2_), channel_id=1, source_target_pairs={{0,1},{1,0},{2,3},{3,2},{4,5},{5,4},{6,7},{7,6},{8,9},{9,8},{10,11... | collective-permute-start | bytes 294920 | tf_op jit(solution)/shard_map/ppermute | solution.py:454
  23.9 1.3 %collective-permute-start.15 = (bf16[384,128]{1,0:T(8,128)(2,1)S(1)}, bf16[384,128]{1,0:T(8,128)(2,1)S(1)}, u32[]{:S(2)}, u32[]{:S(2)}) collective-permute-start(bf16[384,128]{1,0:T(8,128)(2,1)S(1)} %collective-permute-done.11.refs_3_), channel_id=1, source_target_pairs={{0,1},{1,0},{2,3},{3,2},{4,5},{5,4},{6,7},{7,6},{8,9},{9,8},{10,11... | collective-permute-start | bytes 294920 | tf_op jit(solution)/shard_map/ppermute | solution.py:454
  25.2 0.9 %copy-start.1 = (bf16[384,128]{1,0:T(8,128)(2,1)S(1)}, bf16[384,128]{1,0:T(8,128)(2,1)}, u32[]{:S(2)}) copy-start(bf16[384,128]{1,0:T(8,128)(2,1)} %get-tuple-element.53.refs_0_) | copy-start | bytes 294916
  32.7 11.2 %collective-permute-start.16 = (bf16[5,64,128]{2,1,0:T(8,128)(2,1)S(1)}, bf16[5,64,128]{2,1,0:T(8,128)(2,1)S(1)}, u32[]{:S(2)}, u32[]{:S(2)}) collective-permute-start(bf16[5,64,128]{2,1,0:T(8,128)(2,1)S(1)} %get-tuple-element.61), channel_id=1, source_target_pairs={{0,8},{8,0},{2,10},{10,2},{4,12},{12,4},{6,14},{14,6},{16,24},{24,... | collective-permute-start | bytes 245768 | tf_op jit(solution)/shard_map/ppermute | solution.py:521
  33.1 12.7 %collective-permute-start.17 = (bf16[5,64,128]{2,1,0:T(8,128)(2,1)S(1)}, bf16[5,64,128]{2,1,0:T(8,128)(2,1)S(1)}, u32[]{:S(2)}, u32[]{:S(2)}) collective-permute-start(bf16[5,64,128]{2,1,0:T(8,128)(2,1)S(1)} %get-tuple-element.62), channel_id=1, source_target_pairs={{8,16},{16,8},{10,18},{18,10},{12,20},{20,12},{14,22},{22,14},{24,... | collective-permute-start | bytes 245768 | tf_op jit(solution)/shard_map/ppermute | solution.py:522
  47.1 1.6 %collective-permute-start.18 = (bf16[4,224,128]{2,1,0:T(8,128)(2,1)S(1)}, bf16[4,224,128]{2,1,0:T(8,128)(2,1)S(1)}, u32[]{:S(2)}, u32[]{:S(2)}) collective-permute-start(bf16[4,224,128]{2,1,0:T(8,128)(2,1)S(1)} %get-tuple-element.70), channel_id=1, source_target_pairs={{0,1},{1,0},{2,3},{3,2},{4,5},{5,4},{6,7},{7,6},{8,9},{9,8},{10,11... | collective-permute-start | bytes 688136 | tf_op jit(solution)/shard_map/ppermute | solution.py:548
  48.7 6.4 %collective-permute-start.19 = (bf16[224,128]{1,0:T(8,128)(2,1)S(1)}, bf16[224,128]{1,0:T(8,128)(2,1)S(1)}, u32[]{:S(2)}, u32[]{:S(2)}) collective-permute-start(bf16[224,128]{1,0:T(8,128)(2,1)S(1)} %get-tuple-element.85), channel_id=1, source_target_pairs={{0,4},{2,6},{4,0},{6,2},{1,5},{3,7},{5,1},{7,3},{8,12},{10,14},{12... | collective-permute-start | bytes 172040 | tf_op jit(solution)/shard_map/ppermute | solution.py:451
  48.8 7.1 %collective-permute-start.21 = (bf16[224,128]{1,0:T(8,128)(2,1)S(1)}, bf16[224,128]{1,0:T(8,128)(2,1)S(1)}, u32[]{:S(2)}, u32[]{:S(2)}) collective-permute-start(bf16[224,128]{1,0:T(8,128)(2,1)S(1)} %get-tuple-element.86), channel_id=1, source_target_pairs={{0,6},{2,0},{4,2},{6,4},{1,7},{3,1},{5,3},{7,5},{8,14},{10,8},{12,... | collective-permute-start | bytes 172040 | tf_op jit(solution)/shard_map/ppermute | solution.py:451
  49.9 7.0 %collective-permute-start.20 = (bf16[224,128]{1,0:T(8,128)(2,1)S(1)}, bf16[224,128]{1,0:T(8,128)(2,1)S(1)}, u32[]{:S(2)}, u32[]{:S(2)}) collective-permute-start(bf16[224,128]{1,0:T(8,128)(2,1)S(1)} %get-tuple-element.87), channel_id=1, source_target_pairs={{0,2},{2,4},{4,6},{6,0},{1,3},{3,5},{5,7},{7,1},{8,10},{10,12},{12... | collective-permute-start | bytes 172040 | tf_op jit(solution)/shard_map/ppermute | solution.py:451
  50.9 12.1 %collective-permute-start.25 = (bf16[2,64,128]{2,1,0:T(8,128)(2,1)S(1)}, bf16[2,64,128]{2,1,0:T(8,128)(2,1)S(1)}, u32[]{:S(2)}, u32[]{:S(2)}) collective-permute-start(bf16[2,64,128]{2,1,0:T(8,128)(2,1)S(1)} %get-tuple-element.92), channel_id=1, source_target_pairs={{0,6},{2,0},{4,2},{6,4},{1,7},{3,1},{5,3},{7,5},{8,14},{10,8},{12,... | collective-permute-start | bytes 98312 | tf_op jit(solution)/shard_map/ppermute | solution.py:451
  53.8 9.7 %collective-permute-start.24 = (bf16[2,64,128]{2,1,0:T(8,128)(2,1)S(1)}, bf16[2,64,128]{2,1,0:T(8,128)(2,1)S(1)}, u32[]{:S(2)}, u32[]{:S(2)}) collective-permute-start(bf16[2,64,128]{2,1,0:T(8,128)(2,1)S(1)} %get-tuple-element.93), channel_id=1, source_target_pairs={{0,4},{2,6},{4,0},{6,2},{1,5},{3,7},{5,1},{7,3},{8,12},{10,14},{12... | collective-permute-start | bytes 98312 | tf_op jit(solution)/shard_map/ppermute | solution.py:451
  55.1 8.7 %collective-permute-start.23 = (bf16[2,64,128]{2,1,0:T(8,128)(2,1)S(1)}, bf16[2,64,128]{2,1,0:T(8,128)(2,1)S(1)}, u32[]{:S(2)}, u32[]{:S(2)}) collective-permute-start(bf16[2,64,128]{2,1,0:T(8,128)(2,1)S(1)} %get-tuple-element.94), channel_id=1, source_target_pairs={{0,2},{2,4},{4,6},{6,0},{1,3},{3,5},{5,7},{7,1},{8,10},{10,12},{12... | collective-permute-start | bytes 98312 | tf_op jit(solution)/shard_map/ppermute | solution.py:451
  56.9 8.2 %collective-permute-start.22 = (bf16[224,128]{1,0:T(8,128)(2,1)S(1)}, bf16[224,128]{1,0:T(8,128)(2,1)S(1)}, u32[]{:S(2)}, u32[]{:S(2)}) collective-permute-start(bf16[224,128]{1,0:T(8,128)(2,1)S(1)} %fusion.1), channel_id=1, source_target_pairs={{0,32},{32,0},{1,33},{33,1},{2,34},{34,2},{3,35},{35,3},{4,36},{36... | collective-permute-start | bytes 172040 | tf_op jit(solution)/shard_map/ppermute | solution.py:552
  63.0 1.2 %collective-permute-start.26 = (bf16[2,64,128]{2,1,0:T(8,128)(2,1)S(1)}, bf16[2,64,128]{2,1,0:T(8,128)(2,1)S(1)}, u32[]{:S(2)}, u32[]{:S(2)}) collective-permute-start(bf16[2,64,128]{2,1,0:T(8,128)(2,1)S(1)} %get-tuple-element.72.refs_0_), channel_id=1, source_target_pairs={{0,1},{1,0},{2,3},{3,2},{4,5},{5,4},{6,7},{7,6},{8,9},{9,8},{10,11... | collective-permute-start | bytes 98312 | tf_op jit(solution)/shard_map/ppermute | solution.py:454
  63.0 1.4 %collective-permute-start.29 = (bf16[2,64,128]{2,1,0:T(8,128)(2,1)S(1)}, bf16[2,64,128]{2,1,0:T(8,128)(2,1)S(1)}, u32[]{:S(2)}, u32[]{:S(2)}) collective-permute-start(bf16[2,64,128]{2,1,0:T(8,128)(2,1)S(1)} %collective-permute-done.25.refs_3_), channel_id=1, source_target_pairs={{0,1},{1,0},{2,3},{3,2},{4,5},{5,4},{6,7},{7,6},{8,9},{9,8},{10,11... | collective-permute-start | bytes 98312 | tf_op jit(solution)/shard_map/ppermute | solution.py:454
  63.5 1.2 %collective-permute-start.28 = (bf16[2,64,128]{2,1,0:T(8,128)(2,1)S(1)}, bf16[2,64,128]{2,1,0:T(8,128)(2,1)S(1)}, u32[]{:S(2)}, u32[]{:S(2)}) collective-permute-start(bf16[2,64,128]{2,1,0:T(8,128)(2,1)S(1)} %collective-permute-done.24.refs_2_), channel_id=1, source_target_pairs={{0,1},{1,0},{2,3},{3,2},{4,5},{5,4},{6,7},{7,6},{8,9},{9,8},{10,11... | collective-permute-start | bytes 98312 | tf_op jit(solution)/shard_map/ppermute | solution.py:454
  63.8 1.2 %collective-permute-start.27 = (bf16[2,64,128]{2,1,0:T(8,128)(2,1)S(1)}, bf16[2,64,128]{2,1,0:T(8,128)(2,1)S(1)}, u32[]{:S(2)}, u32[]{:S(2)}) collective-permute-start(bf16[2,64,128]{2,1,0:T(8,128)(2,1)S(1)} %collective-permute-done.23.refs_1_), channel_id=1, source_target_pairs={{0,1},{1,0},{2,3},{3,2},{4,5},{5,4},{6,7},{7,6},{8,9},{9,8},{10,11... | collective-permute-start | bytes 98312 | tf_op jit(solution)/shard_map/ppermute | solution.py:454
  65.2 9.9 %collective-permute-start.32 = (bf16[224,128]{1,0:T(8,128)(2,1)S(1)}, bf16[224,128]{1,0:T(8,128)(2,1)S(1)}, u32[]{:S(2)}, u32[]{:S(2)}) collective-permute-start(bf16[224,128]{1,0:T(8,128)(2,1)S(1)} %add_convert_fusion.1), channel_id=1, source_target_pairs={{0,24},{8,0},{16,8},{24,16},{1,25},{9,1},{17,9},{25,17},{2,26},{10... | collective-permute-start | bytes 172040 | tf_op jit(solution)/shard_map/ppermute | solution.py:451
  68.2 7.3 %collective-permute-start.31 = (bf16[224,128]{1,0:T(8,128)(2,1)S(1)}, bf16[224,128]{1,0:T(8,128)(2,1)S(1)}, u32[]{:S(2)}, u32[]{:S(2)}) collective-permute-start(bf16[224,128]{1,0:T(8,128)(2,1)S(1)} %add_convert_fusion.1), channel_id=1, source_target_pairs={{0,8},{8,16},{16,24},{24,0},{1,9},{9,17},{17,25},{25,1},{2,10},{10... | collective-permute-start | bytes 172040 | tf_op jit(solution)/shard_map/ppermute | solution.py:451
  68.2 9.0 %collective-permute-start.30 = (bf16[224,128]{1,0:T(8,128)(2,1)S(1)}, bf16[224,128]{1,0:T(8,128)(2,1)S(1)}, u32[]{:S(2)}, u32[]{:S(2)}) collective-permute-start(bf16[224,128]{1,0:T(8,128)(2,1)S(1)} %add_convert_fusion.1), channel_id=1, source_target_pairs={{0,16},{8,24},{16,0},{24,8},{1,17},{9,25},{17,1},{25,9},{2,18},{10... | collective-permute-start | bytes 172040 | tf_op jit(solution)/shard_map/ppermute | solution.py:451
  77.2 7.2 %collective-permute-start.35 = (bf16[224,128]{1,0:T(8,128)(2,1)S(1)}, bf16[224,128]{1,0:T(8,128)(2,1)S(1)}, u32[]{:S(2)}, u32[]{:S(2)}) collective-permute-start(bf16[224,128]{1,0:T(8,128)(2,1)S(1)} %add_convert_fusion.first), channel_id=1, source_target_pairs={{0,192},{64,0},{128,64},{192,128},{1,193},{65,1},{129,65},{193,129... | collective-permute-start | bytes 172040 | tf_op jit(solution)/shard_map/ppermute | solution.py:451
  82.1 5.7 %collective-permute-start.34 = (bf16[224,128]{1,0:T(8,128)(2,1)S(1)}, bf16[224,128]{1,0:T(8,128)(2,1)S(1)}, u32[]{:S(2)}, u32[]{:S(2)}) collective-permute-start(bf16[224,128]{1,0:T(8,128)(2,1)S(1)} %add_convert_fusion.first), channel_id=1, source_target_pairs={{0,128},{64,192},{128,0},{192,64},{1,129},{65,193},{129,1},{193,65... | collective-permute-start | bytes 172040 | tf_op jit(solution)/shard_map/ppermute | solution.py:451
  82.6 5.8 %collective-permute-start.33 = (bf16[224,128]{1,0:T(8,128)(2,1)S(1)}, bf16[224,128]{1,0:T(8,128)(2,1)S(1)}, u32[]{:S(2)}, u32[]{:S(2)}) collective-permute-start(bf16[224,128]{1,0:T(8,128)(2,1)S(1)} %add_convert_fusion.first), channel_id=1, source_target_pairs={{0,64},{64,128},{128,192},{192,0},{1,65},{65,129},{129,193},{193,1... | collective-permute-start | bytes 172040 | tf_op jit(solution)/shard_map/ppermute | solution.py:451

commit v7 on v6

--- a/solution.py
+++ b/solution.py
@@ -518,8 +518,8 @@
         bias,
         flops=2 * 192 * 576 * 128 * 30,
     )
+    from_odd = lax.ppermute(to_odd, near, odd)
     from_even = lax.ppermute(to_even, near, even)
-    from_odd = lax.ppermute(to_odd, near, odd)
     grad_two, total_two, narrow = call(
         second_grad_kernel,
         [((192, 576), F32), ((64, 128), F32), ((192, 1280), BF16)],

time: 89.9 us -> 89.9 us (level)
  no operation moved by 1% of the time
where the time goes in v7:
time: 89.9 us; the launch traced here: 89.2 us
  starting transfers between devices  54.8 us (61%)
  waiting for transfers between devices  20.5 us (23%)
  Pallas kernels  11.1 us (12%)
  local copies, waits for them, and re-layouts  1.82 us (2%)
    ppermute x18, starting transfers between devices, spread(): lax.ppermute(pieces[k], axis, turns[k])  31.6 us
    ppermute x18, waiting for transfers between devices, spread(): lax.ppermute(pieces[k], axis, turns[k])  13.4 us
    pallas_call x9, Pallas kernels, call(): pl.pallas_call(kernel, out_shape=outs, in_specs=[smem if k in scalars els...  11.1 us
    ppermute x1, starting transfers between devices, shards(): from_odd = lax.ppermute(to_odd, near, odd)  10.2 us
    ppermute x1, starting transfers between devices, shards(): other = lax.ppermute(part, 'h', swap)  6.06 us
    ppermute x1, starting transfers between devices, shards(): near_odd = lax.ppermute(field, near, odd)  3.48 us
    ppermute x12, starting transfers between devices, cross(): return [lax.ppermute(piece, 'c', swap) for piece in pieces]  2.83 us
    ppermute x12, waiting for transfers between devices, cross(): return [lax.ppermute(piece, 'c', swap) for piece in pieces]  2.25 us
  transfers between devices with their start and end apart: 36, of which 21 were waited for; matrix products, arithmetic and copies ran while one was open for 0% of the time, Pallas kernels for 5%

profile of v7, /device:TPU:8, one launch (start us, length us, event | category | flops | bytes accessed | tf_op | source)
XLA Modules:
  0.0 89.2 jit_solution(14434667189415571484)
XLA Ops:
  0.6 0.9 %copy-done = bf16[8,2,32,128]{3,2,1,0:T(8,128)(2,1)S(1)} copy-done((bf16[8,2,32,128]{3,2,1,0:T(8,128)(2,1)S(1)}, bf16[8,2,32,128]{3,2,1,0:T(8,128)(2,1)}, u32[]{:S(2)}) %copy-start) | copy-done | bytes 131096
  1.5 0.3 shard_map.102
  1.9 4.7 %collective-permute-start.2 = (bf16[2,88,128]{2,1,0:T(8,128)(2,1)S(1)}, bf16[2,88,128]{2,1,0:T(8,128)(2,1)S(1)}, u32[]{:S(2)}, u32[]{:S(2)}) collective-permute-start(bf16[2,88,128]{2,1,0:T(8,128)(2,1)S(1)} %get-tuple-element.88), channel_id=1, source_target_pairs={{0,6},{2,0},{4,2},{6,4},{1,7},{3,1},{5,3},{7,5},{8,14},{10,8},{12,... | collective-permute-start | bytes 135176 | tf_op jit(solution)/shard_map/ppermute | solution.py:451
  6.6 0.7 collective-permute-start
  7.3 1.9 %shard_map.101 = (bf16[384,128]{1,0:T(8,128)(2,1)}, bf16[384,128]{1,0:T(8,128)(2,1)}, bf16[384,128]{1,0:T(8,128)(2,1)}, bf16[384,128]{1,0:T(8,128)(2,1)}) custom-call(bf16[8,64,128]{2,1,0:T(8,128)(2,1)} %bitcast.44, bf16[27,8,64]{2,1,0:T(8,128)(2,1)} %bitcast.45, f32[8]{0:T(128)} %bias_one.1, bf16[27,8,64]{2,1,0:T(8,128)(2,1)} %bitcast.46, f32[8]{0:T(128)} %bias_two.1), custom_call_target="tpu_custom_call" | custom-call | tf_op jit(solution)/shard_map/pallas_call | solution.py:417
  9.2 2.4 %collective-permute-done.1.refs_2_ = bf16[2,88,128]{2,1,0:T(8,128)(2,1)S(1)} collective-permute-done((bf16[2,88,128]{2,1,0:T(8,128)(2,1)S(1)}, bf16[2,88,128]{2,1,0:T(8,128)(2,1)S(1)}, u32[]{:S(2)}, u32[]{:S(2)}) %collective-permute-start.1) | collective-permute-done | bytes 45088 | tf_op jit(solution)/shard_map/ppermute | solution.py:451
  11.5 0.9 %collective-permute-done.refs_1_ = bf16[2,88,128]{2,1,0:T(8,128)(2,1)S(1)} collective-permute-done((bf16[2,88,128]{2,1,0:T(8,128)(2,1)S(1)}, bf16[2,88,128]{2,1,0:T(8,128)(2,1)S(1)}, u32[]{:S(2)}, u32[]{:S(2)}) %collective-permute-start) | collective-permute-done | bytes 45088 | tf_op jit(solution)/shard_map/ppermute | solution.py:451
  12.4 0.5 collective-permute-start.4
  13.0 0.5 collective-permute-start.6
  13.7 1.5 %collective-permute-start.10 = (bf16[384,128]{1,0:T(8,128)(2,1)}, bf16[384,128]{1,0:T(8,128)(2,1)S(1)}, u32[]{:S(2)}, u32[]{:S(2)}) collective-permute-start(bf16[384,128]{1,0:T(8,128)(2,1)} %get-tuple-element.55), channel_id=1, source_target_pairs={{0,4},{2,6},{4,0},{6,2},{1,5},{3,7},{5,1},{7,3},{8,12},{10,14},{12... | collective-permute-start | bytes 294920 | tf_op jit(solution)/shard_map/ppermute | solution.py:451
  15.2 2.6 %collective-permute-start.11 = (bf16[384,128]{1,0:T(8,128)(2,1)}, bf16[384,128]{1,0:T(8,128)(2,1)S(1)}, u32[]{:S(2)}, u32[]{:S(2)}) collective-permute-start(bf16[384,128]{1,0:T(8,128)(2,1)} %get-tuple-element.56), channel_id=1, source_target_pairs={{0,6},{2,0},{4,2},{6,4},{1,7},{3,1},{5,3},{7,5},{8,14},{10,8},{12,... | collective-permute-start | bytes 294920 | tf_op jit(solution)/shard_map/ppermute | solution.py:451
  17.8 3.5 %collective-permute-start.8 = (bf16[11,64,128]{2,1,0:T(8,128)(2,1)S(1)}, bf16[11,64,128]{2,1,0:T(8,128)(2,1)S(1)}, u32[]{:S(2)}, u32[]{:S(2)}) collective-permute-start(bf16[11,64,128]{2,1,0:T(8,128)(2,1)S(1)} %shard_map.103.own), channel_id=1, source_target_pairs={{8,16},{16,8},{10,18},{18,10},{12,20},{20,12},{14,22},{22,14},{24,... | collective-permute-start | bytes 540680 | tf_op jit(solution)/shard_map/ppermute | solution.py:491
  21.4 1.9 %collective-permute-done.10.refs_2_ = bf16[384,128]{1,0:T(8,128)(2,1)S(1)} collective-permute-done((bf16[384,128]{1,0:T(8,128)(2,1)}, bf16[384,128]{1,0:T(8,128)(2,1)S(1)}, u32[]{:S(2)}, u32[]{:S(2)}) %collective-permute-start.10) | collective-permute-done | bytes 98336 | tf_op jit(solution)/shard_map/ppermute | solution.py:451
  23.4 0.5 collective-permute-start.14
  24.1 0.5 collective-permute-done.13.refs_5_
  24.8 0.4 collective-permute-done.15.refs_7_
  25.2 0.9 copy-done.1
  26.1 0.6 shard_map.104
  26.7 1.4 %collective-permute-done.7.even = bf16[11,64,128]{2,1,0:T(8,128)(2,1)S(1)} collective-permute-done((bf16[11,64,128]{2,1,0:T(8,128)(2,1)S(1)}, bf16[11,64,128]{2,1,0:T(8,128)(2,1)S(1)}, u32[]{:S(2)}, u32[]{:S(2)}) %collective-permute-start.7) | collective-permute-done | bytes 180256 | tf_op jit(solution)/shard_map/ppermute | solution.py:490
  28.1 4.6 %shard_map.105 = (bf16[192,1536]{1,0:T(8,128)(2,1)S(1)}, bf16[192,2816]{1,0:T(8,128)(2,1)S(1)}, bf16[10,64,128]{2,1,0:T(8,128)(2,1)S(1)}, bf16[4,2,64,128]{3,2,1...) custom-call(bf16[11,64,128]{2,1,0:T(8,128)(2,1)S(1)} %shard_map.103.own, ...), custom_call_target="tpu_custom_call" | custom-call | flops 849346560 | bytes 3342336 | tf_op jit(solution)/shard_map/pallas_call | solution.py:417
  32.7 0.4 collective-permute-start.16
  33.1 10.2 %collective-permute-start.17 = (bf16[5,64,128]{2,1,0:T(8,128)(2,1)S(1)}, bf16[5,64,128]{2,1,0:T(8,128)(2,1)S(1)}, u32[]{:S(2)}, u32[]{:S(2)}) collective-permute-start(bf16[5,64,128]{2,1,0:T(8,128)(2,1)S(1)} %get-tuple-element.62), channel_id=1, source_target_pairs={{8,16},{16,8},{10,18},{18,10},{12,20},{20,12},{14,22},{22,14},{24,... | collective-permute-start | bytes 245768 | tf_op jit(solution)/shard_map/ppermute | solution.py:521
  43.3 0.6 shard_map.106
  44.0 1.8 %collective-permute-done.17.from_odd = bf16[5,64,128]{2,1,0:T(8,128)(2,1)S(1)} collective-permute-done((bf16[5,64,128]{2,1,0:T(8,128)(2,1)S(1)}, bf16[5,64,128]{2,1,0:T(8,128)(2,1)S(1)}, u32[]{:S(2)}, u32[]{:S(2)}) %collective-permute-start.17) | collective-permute-done | bytes 81952 | tf_op jit(solution)/shard_map/ppermute | solution.py:521
  45.7 1.3 %shard_map.107 = (bf16[4,224,128]{2,1,0:T(8,128)(2,1)S(1)}, bf16[4,224,128]{2,1,0:T(8,128)(2,1)S(1)}) custom-call(bf16[10,64,128]{2,1,0:T(8,128)(2,1)S(1)} %get-tuple-element.60.delta, bf16[5,64,128]{2,1,0:T(8,128)(2,1)S(1)} %collective-permute-done.16.from_even, bf16[5,64,128]{2,1,0:T(8,128)(2,1)S(1)} %collective-permute-done.17.from_odd, ...), custom_call_target="tpu_custom_call" | custom-call | flops 452984832 | bytes 2564096 | tf_op jit(solution)/shard_map/pallas_call | solution.py:417
  47.2 1.5 %collective-permute-done.18 = bf16[4,224,128]{2,1,0:T(8,128)(2,1)S(1)} collective-permute-done((bf16[4,224,128]{2,1,0:T(8,128)(2,1)S(1)}, bf16[4,224,128]{2,1,0:T(8,128)(2,1)S(1)}, u32[]{:S(2)}, u32[]{:S(2)}) %collective-permute-start.18) | collective-permute-done | bytes 229408 | tf_op jit(solution)/shard_map/ppermute | solution.py:548
  48.8 1.1 %collective-permute-start.21 = (bf16[224,128]{1,0:T(8,128)(2,1)S(1)}, bf16[224,128]{1,0:T(8,128)(2,1)S(1)}, u32[]{:S(2)}, u32[]{:S(2)}) collective-permute-start(bf16[224,128]{1,0:T(8,128)(2,1)S(1)} %get-tuple-element.86), channel_id=1, source_target_pairs={{0,6},{2,0},{4,2},{6,4},{1,7},{3,1},{5,3},{7,5},{8,14},{10,8},{12,... | collective-permute-start | bytes 172040 | tf_op jit(solution)/shard_map/ppermute | solution.py:451
  49.9 1.0 %collective-permute-start.20 = (bf16[224,128]{1,0:T(8,128)(2,1)S(1)}, bf16[224,128]{1,0:T(8,128)(2,1)S(1)}, u32[]{:S(2)}, u32[]{:S(2)}) collective-permute-start(bf16[224,128]{1,0:T(8,128)(2,1)S(1)} %get-tuple-element.87), channel_id=1, source_target_pairs={{0,2},{2,4},{4,6},{6,0},{1,3},{3,5},{5,7},{7,1},{8,10},{10,12},{12... | collective-permute-start | bytes 172040 | tf_op jit(solution)/shard_map/ppermute | solution.py:451
  50.9 2.9 %collective-permute-start.25 = (bf16[2,64,128]{2,1,0:T(8,128)(2,1)S(1)}, bf16[2,64,128]{2,1,0:T(8,128)(2,1)S(1)}, u32[]{:S(2)}, u32[]{:S(2)}) collective-permute-start(bf16[2,64,128]{2,1,0:T(8,128)(2,1)S(1)} %get-tuple-element.92), channel_id=1, source_target_pairs={{0,6},{2,0},{4,2},{6,4},{1,7},{3,1},{5,3},{7,5},{8,14},{10,8},{12,... | collective-permute-start | bytes 98312 | tf_op jit(solution)/shard_map/ppermute | solution.py:451
  53.9 1.1 %collective-permute-done.19 = bf16[224,128]{1,0:T(8,128)(2,1)S(1)} collective-permute-done((bf16[224,128]{1,0:T(8,128)(2,1)S(1)}, bf16[224,128]{1,0:T(8,128)(2,1)S(1)}, u32[]{:S(2)}, u32[]{:S(2)}) %collective-permute-start.19) | collective-permute-done | bytes 57376 | tf_op jit(solution)/shard_map/ppermute | solution.py:451
  55.1 0.8 collective-permute-start.23
  55.9 1.0 %collective-permute-done.20 = bf16[224,128]{1,0:T(8,128)(2,1)S(1)} collective-permute-done((bf16[224,128]{1,0:T(8,128)(2,1)S(1)}, bf16[224,128]{1,0:T(8,128)(2,1)S(1)}, u32[]{:S(2)}, u32[]{:S(2)}) %collective-permute-start.20) | collective-permute-done | bytes 57376 | tf_op jit(solution)/shard_map/ppermute | solution.py:451
  56.9 6.1 %collective-permute-start.22 = (bf16[224,128]{1,0:T(8,128)(2,1)S(1)}, bf16[224,128]{1,0:T(8,128)(2,1)S(1)}, u32[]{:S(2)}, u32[]{:S(2)}) collective-permute-start(bf16[224,128]{1,0:T(8,128)(2,1)S(1)} %fusion.1), channel_id=1, source_target_pairs={{0,32},{32,0},{1,33},{33,1},{2,34},{34,2},{3,35},{35,3},{4,36},{36... | collective-permute-start | bytes 172040 | tf_op jit(solution)/shard_map/ppermute | solution.py:552
  63.0 0.5 collective-permute-start.29
  63.5 0.3 collective-permute-start.28
  64.3 0.4 collective-permute-done.28.refs_6_
  64.7 0.3 collective-permute-done.27.refs_5_
  65.2 3.0 %collective-permute-start.32 = (bf16[224,128]{1,0:T(8,128)(2,1)S(1)}, bf16[224,128]{1,0:T(8,128)(2,1)S(1)}, u32[]{:S(2)}, u32[]{:S(2)}) collective-permute-start(bf16[224,128]{1,0:T(8,128)(2,1)S(1)} %add_convert_fusion.1), channel_id=1, source_target_pairs={{0,24},{8,0},{16,8},{24,16},{1,25},{9,1},{17,9},{25,17},{2,26},{10... | collective-permute-start | bytes 172040 | tf_op jit(solution)/shard_map/ppermute | solution.py:451
  68.2 6.9 %collective-permute-start.30 = (bf16[224,128]{1,0:T(8,128)(2,1)S(1)}, bf16[224,128]{1,0:T(8,128)(2,1)S(1)}, u32[]{:S(2)}, u32[]{:S(2)}) collective-permute-start(bf16[224,128]{1,0:T(8,128)(2,1)S(1)} %add_convert_fusion.1), channel_id=1, source_target_pairs={{0,16},{8,24},{16,0},{24,8},{1,17},{9,25},{17,1},{25,9},{2,18},{10... | collective-permute-start | bytes 172040 | tf_op jit(solution)/shard_map/ppermute | solution.py:451
  75.1 0.4 collective-permute-done.31
  75.5 1.7 %collective-permute-done.30 = bf16[224,128]{1,0:T(8,128)(2,1)S(1)} collective-permute-done((bf16[224,128]{1,0:T(8,128)(2,1)S(1)}, bf16[224,128]{1,0:T(8,128)(2,1)S(1)}, u32[]{:S(2)}, u32[]{:S(2)}) %collective-permute-start.30) | collective-permute-done | bytes 57376 | tf_op jit(solution)/shard_map/ppermute | solution.py:451
  77.2 4.9 %collective-permute-start.35 = (bf16[224,128]{1,0:T(8,128)(2,1)S(1)}, bf16[224,128]{1,0:T(8,128)(2,1)S(1)}, u32[]{:S(2)}, u32[]{:S(2)}) collective-permute-start(bf16[224,128]{1,0:T(8,128)(2,1)S(1)} %add_convert_fusion.first), channel_id=1, source_target_pairs={{0,192},{64,0},{128,64},{192,128},{1,193},{65,1},{129,65},{193,129... | collective-permute-start | bytes 172040 | tf_op jit(solution)/shard_map/ppermute | solution.py:451
  82.1 0.5 collective-permute-start.34
  82.6 0.9 %collective-permute-start.33 = (bf16[224,128]{1,0:T(8,128)(2,1)S(1)}, bf16[224,128]{1,0:T(8,128)(2,1)S(1)}, u32[]{:S(2)}, u32[]{:S(2)}) collective-permute-start(bf16[224,128]{1,0:T(8,128)(2,1)S(1)} %add_convert_fusion.first), channel_id=1, source_target_pairs={{0,64},{64,128},{128,192},{192,0},{1,65},{65,129},{129,193},{193,1... | collective-permute-start | bytes 172040 | tf_op jit(solution)/shard_map/ppermute | solution.py:451
  83.5 0.9 %shard_map.108 = bf16[8,64,128]{2,1,0:T(8,128)(2,1)} custom-call(bf16[2,64,128]{2,1,0:T(8,128)(2,1)S(1)} %get-tuple-element.72.refs_0_, bf16[2,64,128]{2,1,0:T(8,128)(2,1)S(1)} %collective-permute-done.23.refs_1_, bf16[2,64,128]{2,1,0:T(8,128)(2,1)S(1)} %collective-permute-done.24.refs_2_, bf16[2,64,128]{2,1,0:T(8,128)(2,1)S(1)} %collective-permute-done.25.refs_3_, ...), custom_call_target="tpu_custom_call" | custom-call | tf_op jit(solution)/shard_map/pallas_call | solution.py:417
  84.4 3.4 %collective-permute-done.34.third = bf16[224,128]{1,0:T(8,128)(2,1)S(1)} collective-permute-done((bf16[224,128]{1,0:T(8,128)(2,1)S(1)}, bf16[224,128]{1,0:T(8,128)(2,1)S(1)}, u32[]{:S(2)}, u32[]{:S(2)}) %collective-permute-start.34) | collective-permute-done | bytes 57376 | tf_op jit(solution)/shard_map/ppermute | solution.py:451
  87.8 0.6 collective-permute-done.33.second
  88.4 0.8 shard_map.109
  (43 shorter events, 2.0 us)
Async XLA Ops:
  0.6 0.9 %copy-start = (bf16[8,2,32,128]{3,2,1,0:T(8,128)(2,1)S(1)}, bf16[8,2,32,128]{3,2,1,0:T(8,128)(2,1)}, u32[]{:S(2)}) copy-start(bf16[8,2,32,128]{3,2,1,0:T(8,128)(2,1)} %param.6) | copy-start | bytes 393220
  1.9 7.3 %collective-permute-start.2 = (bf16[2,88,128]{2,1,0:T(8,128)(2,1)S(1)}, bf16[2,88,128]{2,1,0:T(8,128)(2,1)S(1)}, u32[]{:S(2)}, u32[]{:S(2)}) collective-permute-start(bf16[2,88,128]{2,1,0:T(8,128)(2,1)S(1)} %get-tuple-element.88), channel_id=1, source_target_pairs={{0,6},{2,0},{4,2},{6,4},{1,7},{3,1},{5,3},{7,5},{8,14},{10,8},{12,... | collective-permute-start | bytes 135176 | tf_op jit(solution)/shard_map/ppermute | solution.py:451
  6.6 4.9 %collective-permute-start.1 = (bf16[2,88,128]{2,1,0:T(8,128)(2,1)S(1)}, bf16[2,88,128]{2,1,0:T(8,128)(2,1)S(1)}, u32[]{:S(2)}, u32[]{:S(2)}) collective-permute-start(bf16[2,88,128]{2,1,0:T(8,128)(2,1)S(1)} %get-tuple-element.89), channel_id=1, source_target_pairs={{0,4},{2,6},{4,0},{6,2},{1,5},{3,7},{5,1},{7,3},{8,12},{10,14},{12... | collective-permute-start | bytes 135176 | tf_op jit(solution)/shard_map/ppermute | solution.py:451
  6.6 5.8 %collective-permute-start = (bf16[2,88,128]{2,1,0:T(8,128)(2,1)S(1)}, bf16[2,88,128]{2,1,0:T(8,128)(2,1)S(1)}, u32[]{:S(2)}, u32[]{:S(2)}) collective-permute-start(bf16[2,88,128]{2,1,0:T(8,128)(2,1)S(1)} %get-tuple-element.90), channel_id=1, source_target_pairs={{0,2},{2,4},{4,6},{6,0},{1,3},{3,5},{5,7},{7,1},{8,10},{10,12},{12... | collective-permute-start | bytes 135176 | tf_op jit(solution)/shard_map/ppermute | solution.py:451
  12.4 8.9 %collective-permute-start.9 = (bf16[384,128]{1,0:T(8,128)(2,1)}, bf16[384,128]{1,0:T(8,128)(2,1)S(1)}, u32[]{:S(2)}, u32[]{:S(2)}) collective-permute-start(bf16[384,128]{1,0:T(8,128)(2,1)} %get-tuple-element.54), channel_id=1, source_target_pairs={{0,2},{2,4},{4,6},{6,0},{1,3},{3,5},{5,7},{7,1},{8,10},{10,12},{12... | collective-permute-start | bytes 294920 | tf_op jit(solution)/shard_map/ppermute | solution.py:451
  12.4 1.2 %collective-permute-start.3 = (bf16[2,88,128]{2,1,0:T(8,128)(2,1)S(1)}, bf16[2,88,128]{2,1,0:T(8,128)(2,1)S(1)}, u32[]{:S(2)}, u32[]{:S(2)}) collective-permute-start(bf16[2,88,128]{2,1,0:T(8,128)(2,1)S(1)} %get-tuple-element.49.refs_0_), channel_id=1, source_target_pairs={{0,1},{1,0},{2,3},{3,2},{4,5},{5,4},{6,7},{7,6},{8,9},{9,8},{10,11... | collective-permute-start | bytes 135176 | tf_op jit(solution)/shard_map/ppermute | solution.py:454
  12.4 2.7 %collective-permute-start.4 = (bf16[2,88,128]{2,1,0:T(8,128)(2,1)S(1)}, bf16[2,88,128]{2,1,0:T(8,128)(2,1)S(1)}, u32[]{:S(2)}, u32[]{:S(2)}) collective-permute-start(bf16[2,88,128]{2,1,0:T(8,128)(2,1)S(1)} %collective-permute-done.refs_1_), channel_id=1, source_target_pairs={{0,1},{1,0},{2,3},{3,2},{4,5},{5,4},{6,7},{7,6},{8,9},{9,8},{10,11... | collective-permute-start | bytes 135176 | tf_op jit(solution)/shard_map/ppermute | solution.py:454
  13.0 4.8 %collective-permute-start.5 = (bf16[2,88,128]{2,1,0:T(8,128)(2,1)S(1)}, bf16[2,88,128]{2,1,0:T(8,128)(2,1)S(1)}, u32[]{:S(2)}, u32[]{:S(2)}) collective-permute-start(bf16[2,88,128]{2,1,0:T(8,128)(2,1)S(1)} %collective-permute-done.1.refs_2_), channel_id=1, source_target_pairs={{0,1},{1,0},{2,3},{3,2},{4,5},{5,4},{6,7},{7,6},{8,9},{9,8},{10,11... | collective-permute-start | bytes 135176 | tf_op jit(solution)/shard_map/ppermute | solution.py:454
  13.0 4.8 %collective-permute-start.6 = (bf16[2,88,128]{2,1,0:T(8,128)(2,1)S(1)}, bf16[2,88,128]{2,1,0:T(8,128)(2,1)S(1)}, u32[]{:S(2)}, u32[]{:S(2)}) collective-permute-start(bf16[2,88,128]{2,1,0:T(8,128)(2,1)S(1)} %collective-permute-done.2.refs_3_), channel_id=1, source_target_pairs={{0,1},{1,0},{2,3},{3,2},{4,5},{5,4},{6,7},{7,6},{8,9},{9,8},{10,11... | collective-permute-start | bytes 135176 | tf_op jit(solution)/shard_map/ppermute | solution.py:454
  13.7 9.7 %collective-permute-start.10 = (bf16[384,128]{1,0:T(8,128)(2,1)}, bf16[384,128]{1,0:T(8,128)(2,1)S(1)}, u32[]{:S(2)}, u32[]{:S(2)}) collective-permute-start(bf16[384,128]{1,0:T(8,128)(2,1)} %get-tuple-element.55), channel_id=1, source_target_pairs={{0,4},{2,6},{4,0},{6,2},{1,5},{3,7},{5,1},{7,3},{8,12},{10,14},{12... | collective-permute-start | bytes 294920 | tf_op jit(solution)/shard_map/ppermute | solution.py:451
  15.2 8.2 %collective-permute-start.11 = (bf16[384,128]{1,0:T(8,128)(2,1)}, bf16[384,128]{1,0:T(8,128)(2,1)S(1)}, u32[]{:S(2)}, u32[]{:S(2)}) collective-permute-start(bf16[384,128]{1,0:T(8,128)(2,1)} %get-tuple-element.56), channel_id=1, source_target_pairs={{0,6},{2,0},{4,2},{6,4},{1,7},{3,1},{5,3},{7,5},{8,14},{10,8},{12,... | collective-permute-start | bytes 294920 | tf_op jit(solution)/shard_map/ppermute | solution.py:451
  17.7 6.1 %collective-permute-start.12 = (bf16[384,128]{1,0:T(8,128)(2,1)}, bf16[384,128]{1,0:T(8,128)(2,1)S(1)}, u32[]{:S(2)}, u32[]{:S(2)}) collective-permute-start(bf16[384,128]{1,0:T(8,128)(2,1)} %get-tuple-element.53.refs_0_), channel_id=1, source_target_pairs={{0,1},{1,0},{2,3},{3,2},{4,5},{5,4},{6,7},{7,6},{8,9},{9,8},{10,11... | collective-permute-start | bytes 294920 | tf_op jit(solution)/shard_map/ppermute | solution.py:454
  17.8 8.9 %collective-permute-start.8 = (bf16[11,64,128]{2,1,0:T(8,128)(2,1)S(1)}, bf16[11,64,128]{2,1,0:T(8,128)(2,1)S(1)}, u32[]{:S(2)}, u32[]{:S(2)}) collective-permute-start(bf16[11,64,128]{2,1,0:T(8,128)(2,1)S(1)} %shard_map.103.own), channel_id=1, source_target_pairs={{8,16},{16,8},{10,18},{18,10},{12,20},{20,12},{14,22},{22,14},{24,... | collective-permute-start | bytes 540680 | tf_op jit(solution)/shard_map/ppermute | solution.py:491
  21.3 6.8 %collective-permute-start.7 = (bf16[11,64,128]{2,1,0:T(8,128)(2,1)S(1)}, bf16[11,64,128]{2,1,0:T(8,128)(2,1)S(1)}, u32[]{:S(2)}, u32[]{:S(2)}) collective-permute-start(bf16[11,64,128]{2,1,0:T(8,128)(2,1)S(1)} %shard_map.103.own), channel_id=1, source_target_pairs={{0,8},{8,0},{2,10},{10,2},{4,12},{12,4},{6,14},{14,6},{16,24},{24,... | collective-permute-start | bytes 540680 | tf_op jit(solution)/shard_map/ppermute | solution.py:490
  23.3 1.3 %collective-permute-start.13 = (bf16[384,128]{1,0:T(8,128)(2,1)S(1)}, bf16[384,128]{1,0:T(8,128)(2,1)S(1)}, u32[]{:S(2)}, u32[]{:S(2)}) collective-permute-start(bf16[384,128]{1,0:T(8,128)(2,1)S(1)} %collective-permute-done.9.refs_1_), channel_id=1, source_target_pairs={{0,1},{1,0},{2,3},{3,2},{4,5},{5,4},{6,7},{7,6},{8,9},{9,8},{10,11... | collective-permute-start | bytes 294920 | tf_op jit(solution)/shard_map/ppermute | solution.py:454
  23.4 1.5 %collective-permute-start.14 = (bf16[384,128]{1,0:T(8,128)(2,1)S(1)}, bf16[384,128]{1,0:T(8,128)(2,1)S(1)}, u32[]{:S(2)}, u32[]{:S(2)}) collective-permute-start(bf16[384,128]{1,0:T(8,128)(2,1)S(1)} %collective-permute-done.10.refs_2_), channel_id=1, source_target_pairs={{0,1},{1,0},{2,3},{3,2},{4,5},{5,4},{6,7},{7,6},{8,9},{9,8},{10,11... | collective-permute-start | bytes 294920 | tf_op jit(solution)/shard_map/ppermute | solution.py:454
  23.9 1.3 %collective-permute-start.15 = (bf16[384,128]{1,0:T(8,128)(2,1)S(1)}, bf16[384,128]{1,0:T(8,128)(2,1)S(1)}, u32[]{:S(2)}, u32[]{:S(2)}) collective-permute-start(bf16[384,128]{1,0:T(8,128)(2,1)S(1)} %collective-permute-done.11.refs_3_), channel_id=1, source_target_pairs={{0,1},{1,0},{2,3},{3,2},{4,5},{5,4},{6,7},{7,6},{8,9},{9,8},{10,11... | collective-permute-start | bytes 294920 | tf_op jit(solution)/shard_map/ppermute | solution.py:454
  25.2 0.9 %copy-start.1 = (bf16[384,128]{1,0:T(8,128)(2,1)S(1)}, bf16[384,128]{1,0:T(8,128)(2,1)}, u32[]{:S(2)}) copy-start(bf16[384,128]{1,0:T(8,128)(2,1)} %get-tuple-element.53.refs_0_) | copy-start | bytes 294916
  32.7 11.2 %collective-permute-start.16 = (bf16[5,64,128]{2,1,0:T(8,128)(2,1)S(1)}, bf16[5,64,128]{2,1,0:T(8,128)(2,1)S(1)}, u32[]{:S(2)}, u32[]{:S(2)}) collective-permute-start(bf16[5,64,128]{2,1,0:T(8,128)(2,1)S(1)} %get-tuple-element.61), channel_id=1, source_target_pairs={{0,8},{8,0},{2,10},{10,2},{4,12},{12,4},{6,14},{14,6},{16,24},{24,... | collective-permute-start | bytes 245768 | tf_op jit(solution)/shard_map/ppermute | solution.py:522
  33.1 12.7 %collective-permute-start.17 = (bf16[5,64,128]{2,1,0:T(8,128)(2,1)S(1)}, bf16[5,64,128]{2,1,0:T(8,128)(2,1)S(1)}, u32[]{:S(2)}, u32[]{:S(2)}) collective-permute-start(bf16[5,64,128]{2,1,0:T(8,128)(2,1)S(1)} %get-tuple-element.62), channel_id=1, source_target_pairs={{8,16},{16,8},{10,18},{18,10},{12,20},{20,12},{14,22},{22,14},{24,... | collective-permute-start | bytes 245768 | tf_op jit(solution)/shard_map/ppermute | solution.py:521
  47.1 1.6 %collective-permute-start.18 = (bf16[4,224,128]{2,1,0:T(8,128)(2,1)S(1)}, bf16[4,224,128]{2,1,0:T(8,128)(2,1)S(1)}, u32[]{:S(2)}, u32[]{:S(2)}) collective-permute-start(bf16[4,224,128]{2,1,0:T(8,128)(2,1)S(1)} %get-tuple-element.70), channel_id=1, source_target_pairs={{0,1},{1,0},{2,3},{3,2},{4,5},{5,4},{6,7},{7,6},{8,9},{9,8},{10,11... | collective-permute-start | bytes 688136 | tf_op jit(solution)/shard_map/ppermute | solution.py:548
  48.7 6.4 %collective-permute-start.19 = (bf16[224,128]{1,0:T(8,128)(2,1)S(1)}, bf16[224,128]{1,0:T(8,128)(2,1)S(1)}, u32[]{:S(2)}, u32[]{:S(2)}) collective-permute-start(bf16[224,128]{1,0:T(8,128)(2,1)S(1)} %get-tuple-element.85), channel_id=1, source_target_pairs={{0,4},{2,6},{4,0},{6,2},{1,5},{3,7},{5,1},{7,3},{8,12},{10,14},{12... | collective-permute-start | bytes 172040 | tf_op jit(solution)/shard_map/ppermute | solution.py:451
  48.8 7.1 %collective-permute-start.21 = (bf16[224,128]{1,0:T(8,128)(2,1)S(1)}, bf16[224,128]{1,0:T(8,128)(2,1)S(1)}, u32[]{:S(2)}, u32[]{:S(2)}) collective-permute-start(bf16[224,128]{1,0:T(8,128)(2,1)S(1)} %get-tuple-element.86), channel_id=1, source_target_pairs={{0,6},{2,0},{4,2},{6,4},{1,7},{3,1},{5,3},{7,5},{8,14},{10,8},{12,... | collective-permute-start | bytes 172040 | tf_op jit(solution)/shard_map/ppermute | solution.py:451
  49.9 7.0 %collective-permute-start.20 = (bf16[224,128]{1,0:T(8,128)(2,1)S(1)}, bf16[224,128]{1,0:T(8,128)(2,1)S(1)}, u32[]{:S(2)}, u32[]{:S(2)}) collective-permute-start(bf16[224,128]{1,0:T(8,128)(2,1)S(1)} %get-tuple-element.87), channel_id=1, source_target_pairs={{0,2},{2,4},{4,6},{6,0},{1,3},{3,5},{5,7},{7,1},{8,10},{10,12},{12... | collective-permute-start | bytes 172040 | tf_op jit(solution)/shard_map/ppermute | solution.py:451
  50.9 12.1 %collective-permute-start.25 = (bf16[2,64,128]{2,1,0:T(8,128)(2,1)S(1)}, bf16[2,64,128]{2,1,0:T(8,128)(2,1)S(1)}, u32[]{:S(2)}, u32[]{:S(2)}) collective-permute-start(bf16[2,64,128]{2,1,0:T(8,128)(2,1)S(1)} %get-tuple-element.92), channel_id=1, source_target_pairs={{0,6},{2,0},{4,2},{6,4},{1,7},{3,1},{5,3},{7,5},{8,14},{10,8},{12,... | collective-permute-start | bytes 98312 | tf_op jit(solution)/shard_map/ppermute | solution.py:451
  53.8 9.7 %collective-permute-start.24 = (bf16[2,64,128]{2,1,0:T(8,128)(2,1)S(1)}, bf16[2,64,128]{2,1,0:T(8,128)(2,1)S(1)}, u32[]{:S(2)}, u32[]{:S(2)}) collective-permute-start(bf16[2,64,128]{2,1,0:T(8,128)(2,1)S(1)} %get-tuple-element.93), channel_id=1, source_target_pairs={{0,4},{2,6},{4,0},{6,2},{1,5},{3,7},{5,1},{7,3},{8,12},{10,14},{12... | collective-permute-start | bytes 98312 | tf_op jit(solution)/shard_map/ppermute | solution.py:451
  55.1 8.7 %collective-permute-start.23 = (bf16[2,64,128]{2,1,0:T(8,128)(2,1)S(1)}, bf16[2,64,128]{2,1,0:T(8,128)(2,1)S(1)}, u32[]{:S(2)}, u32[]{:S(2)}) collective-permute-start(bf16[2,64,128]{2,1,0:T(8,128)(2,1)S(1)} %get-tuple-element.94), channel_id=1, source_target_pairs={{0,2},{2,4},{4,6},{6,0},{1,3},{3,5},{5,7},{7,1},{8,10},{10,12},{12... | collective-permute-start | bytes 98312 | tf_op jit(solution)/shard_map/ppermute | solution.py:451
  56.9 8.2 %collective-permute-start.22 = (bf16[224,128]{1,0:T(8,128)(2,1)S(1)}, bf16[224,128]{1,0:T(8,128)(2,1)S(1)}, u32[]{:S(2)}, u32[]{:S(2)}) collective-permute-start(bf16[224,128]{1,0:T(8,128)(2,1)S(1)} %fusion.1), channel_id=1, source_target_pairs={{0,32},{32,0},{1,33},{33,1},{2,34},{34,2},{3,35},{35,3},{4,36},{36... | collective-permute-start | bytes 172040 | tf_op jit(solution)/shard_map/ppermute | solution.py:552
  63.0 1.2 %collective-permute-start.26 = (bf16[2,64,128]{2,1,0:T(8,128)(2,1)S(1)}, bf16[2,64,128]{2,1,0:T(8,128)(2,1)S(1)}, u32[]{:S(2)}, u32[]{:S(2)}) collective-permute-start(bf16[2,64,128]{2,1,0:T(8,128)(2,1)S(1)} %get-tuple-element.72.refs_0_), channel_id=1, source_target_pairs={{0,1},{1,0},{2,3},{3,2},{4,5},{5,4},{6,7},{7,6},{8,9},{9,8},{10,11... | collective-permute-start | bytes 98312 | tf_op jit(solution)/shard_map/ppermute | solution.py:454
  63.0 1.4 %collective-permute-start.29 = (bf16[2,64,128]{2,1,0:T(8,128)(2,1)S(1)}, bf16[2,64,128]{2,1,0:T(8,128)(2,1)S(1)}, u32[]{:S(2)}, u32[]{:S(2)}) collective-permute-start(bf16[2,64,128]{2,1,0:T(8,128)(2,1)S(1)} %collective-permute-done.25.refs_3_), channel_id=1, source_target_pairs={{0,1},{1,0},{2,3},{3,2},{4,5},{5,4},{6,7},{7,6},{8,9},{9,8},{10,11... | collective-permute-start | bytes 98312 | tf_op jit(solution)/shard_map/ppermute | solution.py:454
  63.5 1.2 %collective-permute-start.28 = (bf16[2,64,128]{2,1,0:T(8,128)(2,1)S(1)}, bf16[2,64,128]{2,1,0:T(8,128)(2,1)S(1)}, u32[]{:S(2)}, u32[]{:S(2)}) collective-permute-start(bf16[2,64,128]{2,1,0:T(8,128)(2,1)S(1)} %collective-permute-done.24.refs_2_), channel_id=1, source_target_pairs={{0,1},{1,0},{2,3},{3,2},{4,5},{5,4},{6,7},{7,6},{8,9},{9,8},{10,11... | collective-permute-start | bytes 98312 | tf_op jit(solution)/shard_map/ppermute | solution.py:454
  63.8 1.2 %collective-permute-start.27 = (bf16[2,64,128]{2,1,0:T(8,128)(2,1)S(1)}, bf16[2,64,128]{2,1,0:T(8,128)(2,1)S(1)}, u32[]{:S(2)}, u32[]{:S(2)}) collective-permute-start(bf16[2,64,128]{2,1,0:T(8,128)(2,1)S(1)} %collective-permute-done.23.refs_1_), channel_id=1, source_target_pairs={{0,1},{1,0},{2,3},{3,2},{4,5},{5,4},{6,7},{7,6},{8,9},{9,8},{10,11... | collective-permute-start | bytes 98312 | tf_op jit(solution)/shard_map/ppermute | solution.py:454
  65.2 9.9 %collective-permute-start.32 = (bf16[224,128]{1,0:T(8,128)(2,1)S(1)}, bf16[224,128]{1,0:T(8,128)(2,1)S(1)}, u32[]{:S(2)}, u32[]{:S(2)}) collective-permute-start(bf16[224,128]{1,0:T(8,128)(2,1)S(1)} %add_convert_fusion.1), channel_id=1, source_target_pairs={{0,24},{8,0},{16,8},{24,16},{1,25},{9,1},{17,9},{25,17},{2,26},{10... | collective-permute-start | bytes 172040 | tf_op jit(solution)/shard_map/ppermute | solution.py:451
  68.2 7.3 %collective-permute-start.31 = (bf16[224,128]{1,0:T(8,128)(2,1)S(1)}, bf16[224,128]{1,0:T(8,128)(2,1)S(1)}, u32[]{:S(2)}, u32[]{:S(2)}) collective-permute-start(bf16[224,128]{1,0:T(8,128)(2,1)S(1)} %add_convert_fusion.1), channel_id=1, source_target_pairs={{0,8},{8,16},{16,24},{24,0},{1,9},{9,17},{17,25},{25,1},{2,10},{10... | collective-permute-start | bytes 172040 | tf_op jit(solution)/shard_map/ppermute | solution.py:451
  68.2 9.0 %collective-permute-start.30 = (bf16[224,128]{1,0:T(8,128)(2,1)S(1)}, bf16[224,128]{1,0:T(8,128)(2,1)S(1)}, u32[]{:S(2)}, u32[]{:S(2)}) collective-permute-start(bf16[224,128]{1,0:T(8,128)(2,1)S(1)} %add_convert_fusion.1), channel_id=1, source_target_pairs={{0,16},{8,24},{16,0},{24,8},{1,17},{9,25},{17,1},{25,9},{2,18},{10... | collective-permute-start | bytes 172040 | tf_op jit(solution)/shard_map/ppermute | solution.py:451
  77.2 7.2 %collective-permute-start.35 = (bf16[224,128]{1,0:T(8,128)(2,1)S(1)}, bf16[224,128]{1,0:T(8,128)(2,1)S(1)}, u32[]{:S(2)}, u32[]{:S(2)}) collective-permute-start(bf16[224,128]{1,0:T(8,128)(2,1)S(1)} %add_convert_fusion.first), channel_id=1, source_target_pairs={{0,192},{64,0},{128,64},{192,128},{1,193},{65,1},{129,65},{193,129... | collective-permute-start | bytes 172040 | tf_op jit(solution)/shard_map/ppermute | solution.py:451
  82.1 5.7 %collective-permute-start.34 = (bf16[224,128]{1,0:T(8,128)(2,1)S(1)}, bf16[224,128]{1,0:T(8,128)(2,1)S(1)}, u32[]{:S(2)}, u32[]{:S(2)}) collective-permute-start(bf16[224,128]{1,0:T(8,128)(2,1)S(1)} %add_convert_fusion.first), channel_id=1, source_target_pairs={{0,128},{64,192},{128,0},{192,64},{1,129},{65,193},{129,1},{193,65... | collective-permute-start | bytes 172040 | tf_op jit(solution)/shard_map/ppermute | solution.py:451
  82.6 5.8 %collective-permute-start.33 = (bf16[224,128]{1,0:T(8,128)(2,1)S(1)}, bf16[224,128]{1,0:T(8,128)(2,1)S(1)}, u32[]{:S(2)}, u32[]{:S(2)}) collective-permute-start(bf16[224,128]{1,0:T(8,128)(2,1)S(1)} %add_convert_fusion.first), channel_id=1, source_target_pairs={{0,64},{64,128},{128,192},{192,0},{1,65},{65,129},{129,193},{193,1... | collective-permute-start | bytes 172040 | tf_op jit(solution)/shard_map/ppermute | solution.py:451
